TPU v7x, 32 devices: a whole 2x2x4 slice. The times are simulated.
32 devices in a mesh: gx: 4 (over y, core), gy: 8 (over z, x).
Axes of the slice: x: 2, y: 2, z: 4, core: 2. Of those that a mesh axis runs over, the one named last changes fastest.
Arguments:
- right_side: float32 [64, 256, 256], P('gx', 'gy'), may hold values from -30 to 30
- start_field: float32 [64, 256, 256], P('gx', 'gy'), may hold values from -1.8 to 1.8
- coef: float32 [64, 256, 256], P('gx', 'gy'), may hold values from 0.5 to 2
- deflation: float32 [8, 64, 256, 256], P(None, 'gx', 'gy'), may hold values from -9 to 9
Outputs:
- solution: float32 [64, 256, 256], P('gx', 'gy')
- residual: float32 [64, 256, 256], P('gx', 'gy')
- direction: float32 [64, 256, 256], P('gx', 'gy')
All inputs are finite; a program needn't handle non-finite values.
Results may differ from a plain program's by a relative error of at most 0.0003.
Values sent between devices are 32-bit elements; how exact they have to be, the bound alone decides.
No kernel may reach another device: no remote copies, remote signals or barrier semaphores. Data moves between devices by JAX's collectives and lax.ppermute only.
A program may use at most 192 MiB of HBM per device.

v0:
```python
import jax
import jax.numpy as jnp
from jax import lax
from jax.sharding import PartitionSpec as P

ITERS = 2


highest = lax.Precision.HIGHEST


def extended(cells, sides, width):
    for axis, dim in sides:
        count = lax.axis_size(axis)
        ends = count - 1
        head = lax.slice_in_dim(cells, 0, width, axis=dim)
        tail = lax.slice_in_dim(cells, cells.shape[dim] - width, cells.shape[dim], axis=dim)
        cells = jnp.concatenate(
            [
                lax.ppermute(tail, axis, [(i, (i + 1) % count) for i in range(ends)]),
                cells,
                lax.ppermute(head, axis, [((i + 1) % count, i) for i in range(ends)]),
            ],
            axis=dim,
        )
    return cells


def shifted(value, axis, steps):
    count = lax.axis_size(axis)
    initial, last = (max(0, -steps), min(count, count - steps))
    return lax.ppermute(value, axis, [(source, source + steps) for source in range(initial, last)])


def face_coef(padded, along):
    length = padded.shape[along]
    lower_side = lax.slice_in_dim(padded, 0, length - 1, axis=along)
    upper_side = lax.slice_in_dim(padded, 1, length, axis=along)
    inside = (lower_side > 0.0) & (upper_side > 0.0)
    summed = lower_side + upper_side
    return jnp.where(inside, 2.0 * lower_side * upper_side / summed, summed)


def block_operate(vectors, face_rows, face_cols, face_depth, diagonal):
    padded = jnp.pad(vectors, ((0, 0), (1, 1), (1, 1), (1, 1)))
    beside = face_rows[1:] * padded[:, 2:, 1:-1, 1:-1] + face_rows[:-1] * padded[:, :-2, 1:-1, 1:-1]
    beside = (
        beside
        + face_cols[:, 1:] * padded[:, 1:-1, 2:, 1:-1]
        + face_cols[:, :-1] * padded[:, 1:-1, :-2, 1:-1]
    )
    beside = (
        beside
        + face_depth[:, :, 1:] * padded[:, 1:-1, 1:-1, 2:]
        + face_depth[:, :, :-1] * padded[:, 1:-1, 1:-1, :-2]
    )
    return diagonal * vectors - beside


def face_product(lower_part, weights, upper_part):
    return -jnp.einsum("kab,lab->kl", lower_part * weights, upper_part, precision=highest)


def place(selector, blocks):
    return selector.astype(jnp.float32)[:, None, :, None] * blocks[:, :, None, :]


def place_mirror(selector, blocks):
    return selector.astype(jnp.float32)[:, None, :, None] * jnp.transpose(blocks, (2, 0, 1))[None]


def block_masks(block_count, across):
    positions = jnp.arange(block_count, dtype=jnp.int32)
    row_ids = positions[:, None]
    col_ids = positions[None, :]
    self_mask = row_ids == col_ids
    below_rows = col_ids == row_ids - across
    below_cols = (col_ids == row_ids - 1) & (row_ids % across != 0)
    above_rows = col_ids == row_ids + across
    above_cols = (col_ids == row_ids + 1) & (col_ids % across != 0)
    return (self_mask, below_rows, below_cols, above_rows, above_cols)


def per_device(right_side, start_field, coef, deflation):
    num_vectors = deflation.shape[0]
    across = lax.axis_size("gy")
    block_count = lax.axis_size("gx") * across
    own_block = lax.axis_index("gx") * across + lax.axis_index("gy")
    padded = extended(coef, (("gx", 0), ("gy", 1)), 1)
    face_rows = face_coef(padded[:, 1:-1], 0)
    face_cols = face_coef(padded[1:-1], 1)
    face_depth = face_coef(jnp.pad(coef, ((0, 0), (0, 0), (1, 1))), 2)
    diagonal = face_rows[1:] + face_rows[:-1] + face_cols[:, 1:] + face_cols[:, :-1]
    diagonal = diagonal + face_depth[:, :, 1:] + face_depth[:, :, :-1]

    def apply_operator(values):
        rimmed_values = extended(values, (("gx", 0), ("gy", 1)), 1)
        depth_padded = jnp.pad(values, ((0, 0), (0, 0), (1, 1)))
        beside = face_rows[1:] * rimmed_values[2:, 1:-1] + face_rows[:-1] * rimmed_values[:-2, 1:-1]
        beside = (
            beside
            + face_cols[:, 1:] * rimmed_values[1:-1, 2:]
            + face_cols[:, :-1] * rimmed_values[1:-1, :-2]
        )
        beside = (
            beside
            + face_depth[:, :, 1:] * depth_padded[:, :, 2:]
            + face_depth[:, :, :-1] * depth_padded[:, :, :-2]
        )
        return diagonal * values - beside

    acted_on = block_operate(deflation, face_rows, face_cols, face_depth, diagonal)
    diag_block = jnp.einsum("kxyz,lxyz->kl", deflation, acted_on, precision=highest)
    from_rows = shifted(deflation[:, -1], "gx", 1)
    from_cols = shifted(deflation[:, :, -1], "gy", 1)
    below_rows = face_product(deflation[:, 0], face_rows[0], from_rows)
    below_cols = face_product(deflation[:, :, 0], face_cols[:, 0], from_cols)
    blocks = jnp.stack([diag_block, below_rows, below_cols])[None]
    gathered = lax.all_gather(blocks, ("gx", "gy"), axis=0, tiled=True)
    self_mask, mask_below_rows, mask_below_cols, mask_above_rows, mask_above_cols = block_masks(
        block_count, across
    )
    matrix = (
        place(self_mask, gathered[:, 0])
        + place(mask_below_rows, gathered[:, 1])
        + place(mask_below_cols, gathered[:, 2])
    )
    matrix = (
        matrix
        + place_mirror(mask_above_rows, gathered[:, 1])
        + place_mirror(mask_above_cols, gathered[:, 2])
    )
    matrix = matrix.reshape(block_count * num_vectors, block_count * num_vectors)
    factor = jnp.linalg.cholesky(matrix)

    def solve_coarse(gathered_rows):
        flattened = gathered_rows.reshape(-1)
        solved = jax.scipy.linalg.cho_solve((factor, True), flattened)
        return lax.dynamic_slice_in_dim(solved, own_block * num_vectors, num_vectors)

    def restrict(values):
        return jnp.einsum("kxyz,xyz->k", deflation, values, precision=highest)

    def prolong(coarse_values):
        return jnp.einsum("kxyz,k->xyz", deflation, coarse_values, precision=highest)

    def coarse_plain(values):
        gathered_rows = lax.all_gather(restrict(values)[None], ("gx", "gy"), axis=0, tiled=True)
        return prolong(solve_coarse(gathered_rows))

    def coarse_with(values, residual_now, precond_now):
        inner_sum = lax.psum(jnp.sum(residual_now * precond_now), ("gx", "gy"))
        return (coarse_plain(values), inner_sum)

    solution = start_field + coarse_plain(right_side - apply_operator(start_field))
    residual = right_side - apply_operator(solution)
    precond = residual / diagonal
    correction, inner_now = coarse_with(apply_operator(precond), residual, precond)
    direction = precond - correction
    for iteration in range(ITERS):
        applied = apply_operator(direction)
        step_size = inner_now / lax.psum(jnp.sum(direction * applied), ("gx", "gy"))
        solution = solution + step_size * direction
        residual = residual - step_size * applied
        precond = residual / diagonal
        correction, inner_next = coarse_with(apply_operator(precond), residual, precond)
        direction = precond + inner_next / inner_now * direction - correction
        inner_now = inner_next
    return (solution, residual, direction)


def solution(mesh):
    placed = (
        P("gx", "gy", None),
        P("gx", "gy", None),
        P("gx", "gy", None),
        P(None, "gx", "gy", None),
    )
    return jax.shard_map(
        per_device,
        mesh=mesh,
        in_specs=placed,
        out_specs=(P("gx", "gy", None), P("gx", "gy", None), P("gx", "gy", None)),
        check_vma=False,
    )
```

profile of v0, /device:TPU:0, one launch (start us, length us, event | category | flops | bytes accessed | tf_op | source)
XLA Modules:
  0.0 698.4 jit_solution(8890003070100004108)
XLA Ops:
  21.7 5.6 copy.69
  60.6 10.8 %convolution_bitcast_fusion.5 = f32[8]{0:T(128)S(1)} fusion(f32[16,32,256,1]{2,0,1,3:T(8,128)S(1)} %get-tuple-element.67, f32[8,16,32,256]{3,2,1,0:T(8,128)S(1)} %copy-done), kind=kOutput, calls=%fused_computation.36 | convolution fusion | flops 12582912 | bytes 4718624 | tf_op jit(solution)/shard_map/kxyz,xyz->k/dot_general | solution.py:142
  71.6 41.8 %all-reduce.10 = f32[256]{0:T(256)} all-reduce(f32[256]{0:T(256)S(1)} %dynamic-update-slice.14), channel_id=3, replica_groups=mesh['gx'=4,'gy'=8] {'gx','gy'}, use_global_device_ids=true, to_apply=%add.10 | all-reduce | flops 256 | bytes 2048
  118.8 14.6 %fusion.6 = f32[8,16,32,256]{3,2,1,0:T(8,128)} fusion(f32[8,16,32,256]{3,2,1,0:T(8,128)} %param.9, f32[16,32,256]{2,1,0:T(8,128)} %copy.67, f32[16,32,256]{2,1,0:T(8,128)S(1)} %copy-done.17, f32[16,32,256]{2,1,0:T(8,128)} %copy.65, f32[16,32,256]{2,1,0:T(8,128)} %copy.64, f32[16,32,256]{2,1,0:T(8,128)} %copy.63, f32[16,32,256]{2,1,0:T(8,128)} %copy.62, ...), kind=kLoop, calls=%fused_computation.14 | loop fusion | flops 13631488 | bytes 12058624 | tf_op jit(solution)/shard_map/sub | solution.py:57
  133.5 15.2 %fusion.14 = f32[8,8]{0,1:T(8,128)S(1)} fusion(f32[8,16,32,256]{3,2,1,0:T(8,128)} %fusion.6, f32[8,16,32,256]{3,2,1,0:T(8,128)} %param.9), kind=kOutput, calls=%fused_computation.26 | convolution fusion | flops 100663296 | bytes 8388864 | tf_op jit(solution)/shard_map/kxyz,lxyz->kl/dot_general | solution.py:113
  151.7 68.1 %all-gather = f32[96,8,8]{2,1,0:T(8,128)S(1)} all-gather(f32[3,8,8]{2,1,0:T(8,128)S(1)} %pad_maximum_fusion.87), channel_id=2, replica_groups=mesh['gx'=4,'gy'=8] {'gx','gy'}, dimensions={0}, use_global_device_ids=true | all-gather | bytes 25344 | tf_op jit(solution)/shard_map/all_gather | solution.py:119
  232.3 11.7 %cholesky.50 = f32[128,128]{1,0:T(8,128)S(1)} custom-call(f32[128,128]{1,0:T(8,128)S(1)} %cholesky.118), custom_call_target="Cholesky" | custom-call | tf_op jit(solution)/shard_map/jit(cholesky)/cholesky | solution.py:134
  244.7 10.4 %custom-call.16 = f32[1,128,128]{1,2,0:T(8,128)} custom-call(f32[1,128,128]{2,1,0:T(8,128)S(1)} %get-tuple-element.123), custom_call_target="InvertDiagBlocksLowerTriangular" | custom-call | tf_op jit(solution)/shard_map/jit(cholesky)/cholesky | solution.py:134
  257.3 11.7 %cholesky.105 = f32[128,128]{1,0:T(8,128)S(1)} custom-call(f32[128,128]{1,0:T(8,128)S(1)} %convolution_subtract_fusion), custom_call_target="Cholesky" | custom-call | tf_op jit(solution)/shard_map/jit(cholesky)/cholesky | solution.py:134
  272.8 5.2 while.8
  278.0 20.7 %custom-call.20 = f32[2,128,128]{1,2,0:T(8,128)S(1)} custom-call(f32[2,128,128]{2,1,0:T(8,128)} %get-tuple-element.30), custom_call_target="InvertDiagBlocksLowerTriangular" | custom-call | tf_op jit(solution)/shard_map/jit(_cho_solve)/triangular_solve | solution.py:138
  301.1 8.2 %fusion.164 = f32[1,16,32,256]{3,0,2,1:T(1,128)S(1)} fusion(f32[256]{0:T(256)S(1)} %bitcast.326, s32[]{:T(128)S(6)} %select_n.50, f32[8,16,32,256]{3,2,1,0:T(8,128)} %param.9), kind=kOutput, calls=%fused_computation.352 | convolution fusion | flops 12582912 | bytes 4719108 | tf_op jit(solution)/shard_map/kxyz,k->xyz/dot_general | solution.py:145
  333.7 5.3 collective-permute-start.17
  340.7 10.9 %convolution_bitcast_fusion.4 = f32[8]{0:T(128)S(1)} fusion(f32[16,32,256,1]{2,0,1,3:T(8,128)S(1)} %fusion.54, f32[8,16,32,256]{3,2,1,0:T(8,128)S(1)} %copy-done.1), kind=kOutput, calls=%fused_computation.35 | convolution fusion | flops 12582912 | bytes 4718624 | tf_op jit(solution)/shard_map/kxyz,xyz->k/dot_general | solution.py:142
  351.8 44.4 %all-reduce.11 = f32[256]{0:T(256)S(1)} all-reduce(f32[256]{0:T(256)S(1)} %dynamic-update-slice.15), channel_id=4, replica_groups=mesh['gx'=4,'gy'=8] {'gx','gy'}, use_global_device_ids=true, to_apply=%add.11 | all-reduce | flops 256 | bytes 2048
  397.4 8.2 %fusion.162 = f32[1,16,32,256]{3,0,2,1:T(1,128)S(1)} fusion(f32[256]{0:T(256)S(1)} %bitcast.327, s32[]{:T(128)S(6)} %select_n.50, f32[8,16,32,256]{3,2,1,0:T(8,128)} %param.9), kind=kOutput, calls=%fused_computation.350 | convolution fusion | flops 12582912 | bytes 4719108 | tf_op jit(solution)/shard_map/kxyz,k->xyz/dot_general | solution.py:145
  422.1 42.1 %all-reduce.16 = (f32[]{:T(128)}, f32[]{:T(128)}) all-reduce(f32[]{:T(128)} %get-tuple-element.64, f32[]{:T(128)} %get-tuple-element.62), channel_id=1, replica_groups=mesh['gx'=4,'gy'=8] {'gx','gy'}, use_global_device_ids=true, to_apply=%region_5.7 | all-reduce | flops 2 | bytes 16 | tf_op jit(solution)/shard_map/psum | solution.py:152
  483.6 11.1 %convolution_bitcast_fusion.3 = f32[8]{0:T(128)} fusion(f32[16,32,256,1]{2,0,1,3:T(8,128)S(1)} %fusion.65, f32[8,16,32,256]{3,2,1,0:T(8,128)S(1)} %copy-done.2), kind=kOutput, calls=%fused_computation.34 | convolution fusion | flops 12582912 | bytes 4718624 | tf_op jit(solution)/shard_map/kxyz,xyz->k/dot_general | solution.py:142
  496.6 43.6 %all-reduce.15 = (f32[256]{0:T(256)}, f32[]{:T(128)}) all-reduce(f32[256]{0:T(256)} %dynamic-update-slice.16, f32[]{:T(128)} %get-tuple-element.59), channel_id=5, replica_groups=mesh['gx'=4,'gy'=8] {'gx','gy'}, use_global_device_ids=true, to_apply=%add.12 | all-reduce | flops 257 | bytes 2056
  544.0 8.2 %fusion.160 = f32[1,16,32,256]{3,0,2,1:T(1,128)S(1)} fusion(f32[256]{0:T(256)S(1)} %bitcast.328, s32[]{:T(128)S(6)} %select_n.50, f32[8,16,32,256]{3,2,1,0:T(8,128)} %param.9), kind=kOutput, calls=%fused_computation.348 | convolution fusion | flops 12582912 | bytes 4719108 | tf_op jit(solution)/shard_map/kxyz,k->xyz/dot_general | solution.py:145
  569.1 43.1 %psum.38 = f32[]{:T(128)} all-reduce(f32[]{:T(128)} %get-tuple-element.57), channel_id=1, replica_groups=mesh['gx'=4,'gy'=8] {'gx','gy'}, use_global_device_ids=true, to_apply=%region_11.13 | all-reduce | flops 1 | bytes 8 | tf_op jit(solution)/shard_map/psum | solution.py:162
  630.8 10.6 %convolution_bitcast_fusion.2 = f32[8]{0:T(128)S(1)} fusion(f32[16,32,256,1]{2,0,1,3:T(8,128)S(1)} %fusion.76, f32[8,16,32,256]{3,2,1,0:T(8,128)S(1)} %copy-done.3), kind=kOutput, calls=%fused_computation.33 | convolution fusion | flops 12582912 | bytes 4718624 | tf_op jit(solution)/shard_map/kxyz,xyz->k/dot_general | solution.py:142
  641.6 43.3 %all-reduce.14 = (f32[256]{0:T(256)S(1)}, f32[]{:T(128)}) all-reduce(f32[256]{0:T(256)S(1)} %dynamic-update-slice.17, f32[]{:T(128)} %get-tuple-element.54), channel_id=6, replica_groups=mesh['gx'=4,'gy'=8] {'gx','gy'}, use_global_device_ids=true, to_apply=%add.13 | all-reduce | flops 257 | bytes 2056
  687.3 8.2 %fusion.158 = f32[1,16,32,256]{3,0,2,1:T(1,128)S(1)} fusion(f32[256]{0:T(256)S(1)} %bitcast.325, s32[]{:T(128)S(6)} %select_n.50, f32[8,16,32,256]{3,2,1,0:T(8,128)} %param.9), kind=kOutput, calls=%fused_computation.346 | convolution fusion | flops 12582912 | bytes 4719108 | tf_op jit(solution)/shard_map/kxyz,k->xyz/dot_general | solution.py:145
  (247 shorter events, 192.6 us)
Async XLA Ops:
  1.5 35.2 %collective-permute-start.1 = (f32[1,32,256]{2,0,1:T(1,128)S(1)}, f32[1,32,256]{2,0,1:T(1,128)S(1)}, u32[]{:S(2)}, u32[]{:S(2)}) collective-permute-start(f32[1,32,256]{2,0,1:T(1,128)S(1)} %copy.57), channel_id=1, source_target_pairs={{8,0},{16,8},{24,16},{9,1},{17,9},{25,17},{10,2},{18,10},{26,18},{... | collective-permute-start | bytes 98312 | tf_op jit(solution)/shard_map/ppermute | solution.py:22
  2.8 38.9 %collective-permute-start = (f32[1,32,256]{2,0,1:T(1,128)S(1)}, f32[1,32,256]{2,0,1:T(1,128)S(1)}, u32[]{:S(2)}, u32[]{:S(2)}) collective-permute-start(f32[1,32,256]{2,0,1:T(1,128)S(1)} %copy.55), channel_id=1, source_target_pairs={{0,8},{8,16},{16,24},{1,9},{9,17},{17,25},{2,10},{10,18},{18,26},{... | collective-permute-start | bytes 98312 | tf_op jit(solution)/shard_map/ppermute | solution.py:20
  6.7 36.8 %collective-permute-start.6 = (f32[1,32,256]{2,0,1:T(1,128)S(1)}, f32[1,32,256]{2,0,1:T(1,128)S(1)}, u32[]{:S(2)}, u32[]{:S(2)}) collective-permute-start(f32[1,32,256]{2,0,1:T(1,128)S(1)} %copy.80), channel_id=1, source_target_pairs={{8,0},{16,8},{24,16},{9,1},{17,9},{25,17},{10,2},{18,10},{26,18},{... | collective-permute-start | bytes 98312 | tf_op jit(solution)/shard_map/ppermute | solution.py:22
  8.0 35.5 %collective-permute-start.7 = (f32[1,32,256]{2,0,1:T(1,128)S(1)}, f32[1,32,256]{2,0,1:T(1,128)S(1)}, u32[]{:S(2)}, u32[]{:S(2)}) collective-permute-start(f32[1,32,256]{2,0,1:T(1,128)S(1)} %copy.82), channel_id=1, source_target_pairs={{0,8},{8,16},{16,24},{1,9},{9,17},{17,25},{2,10},{10,18},{18,26},{... | collective-permute-start | bytes 98312 | tf_op jit(solution)/shard_map/ppermute | solution.py:20
  16.3 132.5 %collective-permute-start.5 = (f32[8,16,256]{2,0,1:T(8,128)}, f32[8,16,256]{2,0,1:T(8,128)}, u32[]{:S(2)}, u32[]{:S(2)}) collective-permute-start(f32[8,16,256]{2,0,1:T(8,128)} %bitcast.314), channel_id=1, source_target_pairs={{0,1},{1,2},{2,3},{3,4},{4,5},{5,6},{6,7},{8,9},{9,10},{10,11},{11... | collective-permute-start | bytes 393224 | tf_op jit(solution)/shard_map/ppermute | solution.py:32
  36.6 113.4 %collective-permute-start.4 = (f32[8,32,256]{2,0,1:T(8,128)}, f32[8,32,256]{2,0,1:T(8,128)}, u32[]{:S(2)}, u32[]{:S(2)}) collective-permute-start(f32[8,32,256]{2,0,1:T(8,128)} %slice_bitcast_fusion), channel_id=1, source_target_pairs={{0,8},{8,16},{16,24},{1,9},{9,17},{17,25},{2,10},{10,18},{18,26},{... | collective-permute-start | bytes 786440 | tf_op jit(solution)/shard_map/ppermute | solution.py:32
  43.5 16.2 %collective-permute-start.8 = (f32[18,1,256]{2,0,1:T(8,128)S(1)}, f32[18,1,256]{2,0,1:T(8,128)S(1)}, u32[]{:S(2)}, u32[]{:S(2)}) collective-permute-start(f32[18,1,256]{2,0,1:T(8,128)S(1)} %get-tuple-element.89), channel_id=1, source_target_pairs={{1,0},{2,1},{3,2},{4,3},{5,4},{6,5},{7,6},{9,8},{10,9},{11,10},{12... | collective-permute-start | bytes 55304 | tf_op jit(solution)/shard_map/ppermute | solution.py:22
  45.0 8.1 %collective-permute-start.2 = (f32[18,1,256]{2,0,1:T(8,128)S(1)}, f32[18,1,256]{2,0,1:T(8,128)S(1)}, u32[]{:S(2)}, u32[]{:S(2)}) collective-permute-start(f32[18,1,256]{2,0,1:T(8,128)S(1)} %get-tuple-element.91), channel_id=1, source_target_pairs={{0,1},{1,2},{2,3},{3,4},{4,5},{5,6},{6,7},{8,9},{9,10},{10,11},{11... | collective-permute-start | bytes 55304 | tf_op jit(solution)/shard_map/ppermute | solution.py:20
  49.5 8.3 %collective-permute-start.3 = (f32[18,1,256]{2,0,1:T(8,128)S(1)}, f32[18,1,256]{2,0,1:T(8,128)S(1)}, u32[]{:S(2)}, u32[]{:S(2)}) collective-permute-start(f32[18,1,256]{2,0,1:T(8,128)S(1)} %get-tuple-element.92), channel_id=1, source_target_pairs={{1,0},{2,1},{3,2},{4,3},{5,4},{6,5},{7,6},{9,8},{10,9},{11,10},{12... | collective-permute-start | bytes 55304 | tf_op jit(solution)/shard_map/ppermute | solution.py:22
  53.1 6.7 collective-permute-start.9
  315.3 5.9 collective-permute-start.12
  316.6 6.1 collective-permute-start.13
  332.4 6.6 collective-permute-start.16
  333.7 6.4 collective-permute-start.17
  412.9 5.9 collective-permute-start.20
  414.2 6.1 collective-permute-start.21
  469.8 5.9 collective-permute-start.22
  475.7 6.1 collective-permute-start.24
  477.0 6.1 collective-permute-start.25
  553.9 5.8 collective-permute-start.26
  559.8 5.9 collective-permute-start.28
  561.1 6.1 collective-permute-start.29
  622.8 7.1 %collective-permute-start.32 = (f32[18,1,256]{2,0,1:T(8,128)S(1)}, f32[18,1,256]{2,0,1:T(8,128)S(1)}, u32[]{:S(2)}, u32[]{:S(2)}) collective-permute-start(f32[18,1,256]{2,0,1:T(8,128)S(1)} %get-tuple-element.77), channel_id=1, source_target_pairs={{1,0},{2,1},{3,2},{4,3},{5,4},{6,5},{7,6},{9,8},{10,9},{11,10},{12... | collective-permute-start | bytes 55304 | tf_op jit(solution)/shard_map/ppermute | solution.py:22
  624.1 6.1 collective-permute-start.33
  (34 other events, 629.1 us)
where the time goes:
time: 707 us; the launch traced here: 698 us
  blocking collectives  326 us (46%)
  matrix products  104 us (15%)
  other arithmetic  96.7 us (14%)
  starting transfers between devices  84.9 us (12%)
  local copies, waits for them, and re-layouts  48.4 us (7%)
  waiting for transfers between devices  30.2 us (4%)
  between operations  8.21 us (1%)
    unnamed x4, blocking collectives  173 us
    all_gather x1, blocking collectives, per_device(): gathered = lax.all_gather(blocks, ('gx', 'gy'), axis=0, tiled=True)  68.1 us
    ppermute x16, starting transfers between devices, extended(): lax.ppermute(tail, axis, [(i, (i + 1) % count) for i in range(ends)])  56 us
    dot_general x4, matrix products, restrict(): return jnp.einsum('kxyz,xyz->k', deflation, values, precision=highest)  43.4 us
    psum x1, blocking collectives, per_device(): step_size = inner_now / lax.psum(jnp.sum(direction * applied), ('gx', 'gy'))  43.1 us
    psum x1, blocking collectives, coarse_with(): inner_sum = lax.psum(jnp.sum(residual_now * precond_now), ('gx', 'gy'))  42.1 us
    another operation x7, other arithmetic, per_device(): factor = jnp.linalg.cholesky(matrix)  35.2 us
    dot_general x4, matrix products, prolong(): jnp.einsum('kxyz,k->xyz', deflation, coarse_values, precision=highest)  32.7 us
  transfers between devices with their start and end apart: 34, of which 12 were waited for; matrix products, arithmetic and copies ran while one was open for 11% of the time, Pallas kernels for 0%

commit v1 on v0

v1 whole, which is shorter than its diff:
```python
import jax
import jax.numpy as jnp
from jax import lax
from jax.sharding import PartitionSpec as P

ITERS = 2
BOTH = ("gx", "gy")
highest = lax.Precision.HIGHEST


def swap(value, axis, parity):
    count = lax.axis_size(axis)
    pairs = []
    for low in range(parity, count - 1, 2):
        pairs += [(low, low + 1), (low + 1, low)]
    return lax.ppermute(value, axis, pairs)


def halo(low, high, axis):
    even = lax.axis_index(axis) % 2 == 0
    first = swap(jnp.where(even, high, low), axis, 0)
    second = swap(jnp.where(even, low, high), axis, 1)
    return jnp.where(even, second, first), jnp.where(even, first, second)


def everywhere(payload):
    count = lax.axis_size("gx") * lax.axis_size("gy")
    return lax.all_to_all(jnp.broadcast_to(payload[None], (count,) + payload.shape), BOTH, 0, 0)


def face(lower, upper):
    summed = lower + upper
    inside = (lower > 0.0) & (upper > 0.0)
    return jnp.where(inside, 2.0 * lower * upper / summed, summed)


def row_sums(left, right):
    return jnp.einsum("kab,lab->kl", left, right, precision=highest)


def per_device(right_side, start_field, coef, deflation):
    num = deflation.shape[0]
    down, across = lax.axis_size("gx"), lax.axis_size("gy")
    blocks = down * across
    own = lax.axis_index("gx") * across + lax.axis_index("gy")

    pack_x = lambda i: jnp.concatenate([coef[i][None], start_field[i][None], deflation[:, i]])
    pack_y = lambda j: jnp.concatenate([coef[:, j][None], start_field[:, j][None], deflation[:, :, j]])
    x_low, x_high = halo(pack_x(0), pack_x(-1), "gx")
    y_low, y_high = halo(pack_y(0), pack_y(-1), "gy")

    def extend(cells, sides):
        xl, xh, yl, yh = sides
        xs = jnp.concatenate([xl[None], cells, xh[None]], 0)
        ys = jnp.concatenate([yl[:, None], cells, yh[:, None]], 1)
        zs = jnp.pad(cells, ((0, 0), (0, 0), (1, 1)))
        return xs, ys, zs

    cx, cy, cz = extend(coef, (x_low[0], x_high[0], y_low[0], y_high[0]))
    fx, fy, fz = face(cx[:-1], cx[1:]), face(cy[:, :-1], cy[:, 1:]), face(cz[:, :, :-1], cz[:, :, 1:])
    diagonal = fx[1:] + fx[:-1] + fy[:, 1:] + fy[:, :-1] + fz[:, :, 1:] + fz[:, :, :-1]

    def operate(cells, sides):
        vx, vy, vz = extend(cells, sides)
        beside = fx[1:] * vx[2:] + fx[:-1] * vx[:-2] + fy[:, 1:] * vy[:, 2:] + fy[:, :-1] * vy[:, :-2]
        beside = beside + fz[:, :, 1:] * vz[:, :, 2:] + fz[:, :, :-1] * vz[:, :, :-2]
        return diagonal * cells - beside

    none = (jnp.zeros_like(coef[0]),) * 2 + (jnp.zeros_like(coef[:, 0]),) * 2
    acted = jax.vmap(lambda v: operate(v, none))(deflation)
    diag_block = jnp.einsum("kxyz,lxyz->kl", deflation, acted, precision=highest)
    below_x = -row_sums(deflation[:, 0] * fx[0], x_low[2:])
    below_y = -row_sums(deflation[:, :, 0] * fy[:, 0], y_low[2:])
    start_residual = right_side - operate(start_field, (x_low[1], x_high[1], y_low[1], y_high[1]))

    def restrict(values):
        return jnp.einsum("kxyz,xyz->k", deflation, values, precision=highest)

    def pad_row(parts):
        flat = jnp.concatenate([p.reshape(-1) for p in parts])
        size = -(-flat.size // 128) * 128
        return jnp.pad(flat, (0, size - flat.size)).reshape(-1, 128)

    got = everywhere(pad_row([diag_block, below_x, below_y, restrict(start_residual)])).reshape(blocks, -1)
    square = num * num
    d_blocks, r_blocks, c_blocks = (got[:, i * square : (i + 1) * square].reshape(blocks, num, num) for i in range(3))
    ids = jnp.arange(blocks)
    place = lambda mask, part: jnp.where(mask[:, None, :, None], part[:, :, None, :], 0.0)
    mirror = lambda mask, part: jnp.where(mask[:, None, :, None], jnp.transpose(part, (2, 0, 1))[None], 0.0)
    rows, cols = ids[:, None], ids[None]
    matrix = place(rows == cols, d_blocks) + place(cols == rows - across, r_blocks)
    matrix = matrix + place((cols == rows - 1) & (rows % across != 0), c_blocks)
    matrix = matrix + mirror(cols == rows + across, r_blocks)
    matrix = matrix + mirror((cols == rows + 1) & (cols % across != 0), c_blocks)
    factor = jnp.linalg.cholesky(matrix.reshape(blocks * num, blocks * num))

    def solve(vector):
        solved = jax.scipy.linalg.cho_solve((factor, True), vector)
        grid = jnp.pad(solved.reshape(down, across, num), ((1, 1), (1, 1), (0, 0)))
        at = lambda i, j: lax.dynamic_slice(grid, (lax.axis_index("gx") + i, lax.axis_index("gy") + j, 0), (1, 1, num))[0, 0]
        return at(1, 1), (at(0, 1), at(2, 1), at(1, 0), at(1, 2))

    def spread(amounts):
        mine, around = amounts
        cells = jnp.einsum("kxyz,k->xyz", deflation, mine, precision=highest)
        layers = (x_low[2:], x_high[2:], y_low[2:], y_high[2:])
        sides = tuple(jnp.einsum("kab,k->ab", l, y, precision=highest) for l, y in zip(layers, around))
        return cells, operate(cells, sides)

    def full(cells):
        xl, xh = halo(cells[0], cells[-1], "gx")
        yl, yh = halo(cells[:, 0], cells[:, -1], "gy")
        return operate(cells, (xl, xh, yl, yh))

    coarse, image = spread(solve(got[:, 3 * square : 3 * square + num].reshape(-1)))
    solution = start_field + coarse
    residual = start_residual - image
    direction = applied = jnp.zeros_like(solution)
    inner = energy = jnp.float32(1.0)
    for iteration in range(ITERS + 1):
        precond = residual / diagonal
        acted_p = full(precond)
        sums = jnp.stack([jnp.sum(residual * precond), jnp.sum(precond * acted_p), jnp.sum(precond * applied)])
        got = everywhere(pad_row([sums, restrict(acted_p)]))[:, 0]
        new, energy_p, cross = (jnp.sum(got[:, i]) for i in range(3))
        vector = got[:, 3 : 3 + num].reshape(-1)
        solved = jax.scipy.linalg.cho_solve((factor, True), vector)
        grid = jnp.pad(solved.reshape(down, across, num), ((1, 1), (1, 1), (0, 0)))
        at = lambda i, j: lax.dynamic_slice(grid, (lax.axis_index("gx") + i, lax.axis_index("gy") + j, 0), (1, 1, num))[0, 0]
        coarse, image = spread((at(1, 1), (at(0, 1), at(2, 1), at(1, 0), at(1, 2))))
        beta = jnp.where(iteration == 0, 0.0, new / inner)
        direction = precond - coarse + beta * direction
        if iteration == ITERS:
            break
        applied = acted_p - image + beta * applied
        energy = energy_p - jnp.sum(solved * vector) + 2.0 * beta * cross + beta * beta * energy
        step = new / energy
        solution = solution + step * direction
        residual = residual - step * applied
        inner = new
    return solution, residual, direction


def solution(mesh):
    field = P("gx", "gy", None)
    return jax.shard_map(
        per_device,
        mesh=mesh,
        in_specs=(field, field, field, P(None, "gx", "gy", None)),
        out_specs=(field, field, field),
        check_vma=False,
    )
```

time: 707 us -> 384 us (0.54)
  blocking collectives: 326 us -> 29.5 us
  starting transfers between devices: 84.9 us -> 30 us
  local copies, waits for them, and re-layouts: 48.4 us -> 76.8 us
  waiting for transfers between devices: 30.2 us -> 15 us
  matrix products: 104 us -> 112 us
    unnamed x4 -> x0, blocking collectives: 173 us -> none
    psum x2 -> x0, blocking collectives: 85.2 us -> none  [the longest x1 43.1 us: per_device(): step_size = inner_now / lax.psum(jnp.sum(direction * applied), ('gx', 'gy'))]
    ppermute x34 -> x16, starting transfers between devices: 84.9 us -> 14.2 us  [swap(): return lax.ppermute(value, axis, pairs)]
    all_gather x1 -> x0, blocking collectives: 68.1 us -> none  [per_device(): gathered = lax.all_gather(blocks, ('gx', 'gy'), axis=0, tiled=True)]
    all_to_all x0 -> x2, blocking collectives: none -> 29.5 us  [everywhere(): lax.all_to_all(jnp.broadcast_to(payload[None], (count,) + payload.shape),...]
    ppermute x34 -> x16, waiting for transfers between devices: 30.2 us -> 3.38 us  [swap(): return lax.ppermute(value, axis, pairs)]
    all_to_all x0 -> x2, starting transfers between devices: none -> 15.9 us  [everywhere(): lax.all_to_all(jnp.broadcast_to(payload[None], (count,) + payload.shape),...]
    all_to_all x0 -> x2, waiting for transfers between devices: none -> 11.6 us  [everywhere(): lax.all_to_all(jnp.broadcast_to(payload[None], (count,) + payload.shape),...]
  transfers between devices with their start and end apart: 34 -> 18, of which waited for: 12 -> 5; matrix products, arithmetic and copies ran while one was open for 11% -> 6% of each run, Pallas kernels for 0% -> 0%
where the time goes in v1:
time: 384 us; the launch traced here: 377 us
  matrix products  112 us (29%)
  other arithmetic  103 us (27%)
  local copies, waits for them, and re-layouts  76.8 us (20%)
  starting transfers between devices  30 us (8%)
  blocking collectives  29.5 us (8%)
  waiting for transfers between devices  15 us (4%)
  between operations  11 us (3%)
    dot_general x4, matrix products, restrict(): return jnp.einsum('kxyz,xyz->k', deflation, values, precision=highest)  43.1 us
    another operation x7, other arithmetic, per_device(): factor = jnp.linalg.cholesky(matrix.reshape(blocks * num, blocks * num))  35.8 us
    dot_general x4, matrix products, spread(): cells = jnp.einsum('kxyz,k->xyz', deflation, mine, precision=highest)  35.4 us
    all_to_all x2, blocking collectives, everywhere(): lax.all_to_all(jnp.broadcast_to(payload[None], (count,) + payload.shape),...  29.5 us
    another operation x5, other arithmetic, solve(): solved = jax.scipy.linalg.cho_solve((factor, True), vector)  22.8 us
    unnamed x122, local copies, waits for them, and re-layouts  17.2 us
    all_to_all x2, starting transfers between devices, everywhere(): lax.all_to_all(jnp.broadcast_to(payload[None], (count,) + payload.shape),...  15.9 us
    ppermute x16, starting transfers between devices, swap(): return lax.ppermute(value, axis, pairs)  14.2 us
  transfers between devices with their start and end apart: 18, of which 5 were waited for; matrix products, arithmetic and copies ran while one was open for 6% of the time, Pallas kernels for 0%

profile of v1, /device:TPU:0, one launch (start us, length us, event | category | flops | bytes accessed | tf_op | source)
XLA Modules:
  0.0 377.1 jit_solution(14959629772515391262)
XLA Ops:
  8.4 7.5 %copy.134 = f32[8,16,32,256]{3,0,2,1:T(8,128)} copy(f32[8,16,32,256]{3,2,1,0:T(8,128)} %param.9) | data formatting | bytes 8388608 | tf_op args[3]
  37.1 10.8 %convolution_bitcast_fusion.5 = f32[8]{0:T(128)S(1)} fusion(f32[16,32,256,1]{2,0,1,3:T(8,128)S(1)} %get-tuple-element.77, f32[8,16,32,256]{3,2,1,0:T(8,128)S(1)} %copy-done), kind=kOutput, calls=%fused_computation.34 | convolution fusion | flops 12582912 | bytes 4718624 | tf_op jit(solution)/shard_map/kxyz,xyz->k/dot_general | solution.py:77
  56.3 5.3 %fusion.6 = f32[8,16,32,256]{3,2,1,0:T(8,128)S(1)} fusion(f32[8,16,32,256]{3,2,1,0:T(8,128)S(1)} %copy-done.1, f32[16,32,256]{2,1,0:T(8,128)} %copy.155, f32[16,32,256]{2,1,0:T(8,128)S(1)} %copy.154, f32[16,32,256]{2,1,0:T(8,128)} %copy.153, f32[16,32,256]{2,1,0:T(8,128)} %copy.152, f32[16,32,256]{2,1,0:T(8,128)S(1)} %copy.151, f32[16,32,256]{2,1,0:T(8,128)} %copy.150, ...), kind=kLoop, calls=%fused_computation.14 | loop fusion | flops 13631488 | bytes 12058624 | tf_op jit(solution)/shard_map/vmap()/sub | solution.py:67
  61.7 11.7 %fusion.14 = f32[8,8]{0,1:T(8,128)S(1)} fusion(f32[8,16,32,256]{3,2,1,0:T(8,128)S(1)} %fusion.6, f32[8,16,32,256]{3,2,1,0:T(8,128)S(1)} %copy-done.1), kind=kOutput, calls=%fused_computation.26 | convolution fusion | flops 100663296 | bytes 8388864 | tf_op jit(solution)/shard_map/kxyz,lxyz->kl/dot_general | solution.py:71
  74.3 8.2 %all-to-all-start = ((f32[32,2,128]{2,1,0:T(2,128)}), f32[32,2,128]{2,1,0:T(2,128)S(1)}, u32[]{:S(2)}, u32[]{:S(2)}) async-start(f32[32,2,128]{2,1,0:T(2,128)} %broadcast_in_dim.197), calls=%async_computation | async-start | bytes 65536 | tf_op jit(solution)/shard_map/all_to_all | solution.py:28
  83.0 6.7 %all-to-all-done = f32[32,2,128]{2,1,0:T(2,128)S(1)} async-done(((f32[32,2,128]{2,1,0:T(2,128)}), f32[32,2,128]{2,1,0:T(2,128)S(1)}, u32[]{:S(2)}, u32[]{:S(2)}) %all-to-all-start) | async-done | bytes 32800 | tf_op jit(solution)/shard_map/all_to_all | solution.py:28
  95.1 4.5 %select_add_fusion = f32[32,8,32,8]{3,2,1,0:T(8,128)} fusion(f32[8,32,8]{2,1,0:T(8,128)S(1)} %copy.173, f32[8,32,8]{2,1,0:T(8,128)S(1)} %copy.172, f32[32,8,8]{2,1,0:T(8,128)S(1)} %copy.171, f32[32,8,8]{2,1,0:T(8,128)} %copy.170, f32[32,8,8]{2,1,0:T(8,128)} %copy.169, pred[32,32]{1,0:T(8,128)(4,1)} %get-tuple-element.158, ...), kind=kLoop, calls=%fused_computation.22 | loop fusion | flops 589824 | bytes 308224 | tf_op jit(solution)/shard_map/add | solution.py:94
  99.6 4.0 %reshape.371 = f32[256,256]{1,0:T(8,128)S(1)} reshape(f32[32,8,32,8]{3,2,1,0:T(8,128)} %select_add_fusion) | data formatting | bytes 524288 | tf_op jit(solution)/shard_map/add | solution.py:94
  106.2 11.7 %cholesky.49 = f32[128,128]{1,0:T(8,128)S(1)} custom-call(f32[128,128]{1,0:T(8,128)S(1)} %cholesky.115), custom_call_target="Cholesky" | custom-call | tf_op jit(solution)/shard_map/jit(cholesky)/cholesky | solution.py:95
  118.4 9.8 %custom-call.16 = f32[1,128,128]{1,2,0:T(8,128)S(1)} custom-call(f32[1,128,128]{2,1,0:T(8,128)S(1)} %get-tuple-element.150), custom_call_target="InvertDiagBlocksLowerTriangular" | custom-call | tf_op jit(solution)/shard_map/jit(cholesky)/cholesky | solution.py:95
  130.4 11.7 %cholesky.103 = f32[128,128]{1,0:T(8,128)S(1)} custom-call(f32[128,128]{1,0:T(8,128)S(1)} %convolution_subtract_fusion), custom_call_target="Cholesky" | custom-call | tf_op jit(solution)/shard_map/jit(cholesky)/cholesky | solution.py:95
  147.1 5.2 %while.8 = (s32[]{:T(128)}, f32[256,256]{1,0:T(8,128)S(1)}, s32[2,2]{1,0:T(2,128)S(1)}, f32[2,128,128]{2,1,0:T(8,128)}, s32[]{:T(128)}) while((s32[]{:T(128)}, f32[256,256]{1,0:T(8,128)S(1)}, s32[2,2]{1,0:T(2,128)S(1)}, f32[2,128,128]{2,1,0:T(8,128)}, s32[]{:T(128)}) %tuple.106), condition=%wide.while_cond, body=%wide.while_body.sunk | while | flops 2 | bytes 132205 | solution.py:98
  152.4 20.7 %custom-call.20 = f32[2,128,128]{1,2,0:T(8,128)S(1)} custom-call(f32[2,128,128]{2,1,0:T(8,128)} %get-tuple-element.30), custom_call_target="InvertDiagBlocksLowerTriangular" | custom-call | tf_op jit(solution)/shard_map/jit(_cho_solve)/triangular_solve | solution.py:98
  180.3 8.3 %fusion.201 = f32[1,16,32,256]{3,0,2,1:T(1,128)S(1)} fusion(s32[]{:T(128)S(6)} %select_n.345, s32[]{:T(128)S(6)} %select_n.346, f32[4,8,8]{2,1,0:T(8,128)} %reshape.336, f32[8,16,32,256]{3,2,1,0:T(8,128)} %param.9), kind=kOutput, calls=%fused_computation.430 | convolution fusion | flops 12582912 | bytes 4719624 | tf_op jit(solution)/shard_map/kxyz,k->xyz/dot_general | solution.py:105
  196.9 10.8 %convolution_bitcast_fusion.4 = f32[8]{0:T(128)S(1)} fusion(f32[16,32,256,1]{2,0,1,3:T(8,128)S(1)} %bitcast.513, f32[8,16,32,256]{3,2,1,0:T(8,128)S(1)} %copy-done.2), kind=kOutput, calls=%fused_computation.33 | convolution fusion | flops 12582912 | bytes 4718624 | tf_op jit(solution)/shard_map/kxyz,xyz->k/dot_general | solution.py:77
  209.7 14.6 %all_to_all.20 = f32[32,1,128]{2,1,0:T(1,128)S(1)} all-to-all(f32[32,1,128]{2,1,0:T(1,128)S(1)} %broadcast_in_dim.221), channel_id=1, replica_groups=mesh['gx'=4,'gy'=8] {'gx','gy'}, dimensions={0} | all-to-all | bytes 32768 | tf_op jit(solution)/shard_map/all_to_all | solution.py:28
  233.0 9.1 %fusion.195 = f32[1,16,32,256]{3,0,2,1:T(1,128)} fusion(s32[]{:T(128)S(6)} %select_n.345, s32[]{:T(128)S(6)} %select_n.346, f32[4,8,8]{2,1,0:T(8,128)} %reshape.338, f32[8,16,32,256]{3,2,1,0:T(8,128)} %param.9), kind=kOutput, calls=%fused_computation.424 | convolution fusion | flops 12582912 | bytes 4719624 | tf_op jit(solution)/shard_map/kxyz,k->xyz/dot_general | solution.py:105
  265.1 10.7 %convolution_bitcast_fusion.3 = f32[8]{0:T(128)S(1)} fusion(f32[16,32,256,1]{2,0,1,3:T(8,128)S(1)} %bitcast.512, f32[8,16,32,256]{3,2,1,0:T(8,128)S(1)} %copy-done.3), kind=kOutput, calls=%fused_computation.32 | convolution fusion | flops 12582912 | bytes 4718624 | tf_op jit(solution)/shard_map/kxyz,xyz->k/dot_general | solution.py:77
  277.8 14.8 %all_to_all.21 = f32[32,1,128]{2,1,0:T(1,128)S(1)} all-to-all(f32[32,1,128]{2,1,0:T(1,128)S(1)} %broadcast_in_dim.230), channel_id=1, replica_groups=mesh['gx'=4,'gy'=8] {'gx','gy'}, dimensions={0} | all-to-all | bytes 32768 | tf_op jit(solution)/shard_map/all_to_all | solution.py:28
  301.3 9.1 %fusion.189 = f32[1,16,32,256]{3,0,2,1:T(1,128)} fusion(s32[]{:T(128)S(6)} %select_n.345, s32[]{:T(128)S(6)} %select_n.346, f32[4,8,8]{2,1,0:T(8,128)} %reshape.340, f32[8,16,32,256]{3,2,1,0:T(8,128)} %param.9), kind=kOutput, calls=%fused_computation.418 | convolution fusion | flops 12582912 | bytes 4719624 | tf_op jit(solution)/shard_map/kxyz,k->xyz/dot_general | solution.py:105
  329.7 10.7 %convolution_bitcast_fusion.2 = f32[8]{0:T(128)S(1)} fusion(f32[16,32,256,1]{2,0,1,3:T(8,128)S(1)} %bitcast.514, f32[8,16,32,256]{3,2,1,0:T(8,128)S(1)} %copy-done.4), kind=kOutput, calls=%fused_computation.31 | convolution fusion | flops 12582912 | bytes 4718624 | tf_op jit(solution)/shard_map/kxyz,xyz->k/dot_general | solution.py:77
  343.3 7.7 %all-to-all-start.3 = ((f32[32,1,128]{2,1,0:T(1,128)}), f32[32,1,128]{2,1,0:T(1,128)S(1)}, u32[]{:S(2)}, u32[]{:S(2)}) async-start(f32[32,1,128]{2,1,0:T(1,128)} %broadcast_in_dim.239), calls=%async_computation.3 | async-start | bytes 32768 | tf_op jit(solution)/shard_map/all_to_all | solution.py:28
  353.2 5.0 %all-to-all-done.3 = f32[32,1,128]{2,1,0:T(1,128)S(1)} async-done(((f32[32,1,128]{2,1,0:T(1,128)}), f32[32,1,128]{2,1,0:T(1,128)S(1)}, u32[]{:S(2)}, u32[]{:S(2)}) %all-to-all-start.3) | async-done | bytes 16416 | tf_op jit(solution)/shard_map/all_to_all | solution.py:28
  361.6 9.0 %fusion.183 = f32[1,16,32,256]{3,0,2,1:T(1,128)} fusion(s32[]{:T(128)S(6)} %select_n.345, s32[]{:T(128)S(6)} %select_n.346, f32[4,8,8]{2,1,0:T(8,128)S(1)} %reshape.342, f32[8,16,32,256]{3,2,1,0:T(8,128)} %param.9), kind=kOutput, calls=%fused_computation.412 | convolution fusion | flops 12582912 | bytes 4719624 | tf_op jit(solution)/shard_map/kxyz,k->xyz/dot_general | solution.py:105
  (344 shorter events, 143.5 us)
Async XLA Ops:
  3.9 19.3 %collective-permute-start.3 = (f32[10,16,256]{2,0,1:T(8,128)S(1)}, f32[10,16,256]{2,0,1:T(8,128)S(1)}, u32[]{:S(2)}, u32[]{:S(2)}) collective-permute-start(f32[10,16,256]{2,0,1:T(8,128)S(1)} %get-tuple-element.124), channel_id=1, source_target_pairs={{0,1},{1,0},{2,3},{3,2},{4,5},{5,4},{6,7},{7,6},{8,9},{9,8},{10,11... | collective-permute-start | bytes 491528 | tf_op jit(solution)/shard_map/ppermute | solution.py:16
  6.9 16.3 %collective-permute-start.2 = (f32[10,16,256]{2,0,1:T(8,128)S(1)}, f32[10,16,256]{2,0,1:T(8,128)}, u32[]{:S(2)}, u32[]{:S(2)}) collective-permute-start(f32[10,16,256]{2,0,1:T(8,128)S(1)} %get-tuple-element.125), channel_id=1, source_target_pairs={{1,2},{2,1},{3,4},{4,3},{5,6},{6,5},{9,10},{10,9},{11,12},{12,11},... | collective-permute-start | bytes 491528 | tf_op jit(solution)/shard_map/ppermute | solution.py:16
  18.4 12.8 %collective-permute-start.1 = (f32[10,32,256]{2,0,1:T(8,128)}, f32[10,32,256]{2,0,1:T(8,128)S(1)}, u32[]{:S(2)}, u32[]{:S(2)}) collective-permute-start(f32[10,32,256]{2,0,1:T(8,128)} %get-tuple-element.91), channel_id=1, source_target_pairs={{0,8},{8,0},{16,24},{24,16},{1,9},{9,1},{17,25},{25,17},{2,10},{10... | collective-permute-start | bytes 983048 | tf_op jit(solution)/shard_map/ppermute | solution.py:16
  18.4 13.6 %collective-permute-start = (f32[10,32,256]{2,0,1:T(8,128)}, f32[10,32,256]{2,0,1:T(8,128)}, u32[]{:S(2)}, u32[]{:S(2)}) collective-permute-start(f32[10,32,256]{2,0,1:T(8,128)} %get-tuple-element.92), channel_id=1, source_target_pairs={{8,16},{16,8},{9,17},{17,9},{10,18},{18,10},{11,19},{19,11},{12,20... | collective-permute-start | bytes 983048 | tf_op jit(solution)/shard_map/ppermute | solution.py:16
  33.3 156.2 %copy-start.9 = (f32[10,32,256]{2,0,1:T(8,128)}, f32[10,32,256]{2,0,1:T(8,128)S(1)}, u32[]{:S(2)}) copy-start(f32[10,32,256]{2,0,1:T(8,128)S(1)} %get-tuple-element.88) | copy-start | bytes 983044
  74.3 15.3 %all-to-all-start = ((f32[32,2,128]{2,1,0:T(2,128)}), f32[32,2,128]{2,1,0:T(2,128)S(1)}, u32[]{:S(2)}, u32[]{:S(2)}) async-start(f32[32,2,128]{2,1,0:T(2,128)} %broadcast_in_dim.197), calls=%async_computation | async-start | bytes 65536 | tf_op jit(solution)/shard_map/all_to_all | solution.py:28
  191.7 3.8 %collective-permute-start.6 = (f32[16,256]{1,0:T(8,128)S(1)}, f32[16,256]{1,0:T(8,128)S(1)}, u32[]{:S(2)}, u32[]{:S(2)}) collective-permute-start(f32[16,256]{1,0:T(8,128)S(1)} %get-tuple-element.105), channel_id=1, source_target_pairs={{0,1},{1,0},{2,3},{3,2},{4,5},{5,4},{6,7},{7,6},{8,9},{9,8},{10,11... | collective-permute-start | bytes 49160 | tf_op jit(solution)/shard_map/ppermute | solution.py:16
  192.4 3.1 collective-permute-start.7
  193.2 2.3 collective-permute-start.4
  193.3 2.2 collective-permute-start.5
  259.7 3.8 %collective-permute-start.10 = (f32[16,256]{1,0:T(8,128)S(1)}, f32[16,256]{1,0:T(8,128)S(1)}, u32[]{:S(2)}, u32[]{:S(2)}) collective-permute-start(f32[16,256]{1,0:T(8,128)S(1)} %get-tuple-element.101), channel_id=1, source_target_pairs={{0,1},{1,0},{2,3},{3,2},{4,5},{5,4},{6,7},{7,6},{8,9},{9,8},{10,11... | collective-permute-start | bytes 49160 | tf_op jit(solution)/shard_map/ppermute | solution.py:16
  260.4 3.1 collective-permute-start.11
  261.2 2.3 collective-permute-start.8
  261.3 2.2 collective-permute-start.9
  324.3 3.8 %collective-permute-start.14 = (f32[16,256]{1,0:T(8,128)S(1)}, f32[16,256]{1,0:T(8,128)S(1)}, u32[]{:S(2)}, u32[]{:S(2)}) collective-permute-start(f32[16,256]{1,0:T(8,128)S(1)} %get-tuple-element.97), channel_id=1, source_target_pairs={{0,1},{1,0},{2,3},{3,2},{4,5},{5,4},{6,7},{7,6},{8,9},{9,8},{10,11... | collective-permute-start | bytes 49160 | tf_op jit(solution)/shard_map/ppermute | solution.py:16
  325.0 3.1 collective-permute-start.15
  325.8 2.3 collective-permute-start.12
  325.9 2.2 collective-permute-start.13
  340.4 31.5 %copy-start.8 = (f32[16,32,256]{2,0,1:T(8,128)S(1)}, f32[16,32,256]{2,0,1:T(8,128)}, u32[]{:S(2)}) copy-start(f32[16,32,256]{2,0,1:T(8,128)} %copy-done.7) | copy-start | bytes 1572868
  340.4 31.5 %copy-start.21 = (f32[1,16,32,256]{3,0,2,1:T(1,128)S(1)}, f32[1,16,32,256]{3,0,2,1:T(1,128)}, u32[]{:S(2)}) copy-start(f32[1,16,32,256]{3,0,2,1:T(1,128)} %copy-done.20) | copy-start | bytes 1572868
  340.4 31.5 %copy-start.22 = (f32[1,16,32,256]{3,0,2,1:T(1,128)S(1)}, f32[1,16,32,256]{3,0,2,1:T(1,128)}, u32[]{:S(2)}) copy-start(f32[1,16,32,256]{3,0,2,1:T(1,128)} %fusion.195) | copy-start | bytes 1572868
  340.5 31.5 %copy-start.23 = (f32[1,16,32,256]{3,0,2,1:T(1,128)S(1)}, f32[1,16,32,256]{3,0,2,1:T(1,128)}, u32[]{:S(2)}) copy-start(f32[1,16,32,256]{3,0,2,1:T(1,128)} %fusion.189) | copy-start | bytes 1572868
  340.5 31.5 %copy-start.6 = (f32[16,32,256]{2,0,1:T(8,128)S(1)}, f32[16,32,256]{2,0,1:T(8,128)}, u32[]{:S(2)}) copy-start(f32[16,32,256]{2,0,1:T(8,128)} %copy-done.5) | copy-start | bytes 1572868
  343.3 14.8 %all-to-all-start.3 = ((f32[32,1,128]{2,1,0:T(1,128)}), f32[32,1,128]{2,1,0:T(1,128)S(1)}, u32[]{:S(2)}, u32[]{:S(2)}) async-start(f32[32,1,128]{2,1,0:T(1,128)} %broadcast_in_dim.239), calls=%async_computation.3 | async-start | bytes 32768 | tf_op jit(solution)/shard_map/all_to_all | solution.py:28
  (51 other events, 419.0 us)

commit v2 on v1

v2 whole, which is shorter than its diff:
```python
import functools

import jax
import jax.numpy as jnp
from jax import lax
from jax.experimental import pallas as pl
from jax.experimental.pallas import tpu as pltpu
from jax.sharding import PartitionSpec as P

ITERS = 2
BOTH = ("gx", "gy")
HIGH = lax.Precision.HIGHEST
F32 = jnp.float32
VMEM = pl.BlockSpec(memory_space=pltpu.VMEM)
SMEM = pl.BlockSpec(memory_space=pltpu.SMEM)


def swap(value, axis, parity):
    count = lax.axis_size(axis)
    pairs = []
    for low in range(parity, count - 1, 2):
        pairs += [(low, low + 1), (low + 1, low)]
    return lax.ppermute(value, axis, pairs)


def swaps(layers):
    return [swap(v, axis, parity) for v, (axis, parity) in zip(layers, (("gx", 0), ("gx", 1), ("gy", 0), ("gy", 1)))]


def everywhere(payload):
    return lax.all_to_all(payload, BOTH, 0, 0)


def face(lower, upper):
    summed = lower + upper
    inside = (lower > 0.0) & (upper > 0.0)
    return jnp.where(inside, 2.0 * lower * upper / summed, summed)


def iota(shape, dim):
    return lax.broadcasted_iota(jnp.int32, shape, dim)


def dot(a, b):
    return lax.dot_general(a, b, (((1,), (0,)), ((), ())), precision=HIGH, preferred_element_type=F32)


def fold(x):
    pieces = [x[r : r + 8, c : c + 128] for r in range(0, x.shape[0], 8) for c in range(0, x.shape[1], 128)]
    return functools.reduce(jnp.add, pieces)


def row_of(acc, count, width):
    total = functools.reduce(jnp.add, [acc[pl.ds(s, count, stride=8), :] for s in range(8)])
    if width > count:
        total = jnp.concatenate([total, jnp.zeros((width - count, 128), F32)], 0)
    sums = lax.dot_general(jnp.ones((8, 128), F32), total, (((1,), (1,)), ((), ())), precision=HIGH, preferred_element_type=F32)
    return sums[0:1]


def add_to(acc, index, x):
    acc[pl.ds(index * 8, 8), :] += fold(x)


def beside_y(v, low, high):
    rows = v.shape[0]
    row = iota(v.shape, 0)
    below = jnp.where(row == 0, low, pltpu.roll(v, 1, 0))
    above = jnp.where(row == rows - 1, high, pltpu.roll(v, rows - 1, 0))
    return below, above


def beside_z(v):
    return pltpu.roll(v, 1, 1), pltpu.roll(v, v.shape[1] - 1, 1)


def act(i, v, before, after, low, high, faces):
    fx, fyl, fyu, fzl, fzu, diag = faces
    below, above = beside_y(v, low, high)
    left, right = beside_z(v)
    out = diag[i] * v - fx[i] * before - fx[i + 1] * after
    return out - fyl[i] * below - fyu[i] * above - fzl[i] * left - fzu[i] * right


def prepare_kernel(ids, b, x0, coef, z, rx0, rx1, ry0, ry1, fx, fyl, fyu, fzl, fzu, diag, dinv, r0, zxl, zxh, zyl, zyh, out, cext, xext, yrow, acc, zy0):
    num, nx, ny, nz = z.shape
    evx, evy = ids[0] == 1, ids[1] == 1
    cext[0] = jnp.where(evx, rx1[0], rx0[0])
    cext[nx + 1] = jnp.where(evx, rx0[0], rx1[0])
    xext[0] = jnp.where(evx, rx1[1], rx0[1])
    xext[nx + 1] = jnp.where(evx, rx0[1], rx1[1])
    for k in range(num):
        zxl[k] = jnp.where(evx, rx1[2 + k], rx0[2 + k])
        zxh[k] = jnp.where(evx, rx0[2 + k], rx1[2 + k])
        zyl[k] = jnp.where(evy, ry1[2 + k], ry0[2 + k])
        zyh[k] = jnp.where(evy, ry0[2 + k], ry1[2 + k])
    for f in range(2):
        yrow[2 * f] = jnp.where(evy, ry1[f], ry0[f])
        yrow[2 * f + 1] = jnp.where(evy, ry0[f], ry1[f])
    acc[...] = jnp.zeros_like(acc)

    def fill(i, carry):
        cext[i + 1] = coef[i]
        xext[i + 1] = x0[i]
        return carry

    lax.fori_loop(0, nx, fill, 0)

    def faces_x(i, carry):
        fx[i] = face(cext[i], cext[i + 1])
        return carry

    lax.fori_loop(0, nx + 1, faces_x, 0)
    lane, row = iota((ny, nz), 1), iota((ny, nz), 0)

    def faces_yz(i, carry):
        c = cext[i + 1]
        below, above = beside_y(c, yrow[0, pl.ds(i, 1), :], yrow[1, pl.ds(i, 1), :])
        left, right = beside_z(c)
        yl, yu = face(below, c), face(c, above)
        zl, zu = face(jnp.where(lane == 0, 0.0, left), c), face(c, jnp.where(lane == nz - 1, 0.0, right))
        d = fx[i + 1] + fx[i] + yu + yl + zu + zl
        fyl[i], fyu[i] = yl, yu
        fzl[i], fzu[i] = jnp.where(lane == 0, 0.0, zl), jnp.where(lane == nz - 1, 0.0, zu)
        diag[i] = d
        dinv[i] = 1.0 / d
        return carry

    lax.fori_loop(0, nx, faces_yz, 0)
    faces = (fx, fyl, fyu, fzl, fzu, diag)
    square = num * num

    def plane(i, carry):
        r = b[i] - act(i, xext[i + 1], xext[i], xext[i + 2], yrow[2, pl.ds(i, 1), :], yrow[3, pl.ds(i, 1), :], faces)
        r0[i] = r
        fa = jnp.where(i > 0, fx[i], 0.0)
        fb = jnp.where(i < nx - 1, fx[i + 1], 0.0)
        before, after = jnp.maximum(i - 1, 0), jnp.minimum(i + 1, nx - 1)
        yl, yu = jnp.where(row == 0, 0.0, fyl[i]), jnp.where(row == ny - 1, 0.0, fyu[i])
        for k in range(num):
            v = z[k, i]
            left, right = beside_z(v)
            w = diag[i] * v - fa * z[k, before] - fb * z[k, after] - fzl[i] * left - fzu[i] * right
            w = w - yl * pltpu.roll(v, 1, 0) - yu * pltpu.roll(v, ny - 1, 0)
            for m in range(k + 1):
                add_to(acc, 2 * square + m * num + k, w * z[m, i])
            add_to(acc, 3 * square + k, v * r)
            zy0[k, pl.ds(i, 1), :] = v[0:1, :] * fyl[i, 0:1, :]
        return carry

    lax.fori_loop(0, nx, plane, 0)
    for k in range(num):
        for m in range(k):
            acc[pl.ds((2 * square + k * num + m) * 8, 8), :] = acc[pl.ds((2 * square + m * num + k) * 8, 8), :]

    def below_blocks(k, carry):
        weighted = z[k, 0] * fx[0]
        for m in range(num):
            add_to(acc, k * num + m, weighted * zxl[m])
            add_to(acc, square + k * num + m, zy0[k] * zyl[m])
        return carry

    lax.fori_loop(0, num, below_blocks, 0)
    count = acc.shape[0] // 8
    line = row_of(acc, count, count)
    for part in range(count // 128):
        out[:, part, :] = jnp.broadcast_to(line[:, part * 128 : (part + 1) * 128], (out.shape[0], 128))


def small_inverse(p):
    size = p.shape[0]
    lane, row = iota(p.shape, 1), iota(p.shape, 0)
    head = iota((1, size), 1)
    for k in range(0, size, 2):
        r0, r1 = p[k : k + 1, :], p[k + 1 : k + 2, :]
        c0, c1 = p[:, k : k + 1], p[:, k + 1 : k + 2]
        a, b = p[k : k + 1, k : k + 1], p[k : k + 1, k + 1 : k + 2]
        c, d = p[k + 1 : k + 2, k : k + 1], p[k + 1 : k + 2, k + 1 : k + 2]
        over = 1.0 / (a * d - b * c)
        r0 = jnp.where(head == k, 1.0, jnp.where(head == k + 1, 0.0, r0))
        r1 = jnp.where(head == k, 0.0, jnp.where(head == k + 1, 1.0, r1))
        n0 = (d * over) * r0 - (b * over) * r1
        n1 = (a * over) * r1 - (c * over) * r0
        p = jnp.where((lane == k) | (lane == k + 1), 0.0, p) - c0 * n0 - c1 * n1
        p = jnp.where(row == k, n0, jnp.where(row == k + 1, n1, p))
    return p


def invert(e):
    order = e.shape[0]
    size = 32

    def step(s, carry):
        a = e[...]
        pivot = small_inverse(a[0:size, 0:size])
        right = dot(pivot, a[0:size, :])
        lane = iota((1, order), 1) < size
        corner = jnp.concatenate([pivot, jnp.zeros((size, order - size), F32)], 1)
        right = jnp.where(lane, corner, right)
        rest = jnp.where(lane, 0.0, a[size:, :]) - dot(a[size:, 0:size], right)
        e[0 : order - size, :] = pltpu.roll(rest, order - size, 1)
        e[order - size :, :] = pltpu.roll(right, order - size, 1)
        return carry

    lax.fori_loop(0, order // size, step, 0)


def column(g, num, order, offset, base):
    n = g.shape[0]
    pick = jnp.where(iota((order, n), 1) == lax.div(iota((order, n), 0), num) + offset, 1.0, 0.0)
    spread = dot(pick, g)
    lane, row = iota(spread.shape, 1), iota(spread.shape, 0)
    return jnp.sum(jnp.where(lane == base + lax.rem(row, num), spread, 0.0), axis=1, keepdims=True)


def matrix_from(got, num, across, e):
    order = e.shape[0]
    n = got.shape[0]
    square = num * num
    pick = jnp.where(iota((order, n), 1) == lax.div(iota((order, n), 0), num), 1.0, 0.0)
    lane, row = iota((order, 128), 1), iota((order, 128), 0)
    keep = lax.div(lax.rem(lane, square), num) == lax.rem(row, num)
    first = jnp.where(keep, dot(pick, got[:, 0, :]), 0.0)
    second = jnp.where(keep, dot(pick, got[:, 1, :]), 0.0)
    t, c = iota((128, order), 0), iota((128, order), 1)
    same = lax.rem(t, num) == lax.rem(c, num)
    low = jnp.where(same & (t < square), 1.0, 0.0)
    high = jnp.where(same & (t >= square), 1.0, 0.0)
    bi, bj = lax.div(iota((order, order), 0), num), lax.div(iota((order, order), 1), num)
    lower = jnp.where(bj == bi - across, dot(first, low), 0.0) + jnp.where(bj == bi - 1, dot(first, high), 0.0)
    e[...] = jnp.where(bi == bj, dot(second, low), 0.0) - lower - lower.T


def solve(e, col):
    return jnp.sum(e[...] * col, axis=0, keepdims=True)


def amounts(ids, solved, num, across):
    order = solved.shape[1]
    turned = pltpu.roll(jnp.broadcast_to(solved, (8, order)), ids[2], 1)
    take = lambda at: [turned[0:1, (at + k) % order : (at + k) % order + 1] for k in range(num)]
    return [take(at * num) for at in (0, -across, across, -1, 1)]


def combine(y, vectors):
    return functools.reduce(jnp.add, [c * v for c, v in zip(y, vectors)])


def spread_out(ys, z, zxl, zxh, zyl, zyh, gext, gy):
    num, nx, ny, nz = z.shape
    gext[0] = combine(ys[1], [zxl[k] for k in range(num)])
    gext[nx + 1] = combine(ys[2], [zxh[k] for k in range(num)])
    gy[0] = combine(ys[3], [zyl[k] for k in range(num)])
    gy[1] = combine(ys[4], [zyh[k] for k in range(num)])
    wide = [jnp.broadcast_to(c, (ny, nz)) for c in ys[0]]

    def plane(i, carry):
        gext[i + 1] = combine(wide, [z[k, i] for k in range(num)])
        return carry

    lax.fori_loop(0, nx, plane, 0)


def send_rows(i, p, evy, sy0, sy1):
    low, high = p[0:1, :], p[p.shape[0] - 1 :, :]
    sy0[pl.ds(i, 1), :] = jnp.where(evy, high, low)
    sy1[pl.ds(i, 1), :] = jnp.where(evy, low, high)


def send_planes(p, evx, sx0, sx1):
    low, high = p[0], p[p.shape[0] - 1]
    sx0[...] = jnp.where(evx, high, low)
    sx1[...] = jnp.where(evx, low, high)


def start_kernel(across, ids, got, x0, r0, z, zxl, zxh, zyl, zyh, fx, fyl, fyu, fzl, fzu, diag, dinv, e, x, r, p, sx0, sx1, sy0, sy1, gext, gy):
    num, nx, ny, nz = z.shape
    order = e.shape[0]
    matrix_from(got, num, across, e)
    invert(e)
    solved = solve(e, column(got[:, 1, :], num, order, 0, num * num))
    spread_out(amounts(ids, solved, num, across), z, zxl, zxh, zyl, zyh, gext, gy)
    faces = (fx, fyl, fyu, fzl, fzu, diag)
    evx, evy = ids[0] == 1, ids[1] == 1

    def plane(i, carry):
        g = gext[i + 1]
        image = act(i, g, gext[i], gext[i + 2], gy[0, pl.ds(i, 1), :], gy[1, pl.ds(i, 1), :], faces)
        x[i] = x0[i] + g
        rest = r0[i] - image
        r[i] = rest
        pre = rest * dinv[i]
        p[i] = pre
        send_rows(i, pre, evy, sy0, sy1)
        return carry

    lax.fori_loop(0, nx, plane, 0)
    send_planes(p, evx, sx0, sx1)


def product_kernel(first, *refs):
    ids, p, r, z, fx, fyl, fyu, fzl, fzu, diag, rx0, rx1, ry0, ry1 = refs[:14]
    applied = None if first else refs[14]
    ap, out, pext, py, acc = refs[-5:]
    num, nx, ny, nz = z.shape
    faces = (fx, fyl, fyu, fzl, fzu, diag)
    evx, evy = ids[0] == 1, ids[1] == 1
    pext[0] = jnp.where(evx, rx1[...], rx0[...])
    pext[nx + 1] = jnp.where(evx, rx0[...], rx1[...])
    py[0] = jnp.where(evy, ry1[...], ry0[...])
    py[1] = jnp.where(evy, ry0[...], ry1[...])
    acc[...] = jnp.zeros_like(acc)

    def fill(i, carry):
        pext[i + 1] = p[i]
        return carry

    lax.fori_loop(0, nx, fill, 0)

    def plane(i, carry):
        v = pext[i + 1]
        w = act(i, v, pext[i], pext[i + 2], py[0, pl.ds(i, 1), :], py[1, pl.ds(i, 1), :], faces)
        ap[i] = w
        add_to(acc, 0, v * r[i])
        add_to(acc, 1, v * w)
        if not first:
            add_to(acc, 2, v * applied[i])
        for k in range(num):
            add_to(acc, 3 + k, w * z[k, i])
        return carry

    lax.fori_loop(0, nx, plane, 0)
    out[:, 0, :] = jnp.broadcast_to(row_of(acc, acc.shape[0] // 8, 128), (out.shape[0], 128))


def update_kernel(first, last, across, *refs):
    ids, got, e, z, zxl, zxh, zyl, zyh, fx, fyl, fyu, fzl, fzu, diag, dinv, p, ap, x, r = refs[:19]
    at = 19
    if not first:
        d_old, ad_old, state_old = refs[at : at + 3]
        at += 3
    d, ad, x_new, r_new, p_new, state = refs[at : at + 6]
    at += 6
    if last:
        out, gext, gy, acc, py = refs[at:]
    else:
        sx0, sx1, sy0, sy1, gext, gy = refs[at:]
    num, nx, ny, nz = z.shape
    order = e.shape[0]
    faces = (fx, fyl, fyu, fzl, fzu, diag)
    g = got[:, 0, :]
    totals = jnp.sum(g, axis=0, keepdims=True)
    new, energy_p, cross = totals[:, 0:1], totals[:, 1:2], totals[:, 2:3]
    col = column(g, num, order, 0, 3)
    solved = solve(e, col)
    same = iota((order, order), 0) == iota((order, order), 1)
    line = jnp.sum(jnp.where(same, col, 0.0), axis=0, keepdims=True)
    energy = energy_p - jnp.sum(solved * line, axis=1, keepdims=True)
    if not first:
        beta = new / state_old[0:1, 0:1]
        energy = energy + 2.0 * beta * cross + beta * beta * state_old[1:2, 0:1]
        wide_beta = jnp.broadcast_to(beta, (ny, nz))
    step = jnp.broadcast_to(new / energy, (ny, nz))
    state[0:1, :] = jnp.broadcast_to(new, (1, 128))
    state[1:2, :] = jnp.broadcast_to(energy, (1, 128))
    state[2:8, :] = jnp.zeros((6, 128), F32)
    spread_out(amounts(ids, solved, num, across), z, zxl, zxh, zyl, zyh, gext, gy)
    evx, evy = ids[0] == 1, ids[1] == 1

    def plane(i, carry):
        c = gext[i + 1]
        image = act(i, c, gext[i], gext[i + 2], gy[0, pl.ds(i, 1), :], gy[1, pl.ds(i, 1), :], faces)
        way, acted = p[i] - c, ap[i] - image
        if not first:
            way, acted = way + wide_beta * d_old[i], acted + wide_beta * ad_old[i]
        d[i] = way
        ad[i] = acted
        x_new[i] = x[i] + step * way
        rest = r[i] - step * acted
        r_new[i] = rest
        pre = rest * dinv[i]
        p_new[i] = pre
        if last:
            add_to(acc, 0, rest * pre)
            py[0, pl.ds(i, 1), :] = pre[0:1, :] * fyl[i, 0:1, :]
            py[1, pl.ds(i, 1), :] = pre[ny - 1 : ny, :] * fyu[i, ny - 1 : ny, :]
        else:
            send_rows(i, pre, evy, sy0, sy1)
        return carry

    if last:
        acc[...] = jnp.zeros_like(acc)
    lax.fori_loop(0, nx, plane, 0)
    if not last:
        send_planes(p_new, evx, sx0, sx1)
        return
    row = iota((ny, nz), 0)

    def second(i, carry):
        v = p_new[i]
        left, right = beside_z(v)
        fa = jnp.where(i > 0, fx[i], 0.0)
        fb = jnp.where(i < nx - 1, fx[i + 1], 0.0)
        w = diag[i] * v - fa * p_new[jnp.maximum(i - 1, 0)] - fb * p_new[jnp.minimum(i + 1, nx - 1)]
        w = w - fzl[i] * left - fzu[i] * right - jnp.where(row == 0, 0.0, fyl[i]) * pltpu.roll(v, 1, 0)
        w = w - jnp.where(row == ny - 1, 0.0, fyu[i]) * pltpu.roll(v, ny - 1, 0)
        for k in range(num):
            add_to(acc, 8 + k, w * z[k, i])
        return carry

    lax.fori_loop(0, nx, second, 0)
    low, high = p_new[0] * fx[0], p_new[nx - 1] * fx[nx]
    for k in range(num):
        add_to(acc, 8 + num + k, -low * zxl[k])
        add_to(acc, 8 + 2 * num + k, -high * zxh[k])
        add_to(acc, 8 + 3 * num + k, -py[0] * zyl[k])
        add_to(acc, 8 + 4 * num + k, -py[1] * zyh[k])
    out[:, 0, :] = jnp.broadcast_to(row_of(acc, acc.shape[0] // 8, 128), (out.shape[0], 128))


def finish_kernel(across, ids, got, e, z, p, d_old, state_old, d):
    num, nx, ny, nz = z.shape
    order = e.shape[0]
    g = got[:, 0, :]
    beta = jnp.sum(g, axis=0, keepdims=True)[:, 0:1] / state_old[0:1, 0:1]
    col = column(g, num, order, 0, 8)
    for group, offset in ((1, across), (2, -across), (3, 1), (4, -1)):
        col = col + column(g, num, order, offset, 8 + group * num)
    ys = amounts(ids, solve(e, col), num, across)
    wide = [jnp.broadcast_to(c, (ny, nz)) for c in ys[0]]
    wide_beta = jnp.broadcast_to(beta, (ny, nz))

    def plane(i, carry):
        d[i] = p[i] + wide_beta * d_old[i] - combine(wide, [z[k, i] for k in range(num)])
        return carry

    lax.fori_loop(0, nx, plane, 0)


def call(kernel, name, args, outs, scratch):
    return pl.pallas_call(
        kernel,
        name=name,
        in_specs=[SMEM] + [VMEM] * (len(args) - 1),
        out_specs=[VMEM] * len(outs),
        out_shape=[jax.ShapeDtypeStruct(s, F32) for s in outs],
        scratch_shapes=[pltpu.VMEM(s, F32) for s in scratch],
        compiler_params=pltpu.CompilerParams(vmem_limit_bytes=48 * 1024 * 1024),
    )(*args)


def per_device(right_side, start_field, coef, deflation):
    num, nx, ny, nz = deflation.shape
    down, across = lax.axis_size("gx"), lax.axis_size("gy")
    n = down * across
    order = n * num
    ix, iy = lax.axis_index("gx"), lax.axis_index("gy")
    evx, evy = ix % 2 == 0, iy % 2 == 0
    ids = jnp.stack([evx.astype(jnp.int32), evy.astype(jnp.int32), (order - (ix * across + iy) * num) % order])

    def pack(at, index):
        return jnp.concatenate([at(coef, index)[None], at(start_field, index)[None], at(deflation, index)])

    at_x = lambda v, i: lax.dynamic_index_in_dim(v, i, v.ndim - 3, keepdims=False)
    at_y = lambda v, i: lax.dynamic_index_in_dim(v, i, v.ndim - 2, keepdims=False)
    xs = (jnp.where(evx, nx - 1, 0), jnp.where(evx, 0, nx - 1))
    ys = (jnp.where(evy, ny - 1, 0), jnp.where(evy, 0, ny - 1))
    raw = swaps([pack(at_x, xs[0]), pack(at_x, xs[1]), pack(at_y, ys[0]), pack(at_y, ys[1])])

    field, layer_x, layer_y = (nx, ny, nz), (ny, nz), (nx, nz)
    ext, two_y = (nx + 2, ny, nz), (2, nx, nz)
    layers = [layer_x, layer_x, layer_y, layer_y]
    wide = -(-(3 * num * num + num) // 128)
    *faces, dinv, r0, zxl, zxh, zyl, zyh, out = call(
        prepare_kernel,
        "prepare",
        [ids, right_side, start_field, coef, deflation, *raw],
        [(nx + 1, ny, nz)] + [field] * 7 + [(num,) + layer_x] * 2 + [(num,) + layer_y] * 2 + [(n, wide, 128)],
        [ext, ext, (4, nx, nz), (wide * 128 * 8, 128), (num, nx, nz)],
    )
    basis = [deflation, zxl, zxh, zyl, zyh]
    e, x, r, p, *sent = call(
        functools.partial(start_kernel, across),
        "start",
        [ids, everywhere(out), start_field, r0, *basis, *faces, dinv],
        [(order, order)] + [field] * 3 + layers,
        [ext, two_y],
    )
    old = []
    for iteration in range(ITERS):
        first, last = iteration == 0, iteration == ITERS - 1
        ap, out = call(
            functools.partial(product_kernel, first),
            "product",
            [ids, p, r, deflation, *faces, *swaps(sent)] + old[1:2],
            [field, (n, 1, 128)],
            [ext, two_y, (16 * 8, 128)],
        )
        d, ad, x, r, p, state, *sent = call(
            functools.partial(update_kernel, first, last, across),
            "update",
            [ids, everywhere(out), e, *basis, *faces, dinv, p, ap, x, r] + old,
            [field] * 5 + [(8, 128)] + ([(n, 1, 128)] if last else layers),
            [ext, two_y] + ([(48 * 8, 128), two_y] if last else []),
        )
        old = [d, ad, state]
    (direction,) = call(
        functools.partial(finish_kernel, across),
        "finish",
        [ids, everywhere(sent[0]), e, deflation, p, d, state],
        [field],
        [],
    )
    return x, r, direction


def solution(mesh):
    field = P("gx", "gy", None)
    return jax.shard_map(
        per_device,
        mesh=mesh,
        in_specs=(field, field, field, P(None, "gx", "gy", None)),
        out_specs=(field, field, field),
        check_vma=False,
    )
```

time: 384 us -> 169 us (0.44); the launches traced: 377 us -> 169 us
  matrix products: 112 us -> 0 us
  other arithmetic: 103 us -> 0.15 us
  Pallas kernels: 0 us -> 85.2 us
  local copies, waits for them, and re-layouts: 76.8 us -> 8.96 us
  blocking collectives: 29.5 us -> 57.2 us
  starting transfers between devices: 30 us -> 8.73 us
  between operations: 11 us -> 1.05 us
  waiting for transfers between devices: 15 us -> 7.37 us
    dot_general x23 -> x0, matrix products: 101 us -> none  [the longest x4 43.1 us: restrict(): return jnp.einsum('kxyz,xyz->k', deflation, values, precision=highest)]
    pallas_call x0 -> x7, Pallas kernels: none -> 85.2 us  [call(): pl.pallas_call(kernel, name=name, in_specs=[SMEM] + [VMEM] * (len(args) -...]
    another operation x15 -> x1, other arithmetic: 58.6 us -> 0.08 us  [per_device(): jnp.stack([evx.astype(jnp.int32), evy.astype(jnp.int32), (order - (ix * a...]
    all_to_all x2 -> x4, blocking collectives: 29.5 us -> 57.2 us  [everywhere(): return lax.all_to_all(payload, BOTH, 0, 0)]
    all_to_all x2 -> x0, starting transfers between devices: 15.9 us -> none  [everywhere(): lax.all_to_all(jnp.broadcast_to(payload[None], (count,) + payload.shape),...]
    slice x26 -> x0, local copies, waits for them, and re-layouts: 15.5 us -> none  [the longest x2 2.24 us: per_device(): fx[:-1]]
    unnamed x122 -> x46, local copies, waits for them, and re-layouts: 17.2 us -> 4.07 us
    all_to_all x2 -> x0, waiting for transfers between devices: 11.6 us -> none  [everywhere(): lax.all_to_all(jnp.broadcast_to(payload[None], (count,) + payload.shape),...]
  transfers between devices with their start and end apart: 18 -> 12, of which waited for: 5 -> 3; matrix products, arithmetic and copies ran while one was open for 6% -> 2% of each run, Pallas kernels for 0% -> 0%
where the time goes in v2:
time: 169 us
  Pallas kernels  85.2 us (50%)
  blocking collectives  57.2 us (34%)
  local copies, waits for them, and re-layouts  8.96 us (5%)
  starting transfers between devices  8.73 us (5%)
  waiting for transfers between devices  7.37 us (4%)
    pallas_call x7, Pallas kernels, call(): pl.pallas_call(kernel, name=name, in_specs=[SMEM] + [VMEM] * (len(args) -...  85.2 us
    all_to_all x4, blocking collectives, everywhere(): return lax.all_to_all(payload, BOTH, 0, 0)  57.2 us
    ppermute x12, starting transfers between devices, swap(): return lax.ppermute(value, axis, pairs)  8.73 us
    ppermute x12, waiting for transfers between devices, swap(): return lax.ppermute(value, axis, pairs)  7.37 us
    unnamed x46, local copies, waits for them, and re-layouts  4.07 us
  transfers between devices with their start and end apart: 12, of which 3 were waited for; matrix products, arithmetic and copies ran while one was open for 2% of the time, Pallas kernels for 0%

profile of v2, /device:TPU:0, one launch (start us, length us, event | category | flops | bytes accessed | tf_op | source)
XLA Modules:
  0.0 168.7 jit_solution(3327828569468849158)
XLA Ops:
  0.7 1.1 dynamic-slice_bitcast_fusion
  1.8 0.8 constant_dynamic-slice_fusion.6
  3.9 1.2 constant_dynamic-slice_fusion.1
  5.1 1.8 %constant_dynamic-slice_fusion = (f32[8,16,1,256]{3,2,1,0:T(1,128)S(1)}, f32[8,16,1,256]{3,2,1,0:T(1,128)S(1)}) fusion(f32[8,16,32,256]{3,2,1,0:T(8,128)} %z.5, s32[]{:T(128)S(6)} %select_n.50, s32[]{:T(128)S(6)} %select_n.49), kind=kLoop, calls=%fused_computation.12 | loop fusion | bytes 524296 | tf_op jit(solution)/shard_map/jit(dynamic_index_in_dim)/dynamic_slice | solution.py:465
  6.9 2.6 %collective-permute-start.2 = (f32[10,16,256]{2,1,0:T(8,128)S(1)}, f32[10,16,256]{2,1,0:T(8,128)S(1)}, u32[]{:S(2)}, u32[]{:S(2)}) collective-permute-start(f32[10,16,256]{2,1,0:T(8,128)S(1)} %pad_maximum_fusion.2), channel_id=1, source_target_pairs={{0,1},{1,0},{2,3},{3,2},{4,5},{5,4},{6,7},{7,6},{8,9},{9,8},{10,11... | collective-permute-start | bytes 491528 | tf_op jit(solution)/shard_map/ppermute | solution.py:23
  10.3 2.5 %collective-permute-done.2.ry0 = f32[10,16,256]{2,1,0:T(8,128)S(1)} collective-permute-done((f32[10,16,256]{2,1,0:T(8,128)S(1)}, f32[10,16,256]{2,1,0:T(8,128)S(1)}, u32[]{:S(2)}, u32[]{:S(2)}) %collective-permute-start.2) | collective-permute-done | bytes 163872 | tf_op jit(solution)/shard_map/ppermute | solution.py:23
  12.8 11.4 %prepare.1 = (f32[17,32,256]{2,1,0:T(8,128)}, f32[16,32,256]{2,1,0:T(8,128)S(1)}, f32[16,32,256]{2,1,0:T(8,128)S(1)}, f32[16,32,256]{2,1,0:T(8,128)S(1)}, f32[16...) custom-call(s32[3]{0:T(128)S(1)} %pad_add_fusion.ids.refs_0_, ...), custom_call_target="tpu_custom_call" | custom-call | tf_op jit(solution)/shard_map/prepare/pallas_call | solution.py:441
  24.2 0.8 copy-done.3
  25.0 0.8 copy-done.6
  25.8 18.6 %all_to_all.20.got = f32[32,2,128]{2,1,0:T(2,128)S(1)} all-to-all(f32[32,2,128]{2,1,0:T(2,128)S(1)} %get-tuple-element.44), channel_id=1, replica_groups=mesh['gx'=4,'gy'=8] {'gx','gy'}, dimensions={0} | all-to-all | bytes 65536 | tf_op jit(solution)/shard_map/all_to_all | solution.py:31
  44.3 48.1 %start.1 = (f32[256,256]{1,0:T(8,128)S(1)}, f32[16,32,256]{2,1,0:T(8,128)S(1)}, f32[16,32,256]{2,1,0:T(8,128)S(1)}, f32[16,32,256]{2,1,0:T(8,128)S(1)}, f32[32,2...) custom-call(s32[3]{0:T(128)S(1)} %pad_add_fusion.ids.refs_0_, ...), custom_call_target="tpu_custom_call" | custom-call | tf_op jit(solution)/shard_map/start/pallas_call | solution.py:441
  94.7 2.4 %collective-permute-done.6.refs_12_ = f32[16,256]{1,0:T(8,128)S(1)} collective-permute-done((f32[16,256]{1,0:T(8,128)S(1)}, f32[16,256]{1,0:T(8,128)S(1)}, u32[]{:S(2)}, u32[]{:S(2)}) %collective-permute-start.6) | collective-permute-done | bytes 16416 | tf_op jit(solution)/shard_map/ppermute | solution.py:23
  97.2 4.2 %product.2 = (f32[16,32,256]{2,1,0:T(8,128)S(1)}, f32[32,1,128]{2,1,0:T(1,128)S(1)}) custom-call(s32[3]{0:T(128)S(1)} %pad_add_fusion.ids.refs_0_, f32[16,32,256]{2,1,0:T(8,128)S(1)} %get-tuple-element.57.refs_1_.refs_15_, f32[16,32,256]{2,1,0:T(8,128)S(1)} %get-tuple-element.58.refs_2_.refs_18_, f32[8,16,32,256]{3,2,1,0:T(8,128)} %z.5, ...), custom_call_target="tpu_custom_call" | custom-call | tf_op jit(solution)/shard_map/product/pallas_call | solution.py:441
  101.4 0.8 copy-done.18
  102.2 14.9 %all_to_all.21.refs_1_ = f32[32,1,128]{2,1,0:T(1,128)S(1)} all-to-all(f32[32,1,128]{2,1,0:T(1,128)S(1)} %get-tuple-element.63), channel_id=1, replica_groups=mesh['gx'=4,'gy'=8] {'gx','gy'}, dimensions={0} | all-to-all | bytes 32768 | tf_op jit(solution)/shard_map/all_to_all | solution.py:31
  117.1 5.8 %update.2 = (f32[16,32,256]{2,1,0:T(8,128)S(1)}, f32[16,32,256]{2,1,0:T(8,128)S(1)}, f32[16,32,256]{2,1,0:T(8,128)S(1)}, f32[16,32,256]{2,1,0:T(8,128)S(1)}, f32...) custom-call(s32[3]{0:T(128)S(1)} %pad_add_fusion.ids.refs_0_, ...), custom_call_target="tpu_custom_call" | custom-call | tf_op jit(solution)/shard_map/update/pallas_call | solution.py:441
  123.0 0.8 copy-done.14
  125.8 2.5 %collective-permute-done.10.refs_12_ = f32[16,256]{1,0:T(8,128)S(1)} collective-permute-done((f32[16,256]{1,0:T(8,128)S(1)}, f32[16,256]{1,0:T(8,128)S(1)}, u32[]{:S(2)}, u32[]{:S(2)}) %collective-permute-start.10) | collective-permute-done | bytes 16416 | tf_op jit(solution)/shard_map/ppermute | solution.py:23
  128.4 4.3 %product.3 = (f32[16,32,256]{2,1,0:T(8,128)S(1)}, f32[32,1,128]{2,1,0:T(1,128)S(1)}) custom-call(s32[3]{0:T(128)S(1)} %pad_add_fusion.ids.refs_0_, f32[16,32,256]{2,1,0:T(8,128)S(1)} %get-tuple-element.67.refs_1_.refs_15_, f32[16,32,256]{2,1,0:T(8,128)S(1)} %get-tuple-element.68.refs_2_.refs_18_, f32[8,16,32,256]{3,2,1,0:T(8,128)} %z.5, ...), custom_call_target="tpu_custom_call" | custom-call | tf_op jit(solution)/shard_map/product/pallas_call | solution.py:441
  132.7 0.8 copy-done.17
  133.5 14.9 %all_to_all.22.refs_1_ = f32[32,1,128]{2,1,0:T(1,128)S(1)} all-to-all(f32[32,1,128]{2,1,0:T(1,128)S(1)} %get-tuple-element.74), channel_id=1, replica_groups=mesh['gx'=4,'gy'=8] {'gx','gy'}, dimensions={0} | all-to-all | bytes 32768 | tf_op jit(solution)/shard_map/all_to_all | solution.py:31
  148.4 8.8 %update.3 = (f32[16,32,256]{2,1,0:T(8,128)S(1)}, f32[16,32,256]{2,1,0:T(8,128)}, f32[16,32,256]{2,1,0:T(8,128)}, f32[16,32,256]{2,1,0:T(8,128)}, f32[16,32,256]{...) custom-call(s32[3]{0:T(128)S(1)} %pad_add_fusion.ids.refs_0_, f32[32,1,128]{2,1,0:T(1,128)S(1)} %all_to_all.22.refs_1_, ...), custom_call_target="tpu_custom_call" | custom-call | tf_op jit(solution)/shard_map/update/pallas_call | solution.py:441
  157.2 8.8 %all_to_all.23.got = f32[32,1,128]{2,1,0:T(1,128)S(1)} all-to-all(f32[32,1,128]{2,1,0:T(1,128)S(1)} %get-tuple-element.81), channel_id=1, replica_groups=mesh['gx'=4,'gy'=8] {'gx','gy'}, dimensions={0} | all-to-all | bytes 32768 | tf_op jit(solution)/shard_map/all_to_all | solution.py:31
  166.0 2.7 %finish.1 = f32[16,32,256]{2,1,0:T(8,128)} custom-call(s32[3]{0:T(128)S(1)} %pad_add_fusion.ids.refs_0_, f32[32,1,128]{2,1,0:T(1,128)S(1)} %all_to_all.23.got, f32[256,256]{1,0:T(8,128)S(1)} %get-tuple-element.64.refs_2_.e, f32[8,16,32,256]{3,2,1,0:T(8,128)S(1)} %copy-done, f32[16,32,256]{2,1,0:T(8,128)S(1)} %get-tuple-element.82.p, ...), custom_call_target="tpu_custom_call" | custom-call | tf_op jit(solution)/shard_map/finish/pallas_call | solution.py:441
  (66 shorter events, 6.4 us)
Async XLA Ops:
  0.6 12.2 %copy-start.19 = (f32[16,32,256]{2,1,0:T(8,128)S(1)}, f32[16,32,256]{2,1,0:T(8,128)}, u32[]{:S(2)}) copy-start(f32[16,32,256]{2,1,0:T(8,128)} %b.1) | copy-start | bytes 1572868
  2.6 10.1 %collective-permute-start = (f32[10,32,256]{2,1,0:T(8,128)S(1)}, f32[10,32,256]{2,1,0:T(8,128)S(1)}, u32[]{:S(2)}, u32[]{:S(2)}) collective-permute-start(f32[10,32,256]{2,1,0:T(8,128)S(1)} %pad_maximum_fusion), channel_id=1, source_target_pairs={{0,8},{8,0},{16,24},{24,16},{1,9},{9,1},{17,25},{25,17},{2,10},{10... | collective-permute-start | bytes 983048 | tf_op jit(solution)/shard_map/ppermute | solution.py:23
  3.2 9.6 %collective-permute-start.1 = (f32[10,32,256]{2,1,0:T(8,128)S(1)}, f32[10,32,256]{2,1,0:T(8,128)S(1)}, u32[]{:S(2)}, u32[]{:S(2)}) collective-permute-start(f32[10,32,256]{2,1,0:T(8,128)S(1)} %pad_maximum_fusion.1), channel_id=1, source_target_pairs={{8,16},{16,8},{9,17},{17,9},{10,18},{18,10},{11,19},{19,11},{12,20... | collective-permute-start | bytes 983048 | tf_op jit(solution)/shard_map/ppermute | solution.py:23
  6.8 37.5 %copy-start.8 = (f32[16,32,256]{2,1,0:T(8,128)S(1)}, f32[16,32,256]{2,1,0:T(8,128)}, u32[]{:S(2)}) copy-start(f32[16,32,256]{2,1,0:T(8,128)} %x0.3) | copy-start | bytes 1572868
  6.9 5.9 %collective-permute-start.2 = (f32[10,16,256]{2,1,0:T(8,128)S(1)}, f32[10,16,256]{2,1,0:T(8,128)S(1)}, u32[]{:S(2)}, u32[]{:S(2)}) collective-permute-start(f32[10,16,256]{2,1,0:T(8,128)S(1)} %pad_maximum_fusion.2), channel_id=1, source_target_pairs={{0,1},{1,0},{2,3},{3,2},{4,5},{5,4},{6,7},{7,6},{8,9},{9,8},{10,11... | collective-permute-start | bytes 491528 | tf_op jit(solution)/shard_map/ppermute | solution.py:23
  9.5 3.3 %collective-permute-start.3 = (f32[10,16,256]{2,1,0:T(8,128)S(1)}, f32[10,16,256]{2,1,0:T(8,128)S(1)}, u32[]{:S(2)}, u32[]{:S(2)}) collective-permute-start(f32[10,16,256]{2,1,0:T(8,128)S(1)} %pad_maximum_fusion.3), channel_id=1, source_target_pairs={{1,2},{2,1},{3,4},{4,3},{5,6},{6,5},{9,10},{10,9},{11,12},{12,11},... | collective-permute-start | bytes 491528 | tf_op jit(solution)/shard_map/ppermute | solution.py:23
  44.3 52.8 %copy-start.1 = (f32[17,32,256]{2,1,0:T(8,128)S(1)}, f32[17,32,256]{2,1,0:T(8,128)}, u32[]{:S(2)}) copy-start(f32[17,32,256]{2,1,0:T(8,128)} %get-tuple-element.50.fx.refs_4_.refs_8_) | copy-start | bytes 1671172
  44.3 52.8 %copy-start.4 = (f32[16,32,256]{2,1,0:T(8,128)S(1)}, f32[16,32,256]{2,1,0:T(8,128)}, u32[]{:S(2)}) copy-start(f32[16,32,256]{2,1,0:T(8,128)} %copy-done.3) | copy-start | bytes 1572868
  92.5 8.9 %copy-start.12 = (f32[16,32,256]{2,1,0:T(8,128)}, f32[16,32,256]{2,1,0:T(8,128)S(1)}, u32[]{:S(2)}) copy-start(f32[16,32,256]{2,1,0:T(8,128)S(1)} %get-tuple-element.58.refs_2_.refs_18_) | copy-start | bytes 1572868
  92.5 8.9 %copy-start.13 = (f32[16,32,256]{2,1,0:T(8,128)}, f32[16,32,256]{2,1,0:T(8,128)S(1)}, u32[]{:S(2)}) copy-start(f32[16,32,256]{2,1,0:T(8,128)S(1)} %get-tuple-element.57.refs_1_.refs_15_) | copy-start | bytes 1572868
  92.5 8.9 %copy-start.16 = (f32[16,32,256]{2,1,0:T(8,128)}, f32[16,32,256]{2,1,0:T(8,128)S(1)}, u32[]{:S(2)}) copy-start(f32[16,32,256]{2,1,0:T(8,128)S(1)} %get-tuple-element.66.refs_17_) | copy-start | bytes 1572868
  92.5 4.6 %collective-permute-start.4 = (f32[32,256]{1,0:T(8,128)S(1)}, f32[32,256]{1,0:T(8,128)S(1)}, u32[]{:S(2)}, u32[]{:S(2)}) collective-permute-start(f32[32,256]{1,0:T(8,128)S(1)} %get-tuple-element.59), channel_id=1, source_target_pairs={{0,8},{8,0},{16,24},{24,16},{1,9},{9,1},{17,25},{25,17},{2,10},{10... | collective-permute-start | bytes 98312 | tf_op jit(solution)/shard_map/ppermute | solution.py:23
  92.7 4.5 %collective-permute-start.5 = (f32[32,256]{1,0:T(8,128)S(1)}, f32[32,256]{1,0:T(8,128)S(1)}, u32[]{:S(2)}, u32[]{:S(2)}) collective-permute-start(f32[32,256]{1,0:T(8,128)S(1)} %get-tuple-element.60), channel_id=1, source_target_pairs={{8,16},{16,8},{9,17},{17,9},{10,18},{18,10},{11,19},{19,11},{12,20... | collective-permute-start | bytes 98312 | tf_op jit(solution)/shard_map/ppermute | solution.py:23
  93.3 3.8 %collective-permute-start.6 = (f32[16,256]{1,0:T(8,128)S(1)}, f32[16,256]{1,0:T(8,128)S(1)}, u32[]{:S(2)}, u32[]{:S(2)}) collective-permute-start(f32[16,256]{1,0:T(8,128)S(1)} %get-tuple-element.61), channel_id=1, source_target_pairs={{0,1},{1,0},{2,3},{3,2},{4,5},{5,4},{6,7},{7,6},{8,9},{9,8},{10,11... | collective-permute-start | bytes 49160 | tf_op jit(solution)/shard_map/ppermute | solution.py:23
  94.1 3.1 %collective-permute-start.7 = (f32[16,256]{1,0:T(8,128)S(1)}, f32[16,256]{1,0:T(8,128)S(1)}, u32[]{:S(2)}, u32[]{:S(2)}) collective-permute-start(f32[16,256]{1,0:T(8,128)S(1)} %get-tuple-element.62), channel_id=1, source_target_pairs={{1,2},{2,1},{3,4},{4,3},{5,6},{6,5},{9,10},{10,9},{11,12},{12,11},... | collective-permute-start | bytes 49160 | tf_op jit(solution)/shard_map/ppermute | solution.py:23
  117.1 11.2 %copy-start.2 = (f32[17,32,256]{2,1,0:T(8,128)S(1)}, f32[17,32,256]{2,1,0:T(8,128)}, u32[]{:S(2)}) copy-start(f32[17,32,256]{2,1,0:T(8,128)} %get-tuple-element.50.fx.refs_4_.refs_8_) | copy-start | bytes 1671172
  117.1 11.2 %copy-start.5 = (f32[16,32,256]{2,1,0:T(8,128)S(1)}, f32[16,32,256]{2,1,0:T(8,128)}, u32[]{:S(2)}) copy-start(f32[16,32,256]{2,1,0:T(8,128)} %copy-done.3) | copy-start | bytes 1572868
  123.8 8.9 %copy-start.15 = (f32[16,32,256]{2,1,0:T(8,128)}, f32[16,32,256]{2,1,0:T(8,128)S(1)}, u32[]{:S(2)}) copy-start(f32[16,32,256]{2,1,0:T(8,128)S(1)} %get-tuple-element.76.refs_17_) | copy-start | bytes 1572868
  123.8 4.6 %collective-permute-start.8 = (f32[32,256]{1,0:T(8,128)S(1)}, f32[32,256]{1,0:T(8,128)S(1)}, u32[]{:S(2)}, u32[]{:S(2)}) collective-permute-start(f32[32,256]{1,0:T(8,128)S(1)} %get-tuple-element.69), channel_id=1, source_target_pairs={{0,8},{8,0},{16,24},{24,16},{1,9},{9,1},{17,25},{25,17},{2,10},{10... | collective-permute-start | bytes 98312 | tf_op jit(solution)/shard_map/ppermute | solution.py:23
  123.8 4.5 %collective-permute-start.9 = (f32[32,256]{1,0:T(8,128)S(1)}, f32[32,256]{1,0:T(8,128)S(1)}, u32[]{:S(2)}, u32[]{:S(2)}) collective-permute-start(f32[32,256]{1,0:T(8,128)S(1)} %get-tuple-element.70), channel_id=1, source_target_pairs={{8,16},{16,8},{9,17},{17,9},{10,18},{18,10},{11,19},{19,11},{12,20... | collective-permute-start | bytes 98312 | tf_op jit(solution)/shard_map/ppermute | solution.py:23
  124.5 3.8 %collective-permute-start.10 = (f32[16,256]{1,0:T(8,128)S(1)}, f32[16,256]{1,0:T(8,128)S(1)}, u32[]{:S(2)}, u32[]{:S(2)}) collective-permute-start(f32[16,256]{1,0:T(8,128)S(1)} %get-tuple-element.71), channel_id=1, source_target_pairs={{0,1},{1,0},{2,3},{3,2},{4,5},{5,4},{6,7},{7,6},{8,9},{9,8},{10,11... | collective-permute-start | bytes 49160 | tf_op jit(solution)/shard_map/ppermute | solution.py:23
  125.2 3.1 %collective-permute-start.11 = (f32[16,256]{1,0:T(8,128)S(1)}, f32[16,256]{1,0:T(8,128)S(1)}, u32[]{:S(2)}, u32[]{:S(2)}) collective-permute-start(f32[16,256]{1,0:T(8,128)S(1)} %get-tuple-element.72), channel_id=1, source_target_pairs={{1,2},{2,1},{3,4},{4,3},{5,6},{6,5},{9,10},{10,9},{11,12},{12,11},... | collective-permute-start | bytes 49160 | tf_op jit(solution)/shard_map/ppermute | solution.py:23
  128.3 20.1 %copy-start.7 = (f32[16,32,256]{2,1,0:T(8,128)S(1)}, f32[16,32,256]{2,1,0:T(8,128)}, u32[]{:S(2)}) copy-start(f32[16,32,256]{2,1,0:T(8,128)} %copy-done.6) | copy-start | bytes 1572868
  148.4 17.6 %copy-start = (f32[8,16,32,256]{3,2,1,0:T(8,128)S(1)}, f32[8,16,32,256]{3,2,1,0:T(8,128)}, u32[]{:S(2)}) copy-start(f32[8,16,32,256]{3,2,1,0:T(8,128)} %z.5) | copy-start | bytes 12582916
  (8 other events, 30.7 us)

commit v3 on v2

--- a/solution.py
+++ b/solution.py
@@ -167,47 +167,74 @@
         out[:, part, :] = jnp.broadcast_to(line[:, part * 128 : (part + 1) * 128], (out.shape[0], 128))
 
 
-def small_inverse(p):
-    size = p.shape[0]
-    lane, row = iota(p.shape, 1), iota(p.shape, 0)
-    head = iota((1, size), 1)
-    for k in range(0, size, 2):
-        r0, r1 = p[k : k + 1, :], p[k + 1 : k + 2, :]
-        c0, c1 = p[:, k : k + 1], p[:, k + 1 : k + 2]
-        a, b = p[k : k + 1, k : k + 1], p[k : k + 1, k + 1 : k + 2]
-        c, d = p[k + 1 : k + 2, k : k + 1], p[k + 1 : k + 2, k + 1 : k + 2]
-        over = 1.0 / (a * d - b * c)
-        r0 = jnp.where(head == k, 1.0, jnp.where(head == k + 1, 0.0, r0))
-        r1 = jnp.where(head == k, 0.0, jnp.where(head == k + 1, 1.0, r1))
-        n0 = (d * over) * r0 - (b * over) * r1
-        n1 = (a * over) * r1 - (c * over) * r0
-        p = jnp.where((lane == k) | (lane == k + 1), 0.0, p) - c0 * n0 - c1 * n1
-        p = jnp.where(row == k, n0, jnp.where(row == k + 1, n1, p))
-    return p
-
-
-def invert(e):
+def levels(across):
+    found, at, stride = [], 0, 1
+    while stride < across:
+        count = len(range(stride, across, 2 * stride))
+        found.append((at, count, stride))
+        at, stride = at + count, 2 * stride
+    return found + [(at, 1, 0)]
+
+
+def column_at(position, across):
+    value = jnp.zeros_like(position)
+    for at, count, stride in levels(across):
+        value = jnp.where((position >= at) & (position < at + count), (position - at) * 2 * stride + stride, value)
+    return value
+
+
+def position_of(column_id, across):
+    value = jnp.full_like(column_id, across - 1)
+    for at, count, stride in levels(across)[:-1]:
+        value = jnp.where(lax.rem(column_id, 2 * stride) == stride, at + lax.div(column_id, 2 * stride), value)
+    return value
+
+
+def device_of(index, num, down, across):
+    across_id = column_at(lax.div(index, num * down), across)
+    return lax.rem(lax.div(index, num), down) * across + across_id, across_id
+
+
+def small_inverses(blocks, group=4):
+    size = blocks[0].shape[0]
+    lane, row, head = iota((size, size), 1), iota((size, size), 0), iota((1, size), 1)
+    for start in range(0, size, group):
+        wide = [[jnp.broadcast_to(p[:, k : k + 1], (size, size)) for k in range(start, start + group)] for p in blocks]
+        for j in range(group):
+            k = start + j
+            for t, (p, cols) in enumerate(zip(blocks, wide)):
+                over = 1.0 / cols[j][k : k + 1, :]
+                line = jnp.where(head == k, 1.0, p[k : k + 1, :]) * over
+                p = jnp.where(lane == k, 0.0, p) - cols[j] * line
+                blocks[t] = jnp.where(row == k, line, p)
+                for other in range(j + 1, group):
+                    entry = cols[other][k : k + 1, :] * over
+                    cols[other] = jnp.where(row == k, entry, cols[other] - cols[j] * entry)
+    return blocks
+
+
+def invert(e, size, across):
     order = e.shape[0]
-    size = 32
-
-    def step(s, carry):
+    for at, count, _ in levels(across):
+        low, width = at * size, count * size
         a = e[...]
-        pivot = small_inverse(a[0:size, 0:size])
-        right = dot(pivot, a[0:size, :])
-        lane = iota((1, order), 1) < size
-        corner = jnp.concatenate([pivot, jnp.zeros((size, order - size), F32)], 1)
-        right = jnp.where(lane, corner, right)
-        rest = jnp.where(lane, 0.0, a[size:, :]) - dot(a[size:, 0:size], right)
-        e[0 : order - size, :] = pltpu.roll(rest, order - size, 1)
-        e[order - size :, :] = pltpu.roll(right, order - size, 1)
-        return carry
-
-    lax.fori_loop(0, order // size, step, 0)
-
-
-def column(g, num, order, offset, base):
+        parts = small_inverses([a[low + t * size : low + (t + 1) * size, low + t * size : low + (t + 1) * size] for t in range(count)])
+        zero = jnp.zeros((size, size), F32)
+        pivot = jnp.concatenate([jnp.concatenate([parts[t] if t == u else zero for u in range(count)], 1) for t in range(count)], 0) if count > 1 else parts[0]
+        lane = iota((width, order), 1)
+        inside = (lane >= low) & (lane < low + width)
+        unit = jnp.where(lane == iota((width, order), 0) + low, 1.0, 0.0)
+        right = dot(pivot, jnp.where(inside, unit, a[low : low + width, :]))
+        row, col = iota((order, order), 0), iota((order, order), 1)
+        rest = jnp.where((col >= low) & (col < low + width), 0.0, a) - dot(a[:, low : low + width], right)
+        e[...] = rest
+        e[low : low + width, :] = right
+
+
+def column(g, num, order, across, offset, base):
     n = g.shape[0]
-    pick = jnp.where(iota((order, n), 1) == lax.div(iota((order, n), 0), num) + offset, 1.0, 0.0)
+    device, _ = device_of(iota((order, n), 0), num, n // across, across)
+    pick = jnp.where(iota((order, n), 1) == device + offset, 1.0, 0.0)
     spread = dot(pick, g)
     lane, row = iota(spread.shape, 1), iota(spread.shape, 0)
     return jnp.sum(jnp.where(lane == base + lax.rem(row, num), spread, 0.0), axis=1, keepdims=True)
@@ -217,7 +244,9 @@
     order = e.shape[0]
     n = got.shape[0]
     square = num * num
-    pick = jnp.where(iota((order, n), 1) == lax.div(iota((order, n), 0), num), 1.0, 0.0)
+    down = n // across
+    device, _ = device_of(iota((order, n), 0), num, down, across)
+    pick = jnp.where(iota((order, n), 1) == device, 1.0, 0.0)
     lane, row = iota((order, 128), 1), iota((order, 128), 0)
     keep = lax.div(lax.rem(lane, square), num) == lax.rem(row, num)
     first = jnp.where(keep, dot(pick, got[:, 0, :]), 0.0)
@@ -226,7 +255,8 @@
     same = lax.rem(t, num) == lax.rem(c, num)
     low = jnp.where(same & (t < square), 1.0, 0.0)
     high = jnp.where(same & (t >= square), 1.0, 0.0)
-    bi, bj = lax.div(iota((order, order), 0), num), lax.div(iota((order, order), 1), num)
+    bi, _ = device_of(iota((order, 1), 0), num, down, across)
+    bj, _ = device_of(iota((1, order), 1), num, down, across)
     lower = jnp.where(bj == bi - across, dot(first, low), 0.0) + jnp.where(bj == bi - 1, dot(first, high), 0.0)
     e[...] = jnp.where(bi == bj, dot(second, low), 0.0) - lower - lower.T
 
@@ -235,11 +265,11 @@
     return jnp.sum(e[...] * col, axis=0, keepdims=True)
 
 
-def amounts(ids, solved, num, across):
+def amounts(ids, solved, num):
     order = solved.shape[1]
-    turned = pltpu.roll(jnp.broadcast_to(solved, (8, order)), ids[2], 1)
-    take = lambda at: [turned[0:1, (at + k) % order : (at + k) % order + 1] for k in range(num)]
-    return [take(at * num) for at in (0, -across, across, -1, 1)]
+    wide = jnp.broadcast_to(solved, (8, order))
+    groups = [pltpu.roll(wide, ids[2 + group], 1) for group in range(5)]
+    return [[turned[0:1, k : k + 1] for k in range(num)] for turned in groups]
 
 
 def combine(y, vectors):
@@ -277,9 +307,9 @@
     num, nx, ny, nz = z.shape
     order = e.shape[0]
     matrix_from(got, num, across, e)
-    invert(e)
-    solved = solve(e, column(got[:, 1, :], num, order, 0, num * num))
-    spread_out(amounts(ids, solved, num, across), z, zxl, zxh, zyl, zyh, gext, gy)
+    invert(e, got.shape[0] // across * num, across)
+    solved = solve(e, column(got[:, 1, :], num, order, across, 0, num * num))
+    spread_out(amounts(ids, solved, num), z, zxl, zxh, zyl, zyh, gext, gy)
     faces = (fx, fyl, fyu, fzl, fzu, diag)
     evx, evy = ids[0] == 1, ids[1] == 1
 
@@ -351,7 +381,7 @@
     g = got[:, 0, :]
     totals = jnp.sum(g, axis=0, keepdims=True)
     new, energy_p, cross = totals[:, 0:1], totals[:, 1:2], totals[:, 2:3]
-    col = column(g, num, order, 0, 3)
+    col = column(g, num, order, across, 0, 3)
     solved = solve(e, col)
     same = iota((order, order), 0) == iota((order, order), 1)
     line = jnp.sum(jnp.where(same, col, 0.0), axis=0, keepdims=True)
@@ -364,7 +394,7 @@
     state[0:1, :] = jnp.broadcast_to(new, (1, 128))
     state[1:2, :] = jnp.broadcast_to(energy, (1, 128))
     state[2:8, :] = jnp.zeros((6, 128), F32)
-    spread_out(amounts(ids, solved, num, across), z, zxl, zxh, zyl, zyh, gext, gy)
+    spread_out(amounts(ids, solved, num), z, zxl, zxh, zyl, zyh, gext, gy)
     evx, evy = ids[0] == 1, ids[1] == 1
 
     def plane(i, carry):
@@ -423,10 +453,10 @@
     order = e.shape[0]
     g = got[:, 0, :]
     beta = jnp.sum(g, axis=0, keepdims=True)[:, 0:1] / state_old[0:1, 0:1]
-    col = column(g, num, order, 0, 8)
+    col = column(g, num, order, across, 0, 8)
     for group, offset in ((1, across), (2, -across), (3, 1), (4, -1)):
-        col = col + column(g, num, order, offset, 8 + group * num)
-    ys = amounts(ids, solve(e, col), num, across)
+        col = col + column(g, num, order, across, offset, 8 + group * num)
+    ys = amounts(ids, solve(e, col), num)
     wide = [jnp.broadcast_to(c, (ny, nz)) for c in ys[0]]
     wide_beta = jnp.broadcast_to(beta, (ny, nz))
 
@@ -456,7 +486,11 @@
     order = n * num
     ix, iy = lax.axis_index("gx"), lax.axis_index("gy")
     evx, evy = ix % 2 == 0, iy % 2 == 0
-    ids = jnp.stack([evx.astype(jnp.int32), evy.astype(jnp.int32), (order - (ix * across + iy) * num) % order])
+    shifts = []
+    for dx, dy in ((0, 0), (-1, 0), (1, 0), (0, -1), (0, 1)):
+        place = position_of(jnp.clip(iy + dy, 0, across - 1), across) * down + jnp.clip(ix + dx, 0, down - 1)
+        shifts.append((order - place * num) % order)
+    ids = jnp.stack([evx.astype(jnp.int32), evy.astype(jnp.int32)] + shifts)
 
     def pack(at, index):
         return jnp.concatenate([at(coef, index)[None], at(start_field, index)[None], at(deflation, index)])

time: 169 us -> 135 us (0.80)
  Pallas kernels: 85.2 us -> 50.8 us
    pallas_call x7, Pallas kernels: 85.2 us -> 50.8 us  [call(): pl.pallas_call(kernel, name=name, in_specs=[SMEM] + [VMEM] * (len(args) -...]
where the time goes in v3:
time: 135 us; the launch traced here: 134 us
  blocking collectives  57.2 us (42%)
  Pallas kernels  50.8 us (38%)
  local copies, waits for them, and re-layouts  9.05 us (7%)
  starting transfers between devices  8.73 us (6%)
  waiting for transfers between devices  7.28 us (5%)
    all_to_all x4, blocking collectives, everywhere(): return lax.all_to_all(payload, BOTH, 0, 0)  57.2 us
    pallas_call x7, Pallas kernels, call(): pl.pallas_call(kernel, name=name, in_specs=[SMEM] + [VMEM] * (len(args) -...  50.8 us
    ppermute x12, starting transfers between devices, swap(): return lax.ppermute(value, axis, pairs)  8.73 us
    ppermute x12, waiting for transfers between devices, swap(): return lax.ppermute(value, axis, pairs)  7.28 us
    unnamed x46, local copies, waits for them, and re-layouts  4.07 us
    dynamic_slice x2, local copies, waits for them, and re-layouts, per_device(): lax.dynamic_index_in_dim(v, i, v.ndim - 2, keepdims=False)  2.93 us
  transfers between devices with their start and end apart: 12, of which 3 were waited for; matrix products, arithmetic and copies ran while one was open for 2% of the time, Pallas kernels for 0%

profile of v3, /device:TPU:0, one launch (start us, length us, event | category | flops | bytes accessed | tf_op | source)
XLA Modules:
  0.0 134.3 jit_solution(11404804491688769444)
XLA Ops:
  0.7 1.1 dynamic-slice_bitcast_fusion
  1.8 0.8 constant_dynamic-slice_fusion.6
  3.9 1.2 constant_dynamic-slice_fusion.1
  5.1 1.8 %constant_dynamic-slice_fusion = (f32[8,16,1,256]{3,2,1,0:T(1,128)S(1)}, f32[8,16,1,256]{3,2,1,0:T(1,128)S(1)}) fusion(f32[8,16,32,256]{3,2,1,0:T(8,128)} %z.5, s32[]{:T(128)S(6)} %select_n.112, s32[]{:T(128)S(6)} %select_n.111), kind=kLoop, calls=%fused_computation.12 | loop fusion | bytes 524296 | tf_op jit(solution)/shard_map/jit(dynamic_index_in_dim)/dynamic_slice | solution.py:499
  6.9 2.6 %collective-permute-start.2 = (f32[10,16,256]{2,1,0:T(8,128)S(1)}, f32[10,16,256]{2,1,0:T(8,128)S(1)}, u32[]{:S(2)}, u32[]{:S(2)}) collective-permute-start(f32[10,16,256]{2,1,0:T(8,128)S(1)} %pad_maximum_fusion.2), channel_id=1, source_target_pairs={{0,1},{1,0},{2,3},{3,2},{4,5},{5,4},{6,7},{7,6},{8,9},{9,8},{10,11... | collective-permute-start | bytes 491528 | tf_op jit(solution)/shard_map/ppermute | solution.py:23
  10.4 2.4 %collective-permute-done.2.ry0 = f32[10,16,256]{2,1,0:T(8,128)S(1)} collective-permute-done((f32[10,16,256]{2,1,0:T(8,128)S(1)}, f32[10,16,256]{2,1,0:T(8,128)S(1)}, u32[]{:S(2)}, u32[]{:S(2)}) %collective-permute-start.2) | collective-permute-done | bytes 163872 | tf_op jit(solution)/shard_map/ppermute | solution.py:23
  12.8 11.4 %prepare.1 = (f32[17,32,256]{2,1,0:T(8,128)}, f32[16,32,256]{2,1,0:T(8,128)S(1)}, f32[16,32,256]{2,1,0:T(8,128)S(1)}, f32[16,32,256]{2,1,0:T(8,128)S(1)}, f32[16...) custom-call(s32[7]{0:T(128)S(1)} %stack.39.ids.refs_0_, ...), custom_call_target="tpu_custom_call" | custom-call | tf_op jit(solution)/shard_map/prepare/pallas_call | solution.py:471
  24.2 0.8 copy-done.3
  25.0 0.8 copy-done.6
  25.8 18.6 %all_to_all.20.got = f32[32,2,128]{2,1,0:T(2,128)S(1)} all-to-all(f32[32,2,128]{2,1,0:T(2,128)S(1)} %get-tuple-element.44), channel_id=1, replica_groups=mesh['gx'=4,'gy'=8] {'gx','gy'}, dimensions={0} | all-to-all | bytes 65536 | tf_op jit(solution)/shard_map/all_to_all | solution.py:31
  44.3 13.7 %start.1 = (f32[256,256]{1,0:T(8,128)S(1)}, f32[16,32,256]{2,1,0:T(8,128)S(1)}, f32[16,32,256]{2,1,0:T(8,128)S(1)}, f32[16,32,256]{2,1,0:T(8,128)S(1)}, f32[32,2...) custom-call(s32[7]{0:T(128)S(1)} %stack.39.ids.refs_0_, ...), custom_call_target="tpu_custom_call" | custom-call | tf_op jit(solution)/shard_map/start/pallas_call | solution.py:471
  60.3 2.4 %collective-permute-done.6.refs_12_ = f32[16,256]{1,0:T(8,128)S(1)} collective-permute-done((f32[16,256]{1,0:T(8,128)S(1)}, f32[16,256]{1,0:T(8,128)S(1)}, u32[]{:S(2)}, u32[]{:S(2)}) %collective-permute-start.6) | collective-permute-done | bytes 16416 | tf_op jit(solution)/shard_map/ppermute | solution.py:23
  62.7 4.2 %product.2 = (f32[16,32,256]{2,1,0:T(8,128)S(1)}, f32[32,1,128]{2,1,0:T(1,128)S(1)}) custom-call(s32[7]{0:T(128)S(1)} %stack.39.ids.refs_0_, f32[16,32,256]{2,1,0:T(8,128)S(1)} %get-tuple-element.57.refs_1_.refs_15_, f32[16,32,256]{2,1,0:T(8,128)S(1)} %get-tuple-element.58.refs_2_.refs_18_, f32[8,16,32,256]{3,2,1,0:T(8,128)} %z.5, ...), custom_call_target="tpu_custom_call" | custom-call | tf_op jit(solution)/shard_map/product/pallas_call | solution.py:471
  67.0 0.8 copy-done.18
  67.8 14.9 %all_to_all.21.refs_1_ = f32[32,1,128]{2,1,0:T(1,128)S(1)} all-to-all(f32[32,1,128]{2,1,0:T(1,128)S(1)} %get-tuple-element.63), channel_id=1, replica_groups=mesh['gx'=4,'gy'=8] {'gx','gy'}, dimensions={0} | all-to-all | bytes 32768 | tf_op jit(solution)/shard_map/all_to_all | solution.py:31
  82.7 5.8 %update.2 = (f32[16,32,256]{2,1,0:T(8,128)S(1)}, f32[16,32,256]{2,1,0:T(8,128)S(1)}, f32[16,32,256]{2,1,0:T(8,128)S(1)}, f32[16,32,256]{2,1,0:T(8,128)S(1)}, f32...) custom-call(s32[7]{0:T(128)S(1)} %stack.39.ids.refs_0_, ...), custom_call_target="tpu_custom_call" | custom-call | tf_op jit(solution)/shard_map/update/pallas_call | solution.py:471
  88.5 0.8 copy-done.14
  91.4 2.5 %collective-permute-done.10.refs_12_ = f32[16,256]{1,0:T(8,128)S(1)} collective-permute-done((f32[16,256]{1,0:T(8,128)S(1)}, f32[16,256]{1,0:T(8,128)S(1)}, u32[]{:S(2)}, u32[]{:S(2)}) %collective-permute-start.10) | collective-permute-done | bytes 16416 | tf_op jit(solution)/shard_map/ppermute | solution.py:23
  93.9 4.3 %product.3 = (f32[16,32,256]{2,1,0:T(8,128)S(1)}, f32[32,1,128]{2,1,0:T(1,128)S(1)}) custom-call(s32[7]{0:T(128)S(1)} %stack.39.ids.refs_0_, f32[16,32,256]{2,1,0:T(8,128)S(1)} %get-tuple-element.67.refs_1_.refs_15_, f32[16,32,256]{2,1,0:T(8,128)S(1)} %get-tuple-element.68.refs_2_.refs_18_, f32[8,16,32,256]{3,2,1,0:T(8,128)} %z.5, ...), custom_call_target="tpu_custom_call" | custom-call | tf_op jit(solution)/shard_map/product/pallas_call | solution.py:471
  98.2 0.8 copy-done.17
  99.0 14.9 %all_to_all.22.refs_1_ = f32[32,1,128]{2,1,0:T(1,128)S(1)} all-to-all(f32[32,1,128]{2,1,0:T(1,128)S(1)} %get-tuple-element.74), channel_id=1, replica_groups=mesh['gx'=4,'gy'=8] {'gx','gy'}, dimensions={0} | all-to-all | bytes 32768 | tf_op jit(solution)/shard_map/all_to_all | solution.py:31
  114.0 8.8 %update.3 = (f32[16,32,256]{2,1,0:T(8,128)S(1)}, f32[16,32,256]{2,1,0:T(8,128)}, f32[16,32,256]{2,1,0:T(8,128)}, f32[16,32,256]{2,1,0:T(8,128)}, f32[16,32,256]{...) custom-call(s32[7]{0:T(128)S(1)} %stack.39.ids.refs_0_, f32[32,1,128]{2,1,0:T(1,128)S(1)} %all_to_all.22.refs_1_, ...), custom_call_target="tpu_custom_call" | custom-call | tf_op jit(solution)/shard_map/update/pallas_call | solution.py:471
  122.8 8.8 %all_to_all.23.got = f32[32,1,128]{2,1,0:T(1,128)S(1)} all-to-all(f32[32,1,128]{2,1,0:T(1,128)S(1)} %get-tuple-element.81), channel_id=1, replica_groups=mesh['gx'=4,'gy'=8] {'gx','gy'}, dimensions={0} | all-to-all | bytes 32768 | tf_op jit(solution)/shard_map/all_to_all | solution.py:31
  131.6 2.7 %finish.1 = f32[16,32,256]{2,1,0:T(8,128)} custom-call(s32[7]{0:T(128)S(1)} %stack.39.ids.refs_0_, f32[32,1,128]{2,1,0:T(1,128)S(1)} %all_to_all.23.got, f32[256,256]{1,0:T(8,128)S(1)} %get-tuple-element.64.refs_2_.e, f32[8,16,32,256]{3,2,1,0:T(8,128)S(1)} %copy-done, f32[16,32,256]{2,1,0:T(8,128)S(1)} %get-tuple-element.82.p, ...), custom_call_target="tpu_custom_call" | custom-call | tf_op jit(solution)/shard_map/finish/pallas_call | solution.py:471
  (66 shorter events, 6.4 us)
Async XLA Ops:
  0.6 12.2 %copy-start.19 = (f32[16,32,256]{2,1,0:T(8,128)S(1)}, f32[16,32,256]{2,1,0:T(8,128)}, u32[]{:S(2)}) copy-start(f32[16,32,256]{2,1,0:T(8,128)} %b.1) | copy-start | bytes 1572868
  2.6 10.1 %collective-permute-start = (f32[10,32,256]{2,1,0:T(8,128)S(1)}, f32[10,32,256]{2,1,0:T(8,128)S(1)}, u32[]{:S(2)}, u32[]{:S(2)}) collective-permute-start(f32[10,32,256]{2,1,0:T(8,128)S(1)} %pad_maximum_fusion), channel_id=1, source_target_pairs={{0,8},{8,0},{16,24},{24,16},{1,9},{9,1},{17,25},{25,17},{2,10},{10... | collective-permute-start | bytes 983048 | tf_op jit(solution)/shard_map/ppermute | solution.py:23
  3.2 9.6 %collective-permute-start.1 = (f32[10,32,256]{2,1,0:T(8,128)S(1)}, f32[10,32,256]{2,1,0:T(8,128)S(1)}, u32[]{:S(2)}, u32[]{:S(2)}) collective-permute-start(f32[10,32,256]{2,1,0:T(8,128)S(1)} %pad_maximum_fusion.1), channel_id=1, source_target_pairs={{8,16},{16,8},{9,17},{17,9},{10,18},{18,10},{11,19},{19,11},{12,20... | collective-permute-start | bytes 983048 | tf_op jit(solution)/shard_map/ppermute | solution.py:23
  6.9 37.5 %copy-start.8 = (f32[16,32,256]{2,1,0:T(8,128)S(1)}, f32[16,32,256]{2,1,0:T(8,128)}, u32[]{:S(2)}) copy-start(f32[16,32,256]{2,1,0:T(8,128)} %x0.3) | copy-start | bytes 1572868
  6.9 5.9 %collective-permute-start.2 = (f32[10,16,256]{2,1,0:T(8,128)S(1)}, f32[10,16,256]{2,1,0:T(8,128)S(1)}, u32[]{:S(2)}, u32[]{:S(2)}) collective-permute-start(f32[10,16,256]{2,1,0:T(8,128)S(1)} %pad_maximum_fusion.2), channel_id=1, source_target_pairs={{0,1},{1,0},{2,3},{3,2},{4,5},{5,4},{6,7},{7,6},{8,9},{9,8},{10,11... | collective-permute-start | bytes 491528 | tf_op jit(solution)/shard_map/ppermute | solution.py:23
  9.5 3.3 %collective-permute-start.3 = (f32[10,16,256]{2,1,0:T(8,128)S(1)}, f32[10,16,256]{2,1,0:T(8,128)S(1)}, u32[]{:S(2)}, u32[]{:S(2)}) collective-permute-start(f32[10,16,256]{2,1,0:T(8,128)S(1)} %pad_maximum_fusion.3), channel_id=1, source_target_pairs={{1,2},{2,1},{3,4},{4,3},{5,6},{6,5},{9,10},{10,9},{11,12},{12,11},... | collective-permute-start | bytes 491528 | tf_op jit(solution)/shard_map/ppermute | solution.py:23
  44.3 18.4 %copy-start.1 = (f32[17,32,256]{2,1,0:T(8,128)S(1)}, f32[17,32,256]{2,1,0:T(8,128)}, u32[]{:S(2)}) copy-start(f32[17,32,256]{2,1,0:T(8,128)} %get-tuple-element.50.fx.refs_4_.refs_8_) | copy-start | bytes 1671172
  44.3 18.4 %copy-start.4 = (f32[16,32,256]{2,1,0:T(8,128)S(1)}, f32[16,32,256]{2,1,0:T(8,128)}, u32[]{:S(2)}) copy-start(f32[16,32,256]{2,1,0:T(8,128)} %copy-done.3) | copy-start | bytes 1572868
  58.0 8.9 %copy-start.12 = (f32[16,32,256]{2,1,0:T(8,128)}, f32[16,32,256]{2,1,0:T(8,128)S(1)}, u32[]{:S(2)}) copy-start(f32[16,32,256]{2,1,0:T(8,128)S(1)} %get-tuple-element.58.refs_2_.refs_18_) | copy-start | bytes 1572868
  58.0 8.9 %copy-start.13 = (f32[16,32,256]{2,1,0:T(8,128)}, f32[16,32,256]{2,1,0:T(8,128)S(1)}, u32[]{:S(2)}) copy-start(f32[16,32,256]{2,1,0:T(8,128)S(1)} %get-tuple-element.57.refs_1_.refs_15_) | copy-start | bytes 1572868
  58.0 8.9 %copy-start.16 = (f32[16,32,256]{2,1,0:T(8,128)}, f32[16,32,256]{2,1,0:T(8,128)S(1)}, u32[]{:S(2)}) copy-start(f32[16,32,256]{2,1,0:T(8,128)S(1)} %get-tuple-element.66.refs_17_) | copy-start | bytes 1572868
  58.0 4.7 %collective-permute-start.4 = (f32[32,256]{1,0:T(8,128)S(1)}, f32[32,256]{1,0:T(8,128)S(1)}, u32[]{:S(2)}, u32[]{:S(2)}) collective-permute-start(f32[32,256]{1,0:T(8,128)S(1)} %get-tuple-element.59), channel_id=1, source_target_pairs={{0,8},{8,0},{16,24},{24,16},{1,9},{9,1},{17,25},{25,17},{2,10},{10... | collective-permute-start | bytes 98312 | tf_op jit(solution)/shard_map/ppermute | solution.py:23
  58.2 4.5 %collective-permute-start.5 = (f32[32,256]{1,0:T(8,128)S(1)}, f32[32,256]{1,0:T(8,128)S(1)}, u32[]{:S(2)}, u32[]{:S(2)}) collective-permute-start(f32[32,256]{1,0:T(8,128)S(1)} %get-tuple-element.60), channel_id=1, source_target_pairs={{8,16},{16,8},{9,17},{17,9},{10,18},{18,10},{11,19},{19,11},{12,20... | collective-permute-start | bytes 98312 | tf_op jit(solution)/shard_map/ppermute | solution.py:23
  58.9 3.8 %collective-permute-start.6 = (f32[16,256]{1,0:T(8,128)S(1)}, f32[16,256]{1,0:T(8,128)S(1)}, u32[]{:S(2)}, u32[]{:S(2)}) collective-permute-start(f32[16,256]{1,0:T(8,128)S(1)} %get-tuple-element.61), channel_id=1, source_target_pairs={{0,1},{1,0},{2,3},{3,2},{4,5},{5,4},{6,7},{7,6},{8,9},{9,8},{10,11... | collective-permute-start | bytes 49160 | tf_op jit(solution)/shard_map/ppermute | solution.py:23
  59.6 3.1 %collective-permute-start.7 = (f32[16,256]{1,0:T(8,128)S(1)}, f32[16,256]{1,0:T(8,128)S(1)}, u32[]{:S(2)}, u32[]{:S(2)}) collective-permute-start(f32[16,256]{1,0:T(8,128)S(1)} %get-tuple-element.62), channel_id=1, source_target_pairs={{1,2},{2,1},{3,4},{4,3},{5,6},{6,5},{9,10},{10,9},{11,12},{12,11},... | collective-permute-start | bytes 49160 | tf_op jit(solution)/shard_map/ppermute | solution.py:23
  82.7 11.2 %copy-start.2 = (f32[17,32,256]{2,1,0:T(8,128)S(1)}, f32[17,32,256]{2,1,0:T(8,128)}, u32[]{:S(2)}) copy-start(f32[17,32,256]{2,1,0:T(8,128)} %get-tuple-element.50.fx.refs_4_.refs_8_) | copy-start | bytes 1671172
  82.7 11.2 %copy-start.5 = (f32[16,32,256]{2,1,0:T(8,128)S(1)}, f32[16,32,256]{2,1,0:T(8,128)}, u32[]{:S(2)}) copy-start(f32[16,32,256]{2,1,0:T(8,128)} %copy-done.3) | copy-start | bytes 1572868
  89.3 8.9 %copy-start.15 = (f32[16,32,256]{2,1,0:T(8,128)}, f32[16,32,256]{2,1,0:T(8,128)S(1)}, u32[]{:S(2)}) copy-start(f32[16,32,256]{2,1,0:T(8,128)S(1)} %get-tuple-element.76.refs_17_) | copy-start | bytes 1572868
  89.3 4.6 %collective-permute-start.8 = (f32[32,256]{1,0:T(8,128)S(1)}, f32[32,256]{1,0:T(8,128)S(1)}, u32[]{:S(2)}, u32[]{:S(2)}) collective-permute-start(f32[32,256]{1,0:T(8,128)S(1)} %get-tuple-element.69), channel_id=1, source_target_pairs={{0,8},{8,0},{16,24},{24,16},{1,9},{9,1},{17,25},{25,17},{2,10},{10... | collective-permute-start | bytes 98312 | tf_op jit(solution)/shard_map/ppermute | solution.py:23
  89.4 4.5 %collective-permute-start.9 = (f32[32,256]{1,0:T(8,128)S(1)}, f32[32,256]{1,0:T(8,128)S(1)}, u32[]{:S(2)}, u32[]{:S(2)}) collective-permute-start(f32[32,256]{1,0:T(8,128)S(1)} %get-tuple-element.70), channel_id=1, source_target_pairs={{8,16},{16,8},{9,17},{17,9},{10,18},{18,10},{11,19},{19,11},{12,20... | collective-permute-start | bytes 98312 | tf_op jit(solution)/shard_map/ppermute | solution.py:23
  90.1 3.8 %collective-permute-start.10 = (f32[16,256]{1,0:T(8,128)S(1)}, f32[16,256]{1,0:T(8,128)S(1)}, u32[]{:S(2)}, u32[]{:S(2)}) collective-permute-start(f32[16,256]{1,0:T(8,128)S(1)} %get-tuple-element.71), channel_id=1, source_target_pairs={{0,1},{1,0},{2,3},{3,2},{4,5},{5,4},{6,7},{7,6},{8,9},{9,8},{10,11... | collective-permute-start | bytes 49160 | tf_op jit(solution)/shard_map/ppermute | solution.py:23
  90.8 3.1 %collective-permute-start.11 = (f32[16,256]{1,0:T(8,128)S(1)}, f32[16,256]{1,0:T(8,128)S(1)}, u32[]{:S(2)}, u32[]{:S(2)}) collective-permute-start(f32[16,256]{1,0:T(8,128)S(1)} %get-tuple-element.72), channel_id=1, source_target_pairs={{1,2},{2,1},{3,4},{4,3},{5,6},{6,5},{9,10},{10,9},{11,12},{12,11},... | collective-permute-start | bytes 49160 | tf_op jit(solution)/shard_map/ppermute | solution.py:23
  93.9 20.1 %copy-start.7 = (f32[16,32,256]{2,1,0:T(8,128)S(1)}, f32[16,32,256]{2,1,0:T(8,128)}, u32[]{:S(2)}) copy-start(f32[16,32,256]{2,1,0:T(8,128)} %copy-done.6) | copy-start | bytes 1572868
  114.0 17.6 %copy-start = (f32[8,16,32,256]{3,2,1,0:T(8,128)S(1)}, f32[8,16,32,256]{3,2,1,0:T(8,128)}, u32[]{:S(2)}) copy-start(f32[8,16,32,256]{3,2,1,0:T(8,128)} %z.5) | copy-start | bytes 12582916
  (8 other events, 30.7 us)

commit v4 on v3

--- a/solution.py
+++ b/solution.py
@@ -104,7 +104,7 @@
         xext[i + 1] = x0[i]
         return carry
 
-    lax.fori_loop(0, nx, fill, 0)
+    lax.fori_loop(0, nx, fill, 0, unroll=4)
 
     def faces_x(i, carry):
         fx[i] = face(cext[i], cext[i + 1])
@@ -126,7 +126,7 @@
         dinv[i] = 1.0 / d
         return carry
 
-    lax.fori_loop(0, nx, faces_yz, 0)
+    lax.fori_loop(0, nx, faces_yz, 0, unroll=4)
     faces = (fx, fyl, fyu, fzl, fzu, diag)
     square = num * num
 
@@ -148,7 +148,7 @@
             zy0[k, pl.ds(i, 1), :] = v[0:1, :] * fyl[i, 0:1, :]
         return carry
 
-    lax.fori_loop(0, nx, plane, 0)
+    lax.fori_loop(0, nx, plane, 0, unroll=4)
     for k in range(num):
         for m in range(k):
             acc[pl.ds((2 * square + k * num + m) * 8, 8), :] = acc[pl.ds((2 * square + m * num + k) * 8, 8), :]
@@ -288,7 +288,7 @@
         gext[i + 1] = combine(wide, [z[k, i] for k in range(num)])
         return carry
 
-    lax.fori_loop(0, nx, plane, 0)
+    lax.fori_loop(0, nx, plane, 0, unroll=4)
 
 
 def send_rows(i, p, evy, sy0, sy1):
@@ -324,7 +324,7 @@
         send_rows(i, pre, evy, sy0, sy1)
         return carry
 
-    lax.fori_loop(0, nx, plane, 0)
+    lax.fori_loop(0, nx, plane, 0, unroll=4)
     send_planes(p, evx, sx0, sx1)
 
 
@@ -345,7 +345,7 @@
         pext[i + 1] = p[i]
         return carry
 
-    lax.fori_loop(0, nx, fill, 0)
+    lax.fori_loop(0, nx, fill, 0, unroll=4)
 
     def plane(i, carry):
         v = pext[i + 1]
@@ -359,7 +359,7 @@
             add_to(acc, 3 + k, w * z[k, i])
         return carry
 
-    lax.fori_loop(0, nx, plane, 0)
+    lax.fori_loop(0, nx, plane, 0, unroll=4)
     out[:, 0, :] = jnp.broadcast_to(row_of(acc, acc.shape[0] // 8, 128), (out.shape[0], 128))
 
 
@@ -420,7 +420,7 @@
 
     if last:
         acc[...] = jnp.zeros_like(acc)
-    lax.fori_loop(0, nx, plane, 0)
+    lax.fori_loop(0, nx, plane, 0, unroll=4)
     if not last:
         send_planes(p_new, evx, sx0, sx1)
         return
@@ -438,7 +438,7 @@
             add_to(acc, 8 + k, w * z[k, i])
         return carry
 
-    lax.fori_loop(0, nx, second, 0)
+    lax.fori_loop(0, nx, second, 0, unroll=4)
     low, high = p_new[0] * fx[0], p_new[nx - 1] * fx[nx]
     for k in range(num):
         add_to(acc, 8 + num + k, -low * zxl[k])
@@ -464,10 +464,10 @@
         d[i] = p[i] + wide_beta * d_old[i] - combine(wide, [z[k, i] for k in range(num)])
         return carry
 
-    lax.fori_loop(0, nx, plane, 0)
-
-
-def call(kernel, name, args, outs, scratch):
+    lax.fori_loop(0, nx, plane, 0, unroll=4)
+
+
+def call(order, kernel, name, args, outs, scratch):
     return pl.pallas_call(
         kernel,
         name=name,
@@ -475,7 +475,7 @@
         out_specs=[VMEM] * len(outs),
         out_shape=[jax.ShapeDtypeStruct(s, F32) for s in outs],
         scratch_shapes=[pltpu.VMEM(s, F32) for s in scratch],
-        compiler_params=pltpu.CompilerParams(vmem_limit_bytes=48 * 1024 * 1024),
+        compiler_params=pltpu.CompilerParams(vmem_limit_bytes=(16 << 20) + 32 * order * order),
     )(*args)
 
 
@@ -506,6 +506,7 @@
     layers = [layer_x, layer_x, layer_y, layer_y]
     wide = -(-(3 * num * num + num) // 128)
     *faces, dinv, r0, zxl, zxh, zyl, zyh, out = call(
+        order,
         prepare_kernel,
         "prepare",
         [ids, right_side, start_field, coef, deflation, *raw],
@@ -514,6 +515,7 @@
     )
     basis = [deflation, zxl, zxh, zyl, zyh]
     e, x, r, p, *sent = call(
+        order,
         functools.partial(start_kernel, across),
         "start",
         [ids, everywhere(out), start_field, r0, *basis, *faces, dinv],
@@ -524,6 +526,7 @@
     for iteration in range(ITERS):
         first, last = iteration == 0, iteration == ITERS - 1
         ap, out = call(
+            order,
             functools.partial(product_kernel, first),
             "product",
             [ids, p, r, deflation, *faces, *swaps(sent)] + old[1:2],
@@ -531,6 +534,7 @@
             [ext, two_y, (16 * 8, 128)],
         )
         d, ad, x, r, p, state, *sent = call(
+            order,
             functools.partial(update_kernel, first, last, across),
             "update",
             [ids, everywhere(out), e, *basis, *faces, dinv, p, ap, x, r] + old,
@@ -539,6 +543,7 @@
         )
         old = [d, ad, state]
     (direction,) = call(
+        order,
         functools.partial(finish_kernel, across),
         "finish",
         [ids, everywhere(sent[0]), e, deflation, p, d, state],

time: 135 us -> 113 us (0.84)
  Pallas kernels: 50.8 us -> 31.2 us
  local copies, waits for them, and re-layouts: 9.05 us -> 7.26 us
    pallas_call x7, Pallas kernels: 50.8 us -> 31.2 us  [call(): pl.pallas_call(kernel, name=name, in_specs=[SMEM] + [VMEM] * (len(args) -...]
    unnamed x46 -> x14, local copies, waits for them, and re-layouts: 4.07 us -> 2.23 us
  transfers between devices with their start and end apart: 12 -> 12, of which waited for: 3 -> 3; matrix products, arithmetic and copies ran while one was open for 2% -> 3% of each run, Pallas kernels for 0% -> 0%
where the time goes in v4:
time: 113 us
  blocking collectives  57.3 us (51%)
  Pallas kernels  31.2 us (28%)
  starting transfers between devices  8.73 us (8%)
  waiting for transfers between devices  7.28 us (6%)
  local copies, waits for them, and re-layouts  7.26 us (6%)
    all_to_all x4, blocking collectives, everywhere(): return lax.all_to_all(payload, BOTH, 0, 0)  57.3 us
    pallas_call x7, Pallas kernels, call(): pl.pallas_call(kernel, name=name, in_specs=[SMEM] + [VMEM] * (len(args) -...  31.2 us
    ppermute x12, starting transfers between devices, swap(): return lax.ppermute(value, axis, pairs)  8.73 us
    ppermute x12, waiting for transfers between devices, swap(): return lax.ppermute(value, axis, pairs)  7.28 us
    dynamic_slice x2, local copies, waits for them, and re-layouts, per_device(): lax.dynamic_index_in_dim(v, i, v.ndim - 2, keepdims=False)  2.93 us
  transfers between devices with their start and end apart: 12, of which 3 were waited for; matrix products, arithmetic and copies ran while one was open for 3% of the time, Pallas kernels for 0%

profile of v4, /device:TPU:0, one launch (start us, length us, event | category | flops | bytes accessed | tf_op | source)
XLA Modules:
  0.0 112.8 jit_solution(5976023111451704729)
XLA Ops:
  0.7 1.2 %dynamic-slice_bitcast_fusion = (f32[8,32,256]{2,1,0:T(8,128)S(1)}, f32[8,32,256]{2,1,0:T(8,128)S(1)}) fusion(f32[8,16,32,256]{3,2,1,0:T(8,128)} %z.5, s32[]{:T(128)S(6)} %select_n.110, s32[]{:T(128)S(6)} %select_n.109), kind=kLoop, calls=%fused_computation.2 | loop fusion | bytes 1048584 | tf_op jit(solution)/shard_map/jit(dynamic_index_in_dim)/squeeze | solution.py:498
  1.9 0.8 constant_dynamic-slice_fusion.6
  3.3 0.7 collective-permute-start.1
  4.0 1.2 %constant_dynamic-slice_fusion.1 = (f32[16,1,256]{2,1,0:T(1,128)S(1)}, f32[16,1,256]{2,1,0:T(1,128)S(1)}, f32[16,1,256]{2,1,0:T(1,128)S(1)}, f32[16,1,256]{2,1,0:T(1,128)S(1)}) fusion(f32[16,32,256]{2,1,0:T(8,128)} %x0.3, s32[]{:T(128)S(6)} %select_n.112, s32[]{:T(128)S(6)} %select_n.111, f32[16,32,256]{2,1,0:T(8,128)} %coef.1), kind=kLoop, calls=%fused_computation.13 | loop fusion | bytes 131080 | tf_op jit(solution)/shard_map/jit(dynamic_index_in_dim)/dynamic_slice | solution.py:499
  5.1 1.8 %constant_dynamic-slice_fusion = (f32[8,16,1,256]{3,2,1,0:T(1,128)S(1)}, f32[8,16,1,256]{3,2,1,0:T(1,128)S(1)}) fusion(f32[8,16,32,256]{3,2,1,0:T(8,128)} %z.5, s32[]{:T(128)S(6)} %select_n.112, s32[]{:T(128)S(6)} %select_n.111), kind=kLoop, calls=%fused_computation.12 | loop fusion | bytes 524296 | tf_op jit(solution)/shard_map/jit(dynamic_index_in_dim)/dynamic_slice | solution.py:499
  7.0 2.6 %collective-permute-start.2 = (f32[10,16,256]{2,1,0:T(8,128)S(1)}, f32[10,16,256]{2,1,0:T(8,128)S(1)}, u32[]{:S(2)}, u32[]{:S(2)}) collective-permute-start(f32[10,16,256]{2,1,0:T(8,128)S(1)} %pad_maximum_fusion.2), channel_id=1, source_target_pairs={{0,1},{1,0},{2,3},{3,2},{4,5},{5,4},{6,7},{7,6},{8,9},{9,8},{10,11... | collective-permute-start | bytes 491528 | tf_op jit(solution)/shard_map/ppermute | solution.py:23
  9.6 0.7 collective-permute-start.3
  10.5 2.4 %collective-permute-done.2.ry0 = f32[10,16,256]{2,1,0:T(8,128)S(1)} collective-permute-done((f32[10,16,256]{2,1,0:T(8,128)S(1)}, f32[10,16,256]{2,1,0:T(8,128)S(1)}, u32[]{:S(2)}, u32[]{:S(2)}) %collective-permute-start.2) | collective-permute-done | bytes 163872 | tf_op jit(solution)/shard_map/ppermute | solution.py:23
  12.9 2.2 %copy-done = f32[8,16,32,256]{3,2,1,0:T(8,128)S(1)} copy-done((f32[8,16,32,256]{3,2,1,0:T(8,128)S(1)}, f32[8,16,32,256]{3,2,1,0:T(8,128)}, u32[]{:S(2)}) %copy-start) | copy-done | bytes 4194328
  15.1 8.3 %prepare.1 = (f32[17,32,256]{2,1,0:T(8,128)S(1)}, f32[16,32,256]{2,1,0:T(8,128)S(1)}, f32[16,32,256]{2,1,0:T(8,128)S(1)}, f32[16,32,256]{2,1,0:T(8,128)S(1)}, f3...) custom-call(s32[7]{0:T(128)S(1)} %stack.39.ids.refs_0_, ...), custom_call_target="tpu_custom_call" | custom-call | tf_op jit(solution)/shard_map/prepare/pallas_call | solution.py:471
  23.4 18.6 %all_to_all.20.got = f32[32,2,128]{2,1,0:T(2,128)S(1)} all-to-all(f32[32,2,128]{2,1,0:T(2,128)S(1)} %get-tuple-element.44), channel_id=1, replica_groups=mesh['gx'=4,'gy'=8] {'gx','gy'}, dimensions={0} | all-to-all | bytes 65536 | tf_op jit(solution)/shard_map/all_to_all | solution.py:31
  42.0 10.5 %start.1 = (f32[256,256]{1,0:T(8,128)S(1)}, f32[16,32,256]{2,1,0:T(8,128)S(1)}, f32[16,32,256]{2,1,0:T(8,128)S(1)}, f32[16,32,256]{2,1,0:T(8,128)S(1)}, f32[32,2...) custom-call(s32[7]{0:T(128)S(1)} %stack.39.ids.refs_0_, ...), custom_call_target="tpu_custom_call" | custom-call | tf_op jit(solution)/shard_map/start/pallas_call | solution.py:471
  53.4 0.7 collective-permute-start.6
  54.8 2.4 %collective-permute-done.6.refs_12_ = f32[16,256]{1,0:T(8,128)S(1)} collective-permute-done((f32[16,256]{1,0:T(8,128)S(1)}, f32[16,256]{1,0:T(8,128)S(1)}, u32[]{:S(2)}, u32[]{:S(2)}) %collective-permute-start.6) | collective-permute-done | bytes 16416 | tf_op jit(solution)/shard_map/ppermute | solution.py:23
  57.2 1.7 %product.2 = (f32[16,32,256]{2,1,0:T(8,128)S(1)}, f32[32,1,128]{2,1,0:T(1,128)S(1)}) custom-call(s32[7]{0:T(128)S(1)} %stack.39.ids.refs_0_, f32[16,32,256]{2,1,0:T(8,128)S(1)} %get-tuple-element.57.refs_1_.refs_15_, f32[16,32,256]{2,1,0:T(8,128)S(1)} %get-tuple-element.58.refs_2_.refs_18_, f32[8,16,32,256]{3,2,1,0:T(8,128)S(1)} %copy-done, ...), custom_call_target="tpu_custom_call" | custom-call | tf_op jit(solution)/shard_map/product/pallas_call | solution.py:471
  58.9 14.9 %all_to_all.21.refs_1_ = f32[32,1,128]{2,1,0:T(1,128)S(1)} all-to-all(f32[32,1,128]{2,1,0:T(1,128)S(1)} %get-tuple-element.63), channel_id=1, replica_groups=mesh['gx'=4,'gy'=8] {'gx','gy'}, dimensions={0} | all-to-all | bytes 32768 | tf_op jit(solution)/shard_map/all_to_all | solution.py:31
  73.8 2.1 %update.2 = (f32[16,32,256]{2,1,0:T(8,128)S(1)}, f32[16,32,256]{2,1,0:T(8,128)S(1)}, f32[16,32,256]{2,1,0:T(8,128)S(1)}, f32[16,32,256]{2,1,0:T(8,128)S(1)}, f32...) custom-call(s32[7]{0:T(128)S(1)} %stack.39.ids.refs_0_, ...), custom_call_target="tpu_custom_call" | custom-call | tf_op jit(solution)/shard_map/update/pallas_call | solution.py:471
  76.7 0.7 collective-permute-start.10
  78.0 2.5 %collective-permute-done.10.refs_12_ = f32[16,256]{1,0:T(8,128)S(1)} collective-permute-done((f32[16,256]{1,0:T(8,128)S(1)}, f32[16,256]{1,0:T(8,128)S(1)}, u32[]{:S(2)}, u32[]{:S(2)}) %collective-permute-start.10) | collective-permute-done | bytes 16416 | tf_op jit(solution)/shard_map/ppermute | solution.py:23
  80.5 1.7 %product.3 = (f32[16,32,256]{2,1,0:T(8,128)S(1)}, f32[32,1,128]{2,1,0:T(1,128)S(1)}) custom-call(s32[7]{0:T(128)S(1)} %stack.39.ids.refs_0_, f32[16,32,256]{2,1,0:T(8,128)S(1)} %get-tuple-element.67.refs_1_.refs_15_, f32[16,32,256]{2,1,0:T(8,128)S(1)} %get-tuple-element.68.refs_2_.refs_18_, f32[8,16,32,256]{3,2,1,0:T(8,128)S(1)} %copy-done, ...), custom_call_target="tpu_custom_call" | custom-call | tf_op jit(solution)/shard_map/product/pallas_call | solution.py:471
  82.2 15.0 %all_to_all.22.refs_1_ = f32[32,1,128]{2,1,0:T(1,128)S(1)} all-to-all(f32[32,1,128]{2,1,0:T(1,128)S(1)} %get-tuple-element.74), channel_id=1, replica_groups=mesh['gx'=4,'gy'=8] {'gx','gy'}, dimensions={0} | all-to-all | bytes 32768 | tf_op jit(solution)/shard_map/all_to_all | solution.py:31
  97.1 4.3 %update.3 = (f32[16,32,256]{2,1,0:T(8,128)S(1)}, f32[16,32,256]{2,1,0:T(8,128)}, f32[16,32,256]{2,1,0:T(8,128)}, f32[16,32,256]{2,1,0:T(8,128)}, f32[16,32,256]{...) custom-call(s32[7]{0:T(128)S(1)} %stack.39.ids.refs_0_, f32[32,1,128]{2,1,0:T(1,128)S(1)} %all_to_all.22.refs_1_, ...), custom_call_target="tpu_custom_call" | custom-call | tf_op jit(solution)/shard_map/update/pallas_call | solution.py:471
  101.4 8.8 %all_to_all.23.got = f32[32,1,128]{2,1,0:T(1,128)S(1)} all-to-all(f32[32,1,128]{2,1,0:T(1,128)S(1)} %get-tuple-element.81), channel_id=1, replica_groups=mesh['gx'=4,'gy'=8] {'gx','gy'}, dimensions={0} | all-to-all | bytes 32768 | tf_op jit(solution)/shard_map/all_to_all | solution.py:31
  110.2 2.6 %finish.1 = f32[16,32,256]{2,1,0:T(8,128)} custom-call(s32[7]{0:T(128)S(1)} %stack.39.ids.refs_0_, f32[32,1,128]{2,1,0:T(1,128)S(1)} %all_to_all.23.got, f32[256,256]{1,0:T(8,128)S(1)} %get-tuple-element.64.refs_2_.e, f32[8,16,32,256]{3,2,1,0:T(8,128)S(1)} %copy-done, f32[16,32,256]{2,1,0:T(8,128)S(1)} %get-tuple-element.82.p, ...), custom_call_target="tpu_custom_call" | custom-call | tf_op jit(solution)/shard_map/finish/pallas_call | solution.py:471
  (34 shorter events, 3.6 us)
Async XLA Ops:
  0.6 12.2 %copy-start.1 = (f32[16,32,256]{2,1,0:T(8,128)S(1)}, f32[16,32,256]{2,1,0:T(8,128)}, u32[]{:S(2)}) copy-start(f32[16,32,256]{2,1,0:T(8,128)} %x0.3) | copy-start | bytes 1572868
  0.6 12.2 %copy-start.2 = (f32[16,32,256]{2,1,0:T(8,128)S(1)}, f32[16,32,256]{2,1,0:T(8,128)}, u32[]{:S(2)}) copy-start(f32[16,32,256]{2,1,0:T(8,128)} %coef.1) | copy-start | bytes 1572868
  0.7 12.2 %copy-start.3 = (f32[16,32,256]{2,1,0:T(8,128)S(1)}, f32[16,32,256]{2,1,0:T(8,128)}, u32[]{:S(2)}) copy-start(f32[16,32,256]{2,1,0:T(8,128)} %b.1) | copy-start | bytes 1572868
  2.7 10.1 %collective-permute-start = (f32[10,32,256]{2,1,0:T(8,128)S(1)}, f32[10,32,256]{2,1,0:T(8,128)S(1)}, u32[]{:S(2)}, u32[]{:S(2)}) collective-permute-start(f32[10,32,256]{2,1,0:T(8,128)S(1)} %pad_maximum_fusion), channel_id=1, source_target_pairs={{0,8},{8,0},{16,24},{24,16},{1,9},{9,1},{17,25},{25,17},{2,10},{10... | collective-permute-start | bytes 983048 | tf_op jit(solution)/shard_map/ppermute | solution.py:23
  3.3 9.6 %collective-permute-start.1 = (f32[10,32,256]{2,1,0:T(8,128)S(1)}, f32[10,32,256]{2,1,0:T(8,128)S(1)}, u32[]{:S(2)}, u32[]{:S(2)}) collective-permute-start(f32[10,32,256]{2,1,0:T(8,128)S(1)} %pad_maximum_fusion.1), channel_id=1, source_target_pairs={{8,16},{16,8},{9,17},{17,9},{10,18},{18,10},{11,19},{19,11},{12,20... | collective-permute-start | bytes 983048 | tf_op jit(solution)/shard_map/ppermute | solution.py:23
  7.0 5.9 %collective-permute-start.2 = (f32[10,16,256]{2,1,0:T(8,128)S(1)}, f32[10,16,256]{2,1,0:T(8,128)S(1)}, u32[]{:S(2)}, u32[]{:S(2)}) collective-permute-start(f32[10,16,256]{2,1,0:T(8,128)S(1)} %pad_maximum_fusion.2), channel_id=1, source_target_pairs={{0,1},{1,0},{2,3},{3,2},{4,5},{5,4},{6,7},{7,6},{8,9},{9,8},{10,11... | collective-permute-start | bytes 491528 | tf_op jit(solution)/shard_map/ppermute | solution.py:23
  9.6 3.3 %collective-permute-start.3 = (f32[10,16,256]{2,1,0:T(8,128)S(1)}, f32[10,16,256]{2,1,0:T(8,128)S(1)}, u32[]{:S(2)}, u32[]{:S(2)}) collective-permute-start(f32[10,16,256]{2,1,0:T(8,128)S(1)} %pad_maximum_fusion.3), channel_id=1, source_target_pairs={{1,2},{2,1},{3,4},{4,3},{5,6},{6,5},{9,10},{10,9},{11,12},{12,11},... | collective-permute-start | bytes 491528 | tf_op jit(solution)/shard_map/ppermute | solution.py:23
  12.9 2.2 %copy-start = (f32[8,16,32,256]{3,2,1,0:T(8,128)S(1)}, f32[8,16,32,256]{3,2,1,0:T(8,128)}, u32[]{:S(2)}) copy-start(f32[8,16,32,256]{3,2,1,0:T(8,128)} %z.5) | copy-start | bytes 12582916
  52.5 4.7 %collective-permute-start.4 = (f32[32,256]{1,0:T(8,128)S(1)}, f32[32,256]{1,0:T(8,128)S(1)}, u32[]{:S(2)}, u32[]{:S(2)}) collective-permute-start(f32[32,256]{1,0:T(8,128)S(1)} %get-tuple-element.59), channel_id=1, source_target_pairs={{0,8},{8,0},{16,24},{24,16},{1,9},{9,1},{17,25},{25,17},{2,10},{10... | collective-permute-start | bytes 98312 | tf_op jit(solution)/shard_map/ppermute | solution.py:23
  52.7 4.5 %collective-permute-start.5 = (f32[32,256]{1,0:T(8,128)S(1)}, f32[32,256]{1,0:T(8,128)S(1)}, u32[]{:S(2)}, u32[]{:S(2)}) collective-permute-start(f32[32,256]{1,0:T(8,128)S(1)} %get-tuple-element.60), channel_id=1, source_target_pairs={{8,16},{16,8},{9,17},{17,9},{10,18},{18,10},{11,19},{19,11},{12,20... | collective-permute-start | bytes 98312 | tf_op jit(solution)/shard_map/ppermute | solution.py:23
  53.4 3.8 %collective-permute-start.6 = (f32[16,256]{1,0:T(8,128)S(1)}, f32[16,256]{1,0:T(8,128)S(1)}, u32[]{:S(2)}, u32[]{:S(2)}) collective-permute-start(f32[16,256]{1,0:T(8,128)S(1)} %get-tuple-element.61), channel_id=1, source_target_pairs={{0,1},{1,0},{2,3},{3,2},{4,5},{5,4},{6,7},{7,6},{8,9},{9,8},{10,11... | collective-permute-start | bytes 49160 | tf_op jit(solution)/shard_map/ppermute | solution.py:23
  54.1 3.1 %collective-permute-start.7 = (f32[16,256]{1,0:T(8,128)S(1)}, f32[16,256]{1,0:T(8,128)S(1)}, u32[]{:S(2)}, u32[]{:S(2)}) collective-permute-start(f32[16,256]{1,0:T(8,128)S(1)} %get-tuple-element.62), channel_id=1, source_target_pairs={{1,2},{2,1},{3,4},{4,3},{5,6},{6,5},{9,10},{10,9},{11,12},{12,11},... | collective-permute-start | bytes 49160 | tf_op jit(solution)/shard_map/ppermute | solution.py:23
  75.9 4.6 %collective-permute-start.8 = (f32[32,256]{1,0:T(8,128)S(1)}, f32[32,256]{1,0:T(8,128)S(1)}, u32[]{:S(2)}, u32[]{:S(2)}) collective-permute-start(f32[32,256]{1,0:T(8,128)S(1)} %get-tuple-element.69), channel_id=1, source_target_pairs={{0,8},{8,0},{16,24},{24,16},{1,9},{9,1},{17,25},{25,17},{2,10},{10... | collective-permute-start | bytes 98312 | tf_op jit(solution)/shard_map/ppermute | solution.py:23
  76.0 4.5 %collective-permute-start.9 = (f32[32,256]{1,0:T(8,128)S(1)}, f32[32,256]{1,0:T(8,128)S(1)}, u32[]{:S(2)}, u32[]{:S(2)}) collective-permute-start(f32[32,256]{1,0:T(8,128)S(1)} %get-tuple-element.70), channel_id=1, source_target_pairs={{8,16},{16,8},{9,17},{17,9},{10,18},{18,10},{11,19},{19,11},{12,20... | collective-permute-start | bytes 98312 | tf_op jit(solution)/shard_map/ppermute | solution.py:23
  76.7 3.8 %collective-permute-start.10 = (f32[16,256]{1,0:T(8,128)S(1)}, f32[16,256]{1,0:T(8,128)S(1)}, u32[]{:S(2)}, u32[]{:S(2)}) collective-permute-start(f32[16,256]{1,0:T(8,128)S(1)} %get-tuple-element.71), channel_id=1, source_target_pairs={{0,1},{1,0},{2,3},{3,2},{4,5},{5,4},{6,7},{7,6},{8,9},{9,8},{10,11... | collective-permute-start | bytes 49160 | tf_op jit(solution)/shard_map/ppermute | solution.py:23
  77.4 3.1 %collective-permute-start.11 = (f32[16,256]{1,0:T(8,128)S(1)}, f32[16,256]{1,0:T(8,128)S(1)}, u32[]{:S(2)}, u32[]{:S(2)}) collective-permute-start(f32[16,256]{1,0:T(8,128)S(1)} %get-tuple-element.72), channel_id=1, source_target_pairs={{1,2},{2,1},{3,4},{4,3},{5,6},{6,5},{9,10},{10,9},{11,12},{12,11},... | collective-permute-start | bytes 49160 | tf_op jit(solution)/shard_map/ppermute | solution.py:23

commit v5 on v4

--- a/solution.py
+++ b/solution.py
@@ -80,6 +80,16 @@
     left, right = beside_z(v)
     out = diag[i] * v - fx[i] * before - fx[i + 1] * after
     return out - fyl[i] * below - fyu[i] * above - fzl[i] * left - fzu[i] * right
+
+
+def pack_kernel(ids, x0, coef, z, sx0, sx1, sy0, sy1):
+    num, nx, ny, _ = z.shape
+    evx, evy = ids[0] == 1, ids[1] == 1
+    for f, ref in enumerate([coef, x0] + [z.at[k] for k in range(num)]):
+        low, high = ref[0], ref[nx - 1]
+        sx0[f], sx1[f] = jnp.where(evx, high, low), jnp.where(evx, low, high)
+        low, high = ref[:, 0, :], ref[:, ny - 1, :]
+        sy0[f], sy1[f] = jnp.where(evy, high, low), jnp.where(evy, low, high)
 
 
 def prepare_kernel(ids, b, x0, coef, z, rx0, rx1, ry0, ry1, fx, fyl, fyu, fzl, fzu, diag, dinv, r0, zxl, zxh, zyl, zyh, out, cext, xext, yrow, acc, zy0):
@@ -111,14 +121,16 @@
         return carry
 
     lax.fori_loop(0, nx + 1, faces_x, 0)
-    lane, row = iota((ny, nz), 1), iota((ny, nz), 0)
+    lane, deep, row = iota((ny, nz), 1), iota((ny, nz), 0), iota((8, nz), 0)
 
     def faces_yz(i, carry):
         c = cext[i + 1]
-        below, above = beside_y(c, yrow[0, pl.ds(i, 1), :], yrow[1, pl.ds(i, 1), :])
-        left, right = beside_z(c)
-        yl, yu = face(below, c), face(c, above)
-        zl, zu = face(jnp.where(lane == 0, 0.0, left), c), face(c, jnp.where(lane == nz - 1, 0.0, right))
+        below = jnp.where(deep == 0, yrow[0, pl.ds(i, 1), :], pltpu.roll(c, 1, 0))
+        left, _ = beside_z(c)
+        yl, zl = face(below, c), face(jnp.where(lane == 0, 0.0, left), c)
+        edge = face(c[ny - 1 : ny, :], yrow[1, pl.ds(i, 1), :])
+        yu = jnp.where(deep == ny - 1, edge, pltpu.roll(yl, ny - 1, 0))
+        zu = jnp.where(lane == nz - 1, c, pltpu.roll(zl, nz - 1, 1))
         d = fx[i + 1] + fx[i] + yu + yl + zu + zl
         fyl[i], fyu[i] = yl, yu
         fzl[i], fzu[i] = jnp.where(lane == 0, 0.0, zl), jnp.where(lane == nz - 1, 0.0, zu)
@@ -133,19 +145,25 @@
     def plane(i, carry):
         r = b[i] - act(i, xext[i + 1], xext[i], xext[i + 2], yrow[2, pl.ds(i, 1), :], yrow[3, pl.ds(i, 1), :], faces)
         r0[i] = r
-        fa = jnp.where(i > 0, fx[i], 0.0)
-        fb = jnp.where(i < nx - 1, fx[i + 1], 0.0)
         before, after = jnp.maximum(i - 1, 0), jnp.minimum(i + 1, nx - 1)
-        yl, yu = jnp.where(row == 0, 0.0, fyl[i]), jnp.where(row == ny - 1, 0.0, fyu[i])
+        for s in range(0, ny, 8):
+            rows = slice(s, s + 8)
+            fa, fb = jnp.where(i > 0, fx[i, rows, :], 0.0), jnp.where(i < nx - 1, fx[i + 1, rows, :], 0.0)
+            yl, yu, zl, zu, mid = fyl[i, rows, :], fyu[i, rows, :], fzl[i, rows, :], fzu[i, rows, :], diag[i, rows, :]
+            yl = jnp.where(row == 0, 0.0, yl) if s == 0 else yl
+            yu = jnp.where(row == 7, 0.0, yu) if s == ny - 8 else yu
+            strips = [z[k, i, rows, :] for k in range(num)]
+            for k, v in enumerate(strips):
+                left, right = beside_z(v)
+                below = z[k, i, s - 1 : s + 7, :] if s > 0 else pltpu.roll(v, 1, 0)
+                above = z[k, i, s + 1 : s + 9, :] if s < ny - 8 else pltpu.roll(v, 7, 0)
+                w = mid * v - fa * z[k, before, rows, :] - fb * z[k, after, rows, :]
+                w = w - zl * left - zu * right - yl * below - yu * above
+                for m in range(k + 1):
+                    add_to(acc, 2 * square + m * num + k, w * strips[m])
+                add_to(acc, 3 * square + k, v * r[rows, :])
         for k in range(num):
-            v = z[k, i]
-            left, right = beside_z(v)
-            w = diag[i] * v - fa * z[k, before] - fb * z[k, after] - fzl[i] * left - fzu[i] * right
-            w = w - yl * pltpu.roll(v, 1, 0) - yu * pltpu.roll(v, ny - 1, 0)
-            for m in range(k + 1):
-                add_to(acc, 2 * square + m * num + k, w * z[m, i])
-            add_to(acc, 3 * square + k, v * r)
-            zy0[k, pl.ds(i, 1), :] = v[0:1, :] * fyl[i, 0:1, :]
+            zy0[k, pl.ds(i, 1), :] = z[k, i, 0:1, :] * fyl[i, 0:1, :]
         return carry
 
     lax.fori_loop(0, nx, plane, 0, unroll=4)
@@ -195,7 +213,7 @@
     return lax.rem(lax.div(index, num), down) * across + across_id, across_id
 
 
-def small_inverses(blocks, group=4):
+def small_inverses(blocks, group=8):
     size = blocks[0].shape[0]
     lane, row, head = iota((size, size), 1), iota((size, size), 0), iota((1, size), 1)
     for start in range(0, size, group):
@@ -453,10 +471,11 @@
     order = e.shape[0]
     g = got[:, 0, :]
     beta = jnp.sum(g, axis=0, keepdims=True)[:, 0:1] / state_old[0:1, 0:1]
-    col = column(g, num, order, across, 0, 8)
+    parts, n = g, g.shape[0]
     for group, offset in ((1, across), (2, -across), (3, 1), (4, -1)):
-        col = col + column(g, num, order, across, offset, 8 + group * num)
-    ys = amounts(ids, solve(e, col), num)
+        moved = pltpu.roll(pltpu.roll(g, (n - offset) % n, 0), 128 - group * num, 1)
+        parts = parts + moved
+    ys = amounts(ids, solve(e, column(parts, num, order, across, 0, 8)), num)
     wide = [jnp.broadcast_to(c, (ny, nz)) for c in ys[0]]
     wide_beta = jnp.broadcast_to(beta, (ny, nz))
 
@@ -492,18 +511,19 @@
         shifts.append((order - place * num) % order)
     ids = jnp.stack([evx.astype(jnp.int32), evy.astype(jnp.int32)] + shifts)
 
-    def pack(at, index):
-        return jnp.concatenate([at(coef, index)[None], at(start_field, index)[None], at(deflation, index)])
-
-    at_x = lambda v, i: lax.dynamic_index_in_dim(v, i, v.ndim - 3, keepdims=False)
-    at_y = lambda v, i: lax.dynamic_index_in_dim(v, i, v.ndim - 2, keepdims=False)
-    xs = (jnp.where(evx, nx - 1, 0), jnp.where(evx, 0, nx - 1))
-    ys = (jnp.where(evy, ny - 1, 0), jnp.where(evy, 0, ny - 1))
-    raw = swaps([pack(at_x, xs[0]), pack(at_x, xs[1]), pack(at_y, ys[0]), pack(at_y, ys[1])])
-
     field, layer_x, layer_y = (nx, ny, nz), (ny, nz), (nx, nz)
     ext, two_y = (nx + 2, ny, nz), (2, nx, nz)
     layers = [layer_x, layer_x, layer_y, layer_y]
+    raw = swaps(
+        call(
+            order,
+            pack_kernel,
+            "pack",
+            [ids, start_field, coef, deflation],
+            [(2 + num,) + layer_x] * 2 + [(2 + num,) + layer_y] * 2,
+            [],
+        )
+    )
     wide = -(-(3 * num * num + num) // 128)
     *faces, dinv, r0, zxl, zxh, zyl, zyh, out = call(
         order,

time: 113 us -> 110 us (0.973)
  local copies, waits for them, and re-layouts: 7.26 us -> 4.37 us
    dynamic_slice x3 -> x0, local copies, waits for them, and re-layouts: 3.76 us -> none  [the longest x2 2.93 us: per_device(): lax.dynamic_index_in_dim(v, i, v.ndim - 2, keepdims=False)]
    unnamed x14 -> x10, local copies, waits for them, and re-layouts: 2.23 us -> 4.28 us
    squeeze x1 -> x0, local copies, waits for them, and re-layouts: 1.18 us -> none  [per_device(): lax.dynamic_index_in_dim(v, i, v.ndim - 3, keepdims=False)]
    pallas_call x7 -> x8, Pallas kernels: 31.2 us -> 30.6 us  [call(): pl.pallas_call(kernel, name=name, in_specs=[SMEM] + [VMEM] * (len(args) -...]
  transfers between devices with their start and end apart: 12 -> 12, of which waited for: 3 -> 3; matrix products, arithmetic and copies ran while one was open for 3% -> 0% of each run, Pallas kernels for 0% -> 0%
where the time goes in v5:
time: 110 us; the launch traced here: 109 us
  blocking collectives  57.2 us (52%)
  Pallas kernels  30.6 us (28%)
  starting transfers between devices  8.84 us (8%)
  waiting for transfers between devices  7.52 us (7%)
  local copies, waits for them, and re-layouts  4.37 us (4%)
    all_to_all x4, blocking collectives, everywhere(): return lax.all_to_all(payload, BOTH, 0, 0)  57.2 us
    pallas_call x8, Pallas kernels, call(): pl.pallas_call(kernel, name=name, in_specs=[SMEM] + [VMEM] * (len(args) -...  30.6 us
    ppermute x12, starting transfers between devices, swap(): return lax.ppermute(value, axis, pairs)  8.84 us
    ppermute x12, waiting for transfers between devices, swap(): return lax.ppermute(value, axis, pairs)  7.52 us
    unnamed x10, local copies, waits for them, and re-layouts  4.28 us
  transfers between devices with their start and end apart: 12, of which 3 were waited for; matrix products, arithmetic and copies ran while one was open for 0% of the time, Pallas kernels for 0%

profile of v5, /device:TPU:0, one launch (start us, length us, event | category | flops | bytes accessed | tf_op | source)
XLA Modules:
  0.0 109.5 jit_solution(5070865320250552599)
XLA Ops:
  0.8 2.2 %copy-done = f32[8,16,32,256]{3,2,1,0:T(8,128)S(1)} copy-done((f32[8,16,32,256]{3,2,1,0:T(8,128)S(1)}, f32[8,16,32,256]{3,2,1,0:T(8,128)}, u32[]{:S(2)}) %copy-start) | copy-done | bytes 4194328
  3.0 1.0 copy-done.2
  4.1 1.0 copy-done.3
  5.1 0.7 pack.1
  6.4 0.8 collective-permute-start.1
  7.2 2.6 %collective-permute-start.2 = (f32[10,16,256]{2,1,0:T(8,128)S(1)}, f32[10,16,256]{2,1,0:T(8,128)S(1)}, u32[]{:S(2)}, u32[]{:S(2)}) collective-permute-start(f32[10,16,256]{2,1,0:T(8,128)S(1)} %get-tuple-element.50), channel_id=1, source_target_pairs={{0,1},{1,0},{2,3},{3,2},{4,5},{5,4},{6,7},{7,6},{8,9},{9,8},{10,11... | collective-permute-start | bytes 491528 | tf_op jit(solution)/shard_map/ppermute | solution.py:23
  9.8 0.7 collective-permute-start.3
  10.4 2.6 %collective-permute-done.2.ry0 = f32[10,16,256]{2,1,0:T(8,128)S(1)} collective-permute-done((f32[10,16,256]{2,1,0:T(8,128)S(1)}, f32[10,16,256]{2,1,0:T(8,128)S(1)}, u32[]{:S(2)}, u32[]{:S(2)}) %collective-permute-start.2) | collective-permute-done | bytes 163872 | tf_op jit(solution)/shard_map/ppermute | solution.py:23
  13.1 8.3 %prepare.1 = (f32[17,32,256]{2,1,0:T(8,128)S(1)}, f32[16,32,256]{2,1,0:T(8,128)S(1)}, f32[16,32,256]{2,1,0:T(8,128)S(1)}, f32[16,32,256]{2,1,0:T(8,128)S(1)}, f3...) custom-call(s32[7]{0:T(128)S(1)} %stack.39.ids.refs_0_, ...), custom_call_target="tpu_custom_call" | custom-call | tf_op jit(solution)/shard_map/prepare/pallas_call | solution.py:490
  21.4 18.5 %all_to_all.20.got = f32[32,2,128]{2,1,0:T(2,128)S(1)} all-to-all(f32[32,2,128]{2,1,0:T(2,128)S(1)} %get-tuple-element.52), channel_id=1, replica_groups=mesh['gx'=4,'gy'=8] {'gx','gy'}, dimensions={0} | all-to-all | bytes 65536 | tf_op jit(solution)/shard_map/all_to_all | solution.py:31
  39.9 9.5 %start.1 = (f32[256,256]{1,0:T(8,128)S(1)}, f32[16,32,256]{2,1,0:T(8,128)S(1)}, f32[16,32,256]{2,1,0:T(8,128)S(1)}, f32[16,32,256]{2,1,0:T(8,128)S(1)}, f32[32,2...) custom-call(s32[7]{0:T(128)S(1)} %stack.39.ids.refs_0_, ...), custom_call_target="tpu_custom_call" | custom-call | tf_op jit(solution)/shard_map/start/pallas_call | solution.py:490
  50.3 0.7 collective-permute-start.6
  51.7 2.4 %collective-permute-done.6.refs_12_ = f32[16,256]{1,0:T(8,128)S(1)} collective-permute-done((f32[16,256]{1,0:T(8,128)S(1)}, f32[16,256]{1,0:T(8,128)S(1)}, u32[]{:S(2)}, u32[]{:S(2)}) %collective-permute-start.6) | collective-permute-done | bytes 16416 | tf_op jit(solution)/shard_map/ppermute | solution.py:23
  54.1 1.6 %product.2 = (f32[16,32,256]{2,1,0:T(8,128)S(1)}, f32[32,1,128]{2,1,0:T(1,128)S(1)}) custom-call(s32[7]{0:T(128)S(1)} %stack.39.ids.refs_0_, f32[16,32,256]{2,1,0:T(8,128)S(1)} %get-tuple-element.65.refs_1_.refs_15_, f32[16,32,256]{2,1,0:T(8,128)S(1)} %get-tuple-element.66.refs_2_.refs_18_, f32[8,16,32,256]{3,2,1,0:T(8,128)S(1)} %copy-done.1, ...), custom_call_target="tpu_custom_call" | custom-call | tf_op jit(solution)/shard_map/product/pallas_call | solution.py:490
  55.8 14.9 %all_to_all.21.refs_1_ = f32[32,1,128]{2,1,0:T(1,128)S(1)} all-to-all(f32[32,1,128]{2,1,0:T(1,128)S(1)} %get-tuple-element.71), channel_id=1, replica_groups=mesh['gx'=4,'gy'=8] {'gx','gy'}, dimensions={0} | all-to-all | bytes 32768 | tf_op jit(solution)/shard_map/all_to_all | solution.py:31
  70.7 2.1 %update.2 = (f32[16,32,256]{2,1,0:T(8,128)S(1)}, f32[16,32,256]{2,1,0:T(8,128)S(1)}, f32[16,32,256]{2,1,0:T(8,128)S(1)}, f32[16,32,256]{2,1,0:T(8,128)S(1)}, f32...) custom-call(s32[7]{0:T(128)S(1)} %stack.39.ids.refs_0_, ...), custom_call_target="tpu_custom_call" | custom-call | tf_op jit(solution)/shard_map/update/pallas_call | solution.py:490
  72.9 0.7 collective-permute-start.9
  73.6 0.7 collective-permute-start.10
  74.9 2.5 %collective-permute-done.10.refs_12_ = f32[16,256]{1,0:T(8,128)S(1)} collective-permute-done((f32[16,256]{1,0:T(8,128)S(1)}, f32[16,256]{1,0:T(8,128)S(1)}, u32[]{:S(2)}, u32[]{:S(2)}) %collective-permute-start.10) | collective-permute-done | bytes 16416 | tf_op jit(solution)/shard_map/ppermute | solution.py:23
  77.4 1.7 %product.3 = (f32[16,32,256]{2,1,0:T(8,128)S(1)}, f32[32,1,128]{2,1,0:T(1,128)S(1)}) custom-call(s32[7]{0:T(128)S(1)} %stack.39.ids.refs_0_, f32[16,32,256]{2,1,0:T(8,128)S(1)} %get-tuple-element.75.refs_1_.refs_15_, f32[16,32,256]{2,1,0:T(8,128)S(1)} %get-tuple-element.76.refs_2_.refs_18_, f32[8,16,32,256]{3,2,1,0:T(8,128)S(1)} %copy-done.1, ...), custom_call_target="tpu_custom_call" | custom-call | tf_op jit(solution)/shard_map/product/pallas_call | solution.py:490
  79.1 15.0 %all_to_all.22.refs_1_ = f32[32,1,128]{2,1,0:T(1,128)S(1)} all-to-all(f32[32,1,128]{2,1,0:T(1,128)S(1)} %get-tuple-element.82), channel_id=1, replica_groups=mesh['gx'=4,'gy'=8] {'gx','gy'}, dimensions={0} | all-to-all | bytes 32768 | tf_op jit(solution)/shard_map/all_to_all | solution.py:31
  94.0 4.4 %update.3 = (f32[16,32,256]{2,1,0:T(8,128)S(1)}, f32[16,32,256]{2,1,0:T(8,128)}, f32[16,32,256]{2,1,0:T(8,128)}, f32[16,32,256]{2,1,0:T(8,128)}, f32[16,32,256]{...) custom-call(s32[7]{0:T(128)S(1)} %stack.39.ids.refs_0_, f32[32,1,128]{2,1,0:T(1,128)S(1)} %all_to_all.22.refs_1_, ...), custom_call_target="tpu_custom_call" | custom-call | tf_op jit(solution)/shard_map/update/pallas_call | solution.py:490
  98.4 8.8 %all_to_all.23.got = f32[32,1,128]{2,1,0:T(1,128)S(1)} all-to-all(f32[32,1,128]{2,1,0:T(1,128)S(1)} %get-tuple-element.89), channel_id=1, replica_groups=mesh['gx'=4,'gy'=8] {'gx','gy'}, dimensions={0} | all-to-all | bytes 32768 | tf_op jit(solution)/shard_map/all_to_all | solution.py:31
  107.2 2.3 %finish.1 = f32[16,32,256]{2,1,0:T(8,128)} custom-call(s32[7]{0:T(128)S(1)} %stack.39.ids.refs_0_, f32[32,1,128]{2,1,0:T(1,128)S(1)} %all_to_all.23.got, f32[256,256]{1,0:T(8,128)S(1)} %get-tuple-element.72.refs_2_.e, f32[8,16,32,256]{3,2,1,0:T(8,128)S(1)} %copy-done.1, f32[16,32,256]{2,1,0:T(8,128)S(1)} %get-tuple-element.90.p, ...), custom_call_target="tpu_custom_call" | custom-call | tf_op jit(solution)/shard_map/finish/pallas_call | solution.py:490
  (23 shorter events, 2.8 us)
Async XLA Ops:
  0.8 2.2 %copy-start = (f32[8,16,32,256]{3,2,1,0:T(8,128)S(1)}, f32[8,16,32,256]{3,2,1,0:T(8,128)}, u32[]{:S(2)}) copy-start(f32[8,16,32,256]{3,2,1,0:T(8,128)} %z.7) | copy-start | bytes 12582916
  3.0 1.0 copy-start.2
  4.1 1.0 copy-start.3
  5.1 8.0 %copy-start.4 = (f32[16,32,256]{2,1,0:T(8,128)S(1)}, f32[16,32,256]{2,1,0:T(8,128)}, u32[]{:S(2)}) copy-start(f32[16,32,256]{2,1,0:T(8,128)} %b.1) | copy-start | bytes 1572868
  5.8 34.1 %copy-start.1 = (f32[8,16,32,256]{3,2,1,0:T(8,128)S(1)}, f32[8,16,32,256]{3,2,1,0:T(8,128)}, u32[]{:S(2)}) copy-start(f32[8,16,32,256]{3,2,1,0:T(8,128)} %z.7) | copy-start | bytes 12582916
  5.9 7.2 %collective-permute-start = (f32[10,32,256]{2,1,0:T(8,128)S(1)}, f32[10,32,256]{2,1,0:T(8,128)S(1)}, u32[]{:S(2)}, u32[]{:S(2)}) collective-permute-start(f32[10,32,256]{2,1,0:T(8,128)S(1)} %get-tuple-element.48), channel_id=1, source_target_pairs={{0,8},{8,0},{16,24},{24,16},{1,9},{9,1},{17,25},{25,17},{2,10},{10... | collective-permute-start | bytes 983048 | tf_op jit(solution)/shard_map/ppermute | solution.py:23
  6.4 6.7 %collective-permute-start.1 = (f32[10,32,256]{2,1,0:T(8,128)S(1)}, f32[10,32,256]{2,1,0:T(8,128)S(1)}, u32[]{:S(2)}, u32[]{:S(2)}) collective-permute-start(f32[10,32,256]{2,1,0:T(8,128)S(1)} %get-tuple-element.49), channel_id=1, source_target_pairs={{8,16},{16,8},{9,17},{17,9},{10,18},{18,10},{11,19},{19,11},{12,20... | collective-permute-start | bytes 983048 | tf_op jit(solution)/shard_map/ppermute | solution.py:23
  7.2 5.9 %collective-permute-start.2 = (f32[10,16,256]{2,1,0:T(8,128)S(1)}, f32[10,16,256]{2,1,0:T(8,128)S(1)}, u32[]{:S(2)}, u32[]{:S(2)}) collective-permute-start(f32[10,16,256]{2,1,0:T(8,128)S(1)} %get-tuple-element.50), channel_id=1, source_target_pairs={{0,1},{1,0},{2,3},{3,2},{4,5},{5,4},{6,7},{7,6},{8,9},{9,8},{10,11... | collective-permute-start | bytes 491528 | tf_op jit(solution)/shard_map/ppermute | solution.py:23
  9.8 3.3 %collective-permute-start.3 = (f32[10,16,256]{2,1,0:T(8,128)S(1)}, f32[10,16,256]{2,1,0:T(8,128)S(1)}, u32[]{:S(2)}, u32[]{:S(2)}) collective-permute-start(f32[10,16,256]{2,1,0:T(8,128)S(1)} %get-tuple-element.51), channel_id=1, source_target_pairs={{1,2},{2,1},{3,4},{4,3},{5,6},{6,5},{9,10},{10,9},{11,12},{12,11},... | collective-permute-start | bytes 491528 | tf_op jit(solution)/shard_map/ppermute | solution.py:23
  49.4 4.7 %collective-permute-start.4 = (f32[32,256]{1,0:T(8,128)S(1)}, f32[32,256]{1,0:T(8,128)S(1)}, u32[]{:S(2)}, u32[]{:S(2)}) collective-permute-start(f32[32,256]{1,0:T(8,128)S(1)} %get-tuple-element.67), channel_id=1, source_target_pairs={{0,8},{8,0},{16,24},{24,16},{1,9},{9,1},{17,25},{25,17},{2,10},{10... | collective-permute-start | bytes 98312 | tf_op jit(solution)/shard_map/ppermute | solution.py:23
  49.6 4.5 %collective-permute-start.5 = (f32[32,256]{1,0:T(8,128)S(1)}, f32[32,256]{1,0:T(8,128)S(1)}, u32[]{:S(2)}, u32[]{:S(2)}) collective-permute-start(f32[32,256]{1,0:T(8,128)S(1)} %get-tuple-element.68), channel_id=1, source_target_pairs={{8,16},{16,8},{9,17},{17,9},{10,18},{18,10},{11,19},{19,11},{12,20... | collective-permute-start | bytes 98312 | tf_op jit(solution)/shard_map/ppermute | solution.py:23
  50.3 3.8 %collective-permute-start.6 = (f32[16,256]{1,0:T(8,128)S(1)}, f32[16,256]{1,0:T(8,128)S(1)}, u32[]{:S(2)}, u32[]{:S(2)}) collective-permute-start(f32[16,256]{1,0:T(8,128)S(1)} %get-tuple-element.69), channel_id=1, source_target_pairs={{0,1},{1,0},{2,3},{3,2},{4,5},{5,4},{6,7},{7,6},{8,9},{9,8},{10,11... | collective-permute-start | bytes 49160 | tf_op jit(solution)/shard_map/ppermute | solution.py:23
  51.0 3.1 %collective-permute-start.7 = (f32[16,256]{1,0:T(8,128)S(1)}, f32[16,256]{1,0:T(8,128)S(1)}, u32[]{:S(2)}, u32[]{:S(2)}) collective-permute-start(f32[16,256]{1,0:T(8,128)S(1)} %get-tuple-element.70), channel_id=1, source_target_pairs={{1,2},{2,1},{3,4},{4,3},{5,6},{6,5},{9,10},{10,9},{11,12},{12,11},... | collective-permute-start | bytes 49160 | tf_op jit(solution)/shard_map/ppermute | solution.py:23
  72.8 4.6 %collective-permute-start.8 = (f32[32,256]{1,0:T(8,128)S(1)}, f32[32,256]{1,0:T(8,128)S(1)}, u32[]{:S(2)}, u32[]{:S(2)}) collective-permute-start(f32[32,256]{1,0:T(8,128)S(1)} %get-tuple-element.77), channel_id=1, source_target_pairs={{0,8},{8,0},{16,24},{24,16},{1,9},{9,1},{17,25},{25,17},{2,10},{10... | collective-permute-start | bytes 98312 | tf_op jit(solution)/shard_map/ppermute | solution.py:23
  72.9 4.5 %collective-permute-start.9 = (f32[32,256]{1,0:T(8,128)S(1)}, f32[32,256]{1,0:T(8,128)S(1)}, u32[]{:S(2)}, u32[]{:S(2)}) collective-permute-start(f32[32,256]{1,0:T(8,128)S(1)} %get-tuple-element.78), channel_id=1, source_target_pairs={{8,16},{16,8},{9,17},{17,9},{10,18},{18,10},{11,19},{19,11},{12,20... | collective-permute-start | bytes 98312 | tf_op jit(solution)/shard_map/ppermute | solution.py:23
  73.6 3.8 %collective-permute-start.10 = (f32[16,256]{1,0:T(8,128)S(1)}, f32[16,256]{1,0:T(8,128)S(1)}, u32[]{:S(2)}, u32[]{:S(2)}) collective-permute-start(f32[16,256]{1,0:T(8,128)S(1)} %get-tuple-element.79), channel_id=1, source_target_pairs={{0,1},{1,0},{2,3},{3,2},{4,5},{5,4},{6,7},{7,6},{8,9},{9,8},{10,11... | collective-permute-start | bytes 49160 | tf_op jit(solution)/shard_map/ppermute | solution.py:23
  74.3 3.1 %collective-permute-start.11 = (f32[16,256]{1,0:T(8,128)S(1)}, f32[16,256]{1,0:T(8,128)S(1)}, u32[]{:S(2)}, u32[]{:S(2)}) collective-permute-start(f32[16,256]{1,0:T(8,128)S(1)} %get-tuple-element.80), channel_id=1, source_target_pairs={{1,2},{2,1},{3,4},{4,3},{5,6},{6,5},{9,10},{10,9},{11,12},{12,11},... | collective-permute-start | bytes 49160 | tf_op jit(solution)/shard_map/ppermute | solution.py:23

commit v6 on v5

--- a/solution.py
+++ b/solution.py
@@ -92,66 +92,39 @@
         sy0[f], sy1[f] = jnp.where(evy, high, low), jnp.where(evy, low, high)
 
 
-def prepare_kernel(ids, b, x0, coef, z, rx0, rx1, ry0, ry1, fx, fyl, fyu, fzl, fzu, diag, dinv, r0, zxl, zxh, zyl, zyh, out, cext, xext, yrow, acc, zy0):
+def inner_kernel(ids, coef, z, fx, fyl, fyu, fzl, fzu, part, acc):
     num, nx, ny, nz = z.shape
-    evx, evy = ids[0] == 1, ids[1] == 1
-    cext[0] = jnp.where(evx, rx1[0], rx0[0])
-    cext[nx + 1] = jnp.where(evx, rx0[0], rx1[0])
-    xext[0] = jnp.where(evx, rx1[1], rx0[1])
-    xext[nx + 1] = jnp.where(evx, rx0[1], rx1[1])
-    for k in range(num):
-        zxl[k] = jnp.where(evx, rx1[2 + k], rx0[2 + k])
-        zxh[k] = jnp.where(evx, rx0[2 + k], rx1[2 + k])
-        zyl[k] = jnp.where(evy, ry1[2 + k], ry0[2 + k])
-        zyh[k] = jnp.where(evy, ry0[2 + k], ry1[2 + k])
-    for f in range(2):
-        yrow[2 * f] = jnp.where(evy, ry1[f], ry0[f])
-        yrow[2 * f + 1] = jnp.where(evy, ry0[f], ry1[f])
+    lane, deep = iota((ny, nz), 1), iota((ny, nz), 0)
     acc[...] = jnp.zeros_like(acc)
-
-    def fill(i, carry):
-        cext[i + 1] = coef[i]
-        xext[i + 1] = x0[i]
-        return carry
-
-    lax.fori_loop(0, nx, fill, 0, unroll=4)
+    fx[0] = jnp.zeros((ny, nz), F32)
+    fx[nx] = jnp.zeros((ny, nz), F32)
 
     def faces_x(i, carry):
-        fx[i] = face(cext[i], cext[i + 1])
-        return carry
-
-    lax.fori_loop(0, nx + 1, faces_x, 0)
-    lane, deep, row = iota((ny, nz), 1), iota((ny, nz), 0), iota((8, nz), 0)
+        fx[i] = face(coef[i - 1], coef[i])
+        return carry
+
+    lax.fori_loop(1, nx, faces_x, 0)
 
     def faces_yz(i, carry):
-        c = cext[i + 1]
-        below = jnp.where(deep == 0, yrow[0, pl.ds(i, 1), :], pltpu.roll(c, 1, 0))
+        c = coef[i]
         left, _ = beside_z(c)
-        yl, zl = face(below, c), face(jnp.where(lane == 0, 0.0, left), c)
-        edge = face(c[ny - 1 : ny, :], yrow[1, pl.ds(i, 1), :])
-        yu = jnp.where(deep == ny - 1, edge, pltpu.roll(yl, ny - 1, 0))
+        yl = jnp.where(deep == 0, 0.0, face(pltpu.roll(c, 1, 0), c))
+        zl = face(jnp.where(lane == 0, 0.0, left), c)
+        yu = pltpu.roll(yl, ny - 1, 0)
         zu = jnp.where(lane == nz - 1, c, pltpu.roll(zl, nz - 1, 1))
-        d = fx[i + 1] + fx[i] + yu + yl + zu + zl
         fyl[i], fyu[i] = yl, yu
         fzl[i], fzu[i] = jnp.where(lane == 0, 0.0, zl), jnp.where(lane == nz - 1, 0.0, zu)
-        diag[i] = d
-        dinv[i] = 1.0 / d
+        part[i] = fx[i + 1] + fx[i] + yu + yl + zu + zl
         return carry
 
     lax.fori_loop(0, nx, faces_yz, 0, unroll=4)
-    faces = (fx, fyl, fyu, fzl, fzu, diag)
-    square = num * num
 
     def plane(i, carry):
-        r = b[i] - act(i, xext[i + 1], xext[i], xext[i + 2], yrow[2, pl.ds(i, 1), :], yrow[3, pl.ds(i, 1), :], faces)
-        r0[i] = r
         before, after = jnp.maximum(i - 1, 0), jnp.minimum(i + 1, nx - 1)
         for s in range(0, ny, 8):
             rows = slice(s, s + 8)
-            fa, fb = jnp.where(i > 0, fx[i, rows, :], 0.0), jnp.where(i < nx - 1, fx[i + 1, rows, :], 0.0)
-            yl, yu, zl, zu, mid = fyl[i, rows, :], fyu[i, rows, :], fzl[i, rows, :], fzu[i, rows, :], diag[i, rows, :]
-            yl = jnp.where(row == 0, 0.0, yl) if s == 0 else yl
-            yu = jnp.where(row == 7, 0.0, yu) if s == ny - 8 else yu
+            fa, fb, mid = fx[i, rows, :], fx[i + 1, rows, :], part[i, rows, :]
+            yl, yu, zl, zu = fyl[i, rows, :], fyu[i, rows, :], fzl[i, rows, :], fzu[i, rows, :]
             strips = [z[k, i, rows, :] for k in range(num)]
             for k, v in enumerate(strips):
                 left, right = beside_z(v)
@@ -160,29 +133,86 @@
                 w = mid * v - fa * z[k, before, rows, :] - fb * z[k, after, rows, :]
                 w = w - zl * left - zu * right - yl * below - yu * above
                 for m in range(k + 1):
-                    add_to(acc, 2 * square + m * num + k, w * strips[m])
-                add_to(acc, 3 * square + k, v * r[rows, :])
-        for k in range(num):
-            zy0[k, pl.ds(i, 1), :] = z[k, i, 0:1, :] * fyl[i, 0:1, :]
+                    add_to(acc, m * num + k, w * strips[m])
         return carry
 
     lax.fori_loop(0, nx, plane, 0, unroll=4)
     for k in range(num):
         for m in range(k):
-            acc[pl.ds((2 * square + k * num + m) * 8, 8), :] = acc[pl.ds((2 * square + m * num + k) * 8, 8), :]
-
-    def below_blocks(k, carry):
-        weighted = z[k, 0] * fx[0]
+            acc[pl.ds((k * num + m) * 8, 8), :] = acc[pl.ds((m * num + k) * 8, 8), :]
+
+
+def prepare_kernel(ids, b, x0, coef, z, rx0, rx1, ry0, ry1, fx_in, fyl_in, fyu_in, fzl, fzu, part, own, fx, fyl, fyu, diag, dinv, r0, zxl, zxh, zyl, zyh, out, xext, yrow, acc, zy0, zy1, row0, row1):
+    num, nx, ny, nz = z.shape
+    evx, evy = ids[0] == 1, ids[1] == 1
+    xext[0] = jnp.where(evx, rx1[1], rx0[1])
+    xext[nx + 1] = jnp.where(evx, rx0[1], rx1[1])
+    for k in range(num):
+        zxl[k] = jnp.where(evx, rx1[2 + k], rx0[2 + k])
+        zxh[k] = jnp.where(evx, rx0[2 + k], rx1[2 + k])
+        zyl[k] = jnp.where(evy, ry1[2 + k], ry0[2 + k])
+        zyh[k] = jnp.where(evy, ry0[2 + k], ry1[2 + k])
+        row0[k], row1[k] = z[k, :, 0, :], z[k, :, ny - 1, :]
+    for f in range(2):
+        yrow[2 * f] = jnp.where(evy, ry1[f], ry0[f])
+        yrow[2 * f + 1] = jnp.where(evy, ry0[f], ry1[f])
+    square = num * num
+    acc[...] = jnp.zeros_like(acc)
+    acc[pl.ds(2 * square * 8, square * 8), :] = own[...]
+    low_face = face(jnp.where(evx, rx1[0], rx0[0]), coef[0])
+    high_face = face(coef[nx - 1], jnp.where(evx, rx0[0], rx1[0]))
+
+    def fill(i, carry):
+        xext[i + 1] = x0[i]
+        fx[i] = fx_in[i]
+        return carry
+
+    lax.fori_loop(0, nx, fill, 0, unroll=4)
+    fx[0] = low_face
+    fx[nx] = high_face
+    low_y = face(yrow[0], coef[:, 0, :])
+    high_y = face(coef[:, ny - 1, :], yrow[1])
+    for k in range(num):
+        zy0[k], zy1[k] = row0[k] * low_y, row1[k] * high_y
+    yrow[0] = low_y
+    yrow[1] = high_y
+    deep = iota((ny, nz), 0)
+
+    def outer(i, carry):
+        yl = jnp.where(deep == 0, yrow[0, pl.ds(i, 1), :], fyl_in[i])
+        yu = jnp.where(deep == ny - 1, yrow[1, pl.ds(i, 1), :], fyu_in[i])
+        d = part[i] + (yl - fyl_in[i]) + (yu - fyu_in[i]) + (fx[i] - fx_in[i]) + (fx[i + 1] - fx_in[i + 1])
+        fyl[i], fyu[i] = yl, yu
+        diag[i] = d
+        dinv[i] = 1.0 / d
+        return carry
+
+    lax.fori_loop(0, nx, outer, 0, unroll=4)
+    faces = (fx, fyl, fyu, fzl, fzu, diag)
+
+    def plane(i, carry):
+        r = b[i] - act(i, xext[i + 1], xext[i], xext[i + 2], yrow[2, pl.ds(i, 1), :], yrow[3, pl.ds(i, 1), :], faces)
+        r0[i] = r
+        for k in range(num):
+            add_to(acc, 3 * square + k, z[k, i] * r)
+        return carry
+
+    lax.fori_loop(0, nx, plane, 0, unroll=4)
+
+    def edge_blocks(k, carry):
+        low, high = z[k, 0] * fx[0], z[k, nx - 1] * fx[nx]
         for m in range(num):
-            add_to(acc, k * num + m, weighted * zxl[m])
+            add_to(acc, k * num + m, low * zxl[m])
             add_to(acc, square + k * num + m, zy0[k] * zyl[m])
-        return carry
-
-    lax.fori_loop(0, num, below_blocks, 0)
+            at = (2 * square + k * num + m) * 8
+            acc[pl.ds(at, 8), :] += fold(low * z[m, 0] + high * z[m, nx - 1]) + fold(zy0[k] * row0[m] + zy1[k] * row1[m])
+        return carry
+
+    lax.fori_loop(0, num, edge_blocks, 0)
     count = acc.shape[0] // 8
     line = row_of(acc, count, count)
-    for part in range(count // 128):
-        out[:, part, :] = jnp.broadcast_to(line[:, part * 128 : (part + 1) * 128], (out.shape[0], 128))
+    for piece in range(count // 128):
+        out[:, piece, :] = jnp.broadcast_to(line[:, piece * 128 : (piece + 1) * 128], (out.shape[0], 128))
 
 
 def levels(across):
@@ -486,10 +516,11 @@
     lax.fori_loop(0, nx, plane, 0, unroll=4)
 
 
-def call(order, kernel, name, args, outs, scratch):
+def call(order, kernel, name, args, outs, scratch, cost=None):
     return pl.pallas_call(
         kernel,
         name=name,
+        cost_estimate=cost,
         in_specs=[SMEM] + [VMEM] * (len(args) - 1),
         out_specs=[VMEM] * len(outs),
         out_shape=[jax.ShapeDtypeStruct(s, F32) for s in outs],
@@ -525,14 +556,24 @@
         )
     )
     wide = -(-(3 * num * num + num) // 128)
-    *faces, dinv, r0, zxl, zxh, zyl, zyh, out = call(
+    fx, fyl, fyu, fzl, fzu, part, own = call(
+        order,
+        inner_kernel,
+        "inner",
+        [ids, coef, deflation],
+        [(nx + 1, ny, nz)] + [field] * 5 + [(num * num * 8, 128)],
+        [],
+        pl.CostEstimate(flops=250 * num * nx * ny * nz, bytes_accessed=16 << 20, transcendentals=0),
+    )
+    fx, fyl, fyu, diag, dinv, r0, zxl, zxh, zyl, zyh, out = call(
         order,
         prepare_kernel,
         "prepare",
-        [ids, right_side, start_field, coef, deflation, *raw],
-        [(nx + 1, ny, nz)] + [field] * 7 + [(num,) + layer_x] * 2 + [(num,) + layer_y] * 2 + [(n, wide, 128)],
-        [ext, ext, (4, nx, nz), (wide * 128 * 8, 128), (num, nx, nz)],
+        [ids, right_side, start_field, coef, deflation, *raw, fx, fyl, fyu, fzl, fzu, part, own],
+        [(nx + 1, ny, nz)] + [field] * 5 + [(num,) + layer_x] * 2 + [(num,) + layer_y] * 2 + [(n, wide, 128)],
+        [ext, (4, nx, nz), (wide * 128 * 8, 128)] + [(num, nx, nz)] * 4,
     )
+    faces = [fx, fyl, fyu, fzl, fzu, diag]
     basis = [deflation, zxl, zxh, zyl, zyh]
     e, x, r, p, *sent = call(
         order,

time: 110 us -> 106 us (0.964)
  waiting for transfers between devices: 7.52 us -> 4.89 us
  blocking collectives: 57.2 us -> 55 us
    ppermute x12, waiting for transfers between devices: 7.52 us -> 4.89 us  [swap(): return lax.ppermute(value, axis, pairs)]
    all_to_all x4, blocking collectives: 57.2 us -> 55 us  [everywhere(): return lax.all_to_all(payload, BOTH, 0, 0)]
    pallas_call x8 -> x9, Pallas kernels: 30.6 us -> 31.4 us  [call(): pl.pallas_call(kernel, name=name, cost_estimate=cost, in_specs=[SMEM] + [...]
  transfers between devices with their start and end apart: 12 -> 12, of which waited for: 3 -> 2; matrix products, arithmetic and copies ran while one was open for 0% -> 0% of each run, Pallas kernels for 0% -> 6%
where the time goes in v6:
time: 106 us; the launch traced here: 105 us
  blocking collectives  55 us (52%)
  Pallas kernels  31.4 us (30%)
  starting transfers between devices  8.85 us (8%)
  waiting for transfers between devices  4.89 us (5%)
  local copies, waits for them, and re-layouts  4.37 us (4%)
    all_to_all x4, blocking collectives, everywhere(): return lax.all_to_all(payload, BOTH, 0, 0)  55 us
    pallas_call x9, Pallas kernels, call(): pl.pallas_call(kernel, name=name, cost_estimate=cost, in_specs=[SMEM] + [...  31.4 us
    ppermute x12, starting transfers between devices, swap(): return lax.ppermute(value, axis, pairs)  8.85 us
    ppermute x12, waiting for transfers between devices, swap(): return lax.ppermute(value, axis, pairs)  4.89 us
    unnamed x10, local copies, waits for them, and re-layouts  4.28 us
  transfers between devices with their start and end apart: 12, of which 2 were waited for; matrix products, arithmetic and copies ran while one was open for 0% of the time, Pallas kernels for 6%

profile of v6, /device:TPU:0, one launch (start us, length us, event | category | flops | bytes accessed | tf_op | source)
XLA Modules:
  0.0 105.4 jit_solution(14903763445664879297)
XLA Ops:
  0.8 2.2 %copy-done = f32[8,16,32,256]{3,2,1,0:T(8,128)S(1)} copy-done((f32[8,16,32,256]{3,2,1,0:T(8,128)S(1)}, f32[8,16,32,256]{3,2,1,0:T(8,128)}, u32[]{:S(2)}) %copy-start) | copy-done | bytes 4194328
  3.0 1.0 copy-done.2
  4.1 1.0 copy-done.3
  5.1 0.7 pack.1
  6.4 0.8 collective-permute-start.1
  7.2 2.6 %collective-permute-start.2 = (f32[10,16,256]{2,1,0:T(8,128)S(1)}, f32[10,16,256]{2,1,0:T(8,128)S(1)}, u32[]{:S(2)}, u32[]{:S(2)}) collective-permute-start(f32[10,16,256]{2,1,0:T(8,128)S(1)} %get-tuple-element.55), channel_id=1, source_target_pairs={{0,1},{1,0},{2,3},{3,2},{4,5},{5,4},{6,7},{7,6},{8,9},{9,8},{10,11... | collective-permute-start | bytes 491528 | tf_op jit(solution)/shard_map/ppermute | solution.py:23
  9.7 0.7 collective-permute-start.3
  10.4 5.8 %inner.1 = (f32[17,32,256]{2,1,0:T(8,128)S(1)}, f32[16,32,256]{2,1,0:T(8,128)S(1)}, f32[16,32,256]{2,1,0:T(8,128)S(1)}, f32[16,32,256]{2,1,0:T(8,128)S(1)}, f32[...) custom-call(s32[7]{0:T(128)S(1)} %stack.39.ids.refs_0_, f32[16,32,256]{2,1,0:T(8,128)S(1)} %copy-done.2, ...), custom_call_target="tpu_custom_call" | custom-call | flops 262144000 | bytes 16777216 | tf_op jit(solution)/shard_map/inner/pallas_call | solution.py:520
  16.3 3.2 %prepare.1 = (f32[17,32,256]{2,1,0:T(8,128)S(1)}, f32[16,32,256]{2,1,0:T(8,128)S(1)}, f32[16,32,256]{2,1,0:T(8,128)S(1)}, f32[16,32,256]{2,1,0:T(8,128)S(1)}, f3...) custom-call(s32[7]{0:T(128)S(1)} %stack.39.ids.refs_0_, ...), custom_call_target="tpu_custom_call" | custom-call | tf_op jit(solution)/shard_map/prepare/pallas_call | solution.py:520
  19.5 16.3 %all_to_all.20.got = f32[32,2,128]{2,1,0:T(2,128)S(1)} all-to-all(f32[32,2,128]{2,1,0:T(2,128)S(1)} %get-tuple-element.64), channel_id=1, replica_groups=mesh['gx'=4,'gy'=8] {'gx','gy'}, dimensions={0} | all-to-all | bytes 65536 | tf_op jit(solution)/shard_map/all_to_all | solution.py:31
  35.8 9.5 %start.1 = (f32[256,256]{1,0:T(8,128)S(1)}, f32[16,32,256]{2,1,0:T(8,128)S(1)}, f32[16,32,256]{2,1,0:T(8,128)S(1)}, f32[16,32,256]{2,1,0:T(8,128)S(1)}, f32[32,2...) custom-call(s32[7]{0:T(128)S(1)} %stack.39.ids.refs_0_, ...), custom_call_target="tpu_custom_call" | custom-call | tf_op jit(solution)/shard_map/start/pallas_call | solution.py:520
  46.1 0.7 collective-permute-start.6
  47.5 2.4 %collective-permute-done.6.refs_12_ = f32[16,256]{1,0:T(8,128)S(1)} collective-permute-done((f32[16,256]{1,0:T(8,128)S(1)}, f32[16,256]{1,0:T(8,128)S(1)}, u32[]{:S(2)}, u32[]{:S(2)}) %collective-permute-start.6) | collective-permute-done | bytes 16416 | tf_op jit(solution)/shard_map/ppermute | solution.py:23
  49.9 1.7 %product.2 = (f32[16,32,256]{2,1,0:T(8,128)S(1)}, f32[32,1,128]{2,1,0:T(1,128)S(1)}) custom-call(s32[7]{0:T(128)S(1)} %stack.39.ids.refs_0_, f32[16,32,256]{2,1,0:T(8,128)S(1)} %get-tuple-element.75.refs_1_.refs_15_, f32[16,32,256]{2,1,0:T(8,128)S(1)} %get-tuple-element.76.refs_2_.refs_18_, f32[8,16,32,256]{3,2,1,0:T(8,128)S(1)} %copy-done.1, ...), custom_call_target="tpu_custom_call" | custom-call | tf_op jit(solution)/shard_map/product/pallas_call | solution.py:520
  51.6 14.9 %all_to_all.21.refs_1_ = f32[32,1,128]{2,1,0:T(1,128)S(1)} all-to-all(f32[32,1,128]{2,1,0:T(1,128)S(1)} %get-tuple-element.81), channel_id=1, replica_groups=mesh['gx'=4,'gy'=8] {'gx','gy'}, dimensions={0} | all-to-all | bytes 32768 | tf_op jit(solution)/shard_map/all_to_all | solution.py:31
  66.6 2.2 %update.2 = (f32[16,32,256]{2,1,0:T(8,128)S(1)}, f32[16,32,256]{2,1,0:T(8,128)S(1)}, f32[16,32,256]{2,1,0:T(8,128)S(1)}, f32[16,32,256]{2,1,0:T(8,128)S(1)}, f32...) custom-call(s32[7]{0:T(128)S(1)} %stack.39.ids.refs_0_, ...), custom_call_target="tpu_custom_call" | custom-call | tf_op jit(solution)/shard_map/update/pallas_call | solution.py:520
  68.8 0.7 collective-permute-start.9
  69.5 0.7 collective-permute-start.10
  70.8 2.5 %collective-permute-done.10.refs_12_ = f32[16,256]{1,0:T(8,128)S(1)} collective-permute-done((f32[16,256]{1,0:T(8,128)S(1)}, f32[16,256]{1,0:T(8,128)S(1)}, u32[]{:S(2)}, u32[]{:S(2)}) %collective-permute-start.10) | collective-permute-done | bytes 16416 | tf_op jit(solution)/shard_map/ppermute | solution.py:23
  73.3 1.7 %product.3 = (f32[16,32,256]{2,1,0:T(8,128)S(1)}, f32[32,1,128]{2,1,0:T(1,128)S(1)}) custom-call(s32[7]{0:T(128)S(1)} %stack.39.ids.refs_0_, f32[16,32,256]{2,1,0:T(8,128)S(1)} %get-tuple-element.85.refs_1_.refs_15_, f32[16,32,256]{2,1,0:T(8,128)S(1)} %get-tuple-element.86.refs_2_.refs_18_, f32[8,16,32,256]{3,2,1,0:T(8,128)S(1)} %copy-done.1, ...), custom_call_target="tpu_custom_call" | custom-call | tf_op jit(solution)/shard_map/product/pallas_call | solution.py:520
  75.0 15.0 %all_to_all.22.refs_1_ = f32[32,1,128]{2,1,0:T(1,128)S(1)} all-to-all(f32[32,1,128]{2,1,0:T(1,128)S(1)} %get-tuple-element.92), channel_id=1, replica_groups=mesh['gx'=4,'gy'=8] {'gx','gy'}, dimensions={0} | all-to-all | bytes 32768 | tf_op jit(solution)/shard_map/all_to_all | solution.py:31
  90.0 4.4 %update.3 = (f32[16,32,256]{2,1,0:T(8,128)S(1)}, f32[16,32,256]{2,1,0:T(8,128)}, f32[16,32,256]{2,1,0:T(8,128)}, f32[16,32,256]{2,1,0:T(8,128)}, f32[16,32,256]{...) custom-call(s32[7]{0:T(128)S(1)} %stack.39.ids.refs_0_, f32[32,1,128]{2,1,0:T(1,128)S(1)} %all_to_all.22.refs_1_, ...), custom_call_target="tpu_custom_call" | custom-call | tf_op jit(solution)/shard_map/update/pallas_call | solution.py:520
  94.3 8.8 %all_to_all.23.got = f32[32,1,128]{2,1,0:T(1,128)S(1)} all-to-all(f32[32,1,128]{2,1,0:T(1,128)S(1)} %get-tuple-element.99), channel_id=1, replica_groups=mesh['gx'=4,'gy'=8] {'gx','gy'}, dimensions={0} | all-to-all | bytes 32768 | tf_op jit(solution)/shard_map/all_to_all | solution.py:31
  103.1 2.3 %finish.1 = f32[16,32,256]{2,1,0:T(8,128)} custom-call(s32[7]{0:T(128)S(1)} %stack.39.ids.refs_0_, f32[32,1,128]{2,1,0:T(1,128)S(1)} %all_to_all.23.got, f32[256,256]{1,0:T(8,128)S(1)} %get-tuple-element.82.refs_2_.e, f32[8,16,32,256]{3,2,1,0:T(8,128)S(1)} %copy-done.1, f32[16,32,256]{2,1,0:T(8,128)S(1)} %get-tuple-element.100.p, ...), custom_call_target="tpu_custom_call" | custom-call | tf_op jit(solution)/shard_map/finish/pallas_call | solution.py:520
  (24 shorter events, 2.8 us)
Async XLA Ops:
  0.8 2.2 %copy-start = (f32[8,16,32,256]{3,2,1,0:T(8,128)S(1)}, f32[8,16,32,256]{3,2,1,0:T(8,128)}, u32[]{:S(2)}) copy-start(f32[8,16,32,256]{3,2,1,0:T(8,128)} %z.9) | copy-start | bytes 12582916
  3.0 1.0 copy-start.2
  4.1 1.0 copy-start.3
  5.1 5.3 %copy-start.1 = (f32[8,16,32,256]{3,2,1,0:T(8,128)S(1)}, f32[8,16,32,256]{3,2,1,0:T(8,128)}, u32[]{:S(2)}) copy-start(f32[8,16,32,256]{3,2,1,0:T(8,128)} %z.9) | copy-start | bytes 12582916
  5.1 11.2 %copy-start.4 = (f32[16,32,256]{2,1,0:T(8,128)S(1)}, f32[16,32,256]{2,1,0:T(8,128)}, u32[]{:S(2)}) copy-start(f32[16,32,256]{2,1,0:T(8,128)} %b.1) | copy-start | bytes 1572868
  5.8 10.4 %collective-permute-start = (f32[10,32,256]{2,1,0:T(8,128)S(1)}, f32[10,32,256]{2,1,0:T(8,128)S(1)}, u32[]{:S(2)}, u32[]{:S(2)}) collective-permute-start(f32[10,32,256]{2,1,0:T(8,128)S(1)} %get-tuple-element.53), channel_id=1, source_target_pairs={{0,8},{8,0},{16,24},{24,16},{1,9},{9,1},{17,25},{25,17},{2,10},{10... | collective-permute-start | bytes 983048 | tf_op jit(solution)/shard_map/ppermute | solution.py:23
  6.4 9.9 %collective-permute-start.1 = (f32[10,32,256]{2,1,0:T(8,128)S(1)}, f32[10,32,256]{2,1,0:T(8,128)S(1)}, u32[]{:S(2)}, u32[]{:S(2)}) collective-permute-start(f32[10,32,256]{2,1,0:T(8,128)S(1)} %get-tuple-element.54), channel_id=1, source_target_pairs={{8,16},{16,8},{9,17},{17,9},{10,18},{18,10},{11,19},{19,11},{12,20... | collective-permute-start | bytes 983048 | tf_op jit(solution)/shard_map/ppermute | solution.py:23
  7.2 9.1 %collective-permute-start.2 = (f32[10,16,256]{2,1,0:T(8,128)S(1)}, f32[10,16,256]{2,1,0:T(8,128)S(1)}, u32[]{:S(2)}, u32[]{:S(2)}) collective-permute-start(f32[10,16,256]{2,1,0:T(8,128)S(1)} %get-tuple-element.55), channel_id=1, source_target_pairs={{0,1},{1,0},{2,3},{3,2},{4,5},{5,4},{6,7},{7,6},{8,9},{9,8},{10,11... | collective-permute-start | bytes 491528 | tf_op jit(solution)/shard_map/ppermute | solution.py:23
  9.7 6.5 %collective-permute-start.3 = (f32[10,16,256]{2,1,0:T(8,128)S(1)}, f32[10,16,256]{2,1,0:T(8,128)S(1)}, u32[]{:S(2)}, u32[]{:S(2)}) collective-permute-start(f32[10,16,256]{2,1,0:T(8,128)S(1)} %get-tuple-element.56), channel_id=1, source_target_pairs={{1,2},{2,1},{3,4},{4,3},{5,6},{6,5},{9,10},{10,9},{11,12},{12,11},... | collective-permute-start | bytes 491528 | tf_op jit(solution)/shard_map/ppermute | solution.py:23
  45.3 4.7 %collective-permute-start.4 = (f32[32,256]{1,0:T(8,128)S(1)}, f32[32,256]{1,0:T(8,128)S(1)}, u32[]{:S(2)}, u32[]{:S(2)}) collective-permute-start(f32[32,256]{1,0:T(8,128)S(1)} %get-tuple-element.77), channel_id=1, source_target_pairs={{0,8},{8,0},{16,24},{24,16},{1,9},{9,1},{17,25},{25,17},{2,10},{10... | collective-permute-start | bytes 98312 | tf_op jit(solution)/shard_map/ppermute | solution.py:23
  45.5 4.5 %collective-permute-start.5 = (f32[32,256]{1,0:T(8,128)S(1)}, f32[32,256]{1,0:T(8,128)S(1)}, u32[]{:S(2)}, u32[]{:S(2)}) collective-permute-start(f32[32,256]{1,0:T(8,128)S(1)} %get-tuple-element.78), channel_id=1, source_target_pairs={{8,16},{16,8},{9,17},{17,9},{10,18},{18,10},{11,19},{19,11},{12,20... | collective-permute-start | bytes 98312 | tf_op jit(solution)/shard_map/ppermute | solution.py:23
  46.1 3.8 %collective-permute-start.6 = (f32[16,256]{1,0:T(8,128)S(1)}, f32[16,256]{1,0:T(8,128)S(1)}, u32[]{:S(2)}, u32[]{:S(2)}) collective-permute-start(f32[16,256]{1,0:T(8,128)S(1)} %get-tuple-element.79), channel_id=1, source_target_pairs={{0,1},{1,0},{2,3},{3,2},{4,5},{5,4},{6,7},{7,6},{8,9},{9,8},{10,11... | collective-permute-start | bytes 49160 | tf_op jit(solution)/shard_map/ppermute | solution.py:23
  46.9 3.1 %collective-permute-start.7 = (f32[16,256]{1,0:T(8,128)S(1)}, f32[16,256]{1,0:T(8,128)S(1)}, u32[]{:S(2)}, u32[]{:S(2)}) collective-permute-start(f32[16,256]{1,0:T(8,128)S(1)} %get-tuple-element.80), channel_id=1, source_target_pairs={{1,2},{2,1},{3,4},{4,3},{5,6},{6,5},{9,10},{10,9},{11,12},{12,11},... | collective-permute-start | bytes 49160 | tf_op jit(solution)/shard_map/ppermute | solution.py:23
  68.7 4.6 %collective-permute-start.8 = (f32[32,256]{1,0:T(8,128)S(1)}, f32[32,256]{1,0:T(8,128)S(1)}, u32[]{:S(2)}, u32[]{:S(2)}) collective-permute-start(f32[32,256]{1,0:T(8,128)S(1)} %get-tuple-element.87), channel_id=1, source_target_pairs={{0,8},{8,0},{16,24},{24,16},{1,9},{9,1},{17,25},{25,17},{2,10},{10... | collective-permute-start | bytes 98312 | tf_op jit(solution)/shard_map/ppermute | solution.py:23
  68.8 4.5 %collective-permute-start.9 = (f32[32,256]{1,0:T(8,128)S(1)}, f32[32,256]{1,0:T(8,128)S(1)}, u32[]{:S(2)}, u32[]{:S(2)}) collective-permute-start(f32[32,256]{1,0:T(8,128)S(1)} %get-tuple-element.88), channel_id=1, source_target_pairs={{8,16},{16,8},{9,17},{17,9},{10,18},{18,10},{11,19},{19,11},{12,20... | collective-permute-start | bytes 98312 | tf_op jit(solution)/shard_map/ppermute | solution.py:23
  69.5 3.8 %collective-permute-start.10 = (f32[16,256]{1,0:T(8,128)S(1)}, f32[16,256]{1,0:T(8,128)S(1)}, u32[]{:S(2)}, u32[]{:S(2)}) collective-permute-start(f32[16,256]{1,0:T(8,128)S(1)} %get-tuple-element.89), channel_id=1, source_target_pairs={{0,1},{1,0},{2,3},{3,2},{4,5},{5,4},{6,7},{7,6},{8,9},{9,8},{10,11... | collective-permute-start | bytes 49160 | tf_op jit(solution)/shard_map/ppermute | solution.py:23
  70.2 3.1 %collective-permute-start.11 = (f32[16,256]{1,0:T(8,128)S(1)}, f32[16,256]{1,0:T(8,128)S(1)}, u32[]{:S(2)}, u32[]{:S(2)}) collective-permute-start(f32[16,256]{1,0:T(8,128)S(1)} %get-tuple-element.90), channel_id=1, source_target_pairs={{1,2},{2,1},{3,4},{4,3},{5,6},{6,5},{9,10},{10,9},{11,12},{12,11},... | collective-permute-start | bytes 49160 | tf_op jit(solution)/shard_map/ppermute | solution.py:23

commit v7 on v6

--- a/solution.py
+++ b/solution.py
@@ -82,10 +82,10 @@
     return out - fyl[i] * below - fyu[i] * above - fzl[i] * left - fzu[i] * right
 
 
-def pack_kernel(ids, x0, coef, z, sx0, sx1, sy0, sy1):
+def pack_kernel(ids, two, z, sx0, sx1, sy0, sy1):
     num, nx, ny, _ = z.shape
     evx, evy = ids[0] == 1, ids[1] == 1
-    for f, ref in enumerate([coef, x0] + [z.at[k] for k in range(num)]):
+    for f, ref in enumerate([two.at[0], two.at[1]] + [z.at[k] for k in range(num)]):
         low, high = ref[0], ref[nx - 1]
         sx0[f], sx1[f] = jnp.where(evx, high, low), jnp.where(evx, low, high)
         low, high = ref[:, 0, :], ref[:, ny - 1, :]
@@ -550,7 +550,7 @@
             order,
             pack_kernel,
             "pack",
-            [ids, start_field, coef, deflation],
+            [ids, jnp.stack([coef, start_field]), deflation],
             [(2 + num,) + layer_x] * 2 + [(2 + num,) + layer_y] * 2,
             [],
         )

time: 106 us -> 105 us (level)
  local copies, waits for them, and re-layouts: 4.37 us -> 2.29 us
  other arithmetic: 0 us -> 1.31 us
    unnamed x10, local copies, waits for them, and re-layouts: 4.28 us -> 2.2 us
    another operation x0 -> x1, other arithmetic: none -> 1.31 us  [per_device(): jnp.stack([coef, start_field])]
where the time goes in v7:
time: 105 us
  blocking collectives  55.1 us (52%)
  Pallas kernels  31.4 us (30%)
  starting transfers between devices  8.85 us (8%)
  waiting for transfers between devices  4.89 us (5%)
  local copies, waits for them, and re-layouts  2.29 us (2%)
  other arithmetic  1.31 us (1%)
    all_to_all x4, blocking collectives, everywhere(): return lax.all_to_all(payload, BOTH, 0, 0)  55.1 us
    pallas_call x9, Pallas kernels, call(): pl.pallas_call(kernel, name=name, cost_estimate=cost, in_specs=[SMEM] + [...  31.4 us
    ppermute x12, starting transfers between devices, swap(): return lax.ppermute(value, axis, pairs)  8.85 us
    ppermute x12, waiting for transfers between devices, swap(): return lax.ppermute(value, axis, pairs)  4.89 us
    unnamed x10, local copies, waits for them, and re-layouts  2.2 us
  transfers between devices with their start and end apart: 12, of which 2 were waited for; matrix products, arithmetic and copies ran while one was open for 0% of the time, Pallas kernels for 6%

profile of v7, /device:TPU:0, one launch (start us, length us, event | category | flops | bytes accessed | tf_op | source)
XLA Modules:
  0.0 104.8 jit_solution(3049311299058996154)
XLA Ops:
  0.8 1.3 %pad_maximum_fusion.two = f32[2,16,32,256]{3,2,1,0:T(8,128)S(1)} fusion(f32[1,16,32,256]{3,2,1,0:T(8,128)} %bitcast.10, f32[1,16,32,256]{3,2,1,0:T(8,128)} %bitcast.9), kind=kLoop, calls=%fused_computation | loop fusion | flops 262144 | bytes 2097152 | tf_op jit(solution)/shard_map/stack | solution.py:553
  2.2 2.2 %copy-done = f32[8,16,32,256]{3,2,1,0:T(8,128)S(1)} copy-done((f32[8,16,32,256]{3,2,1,0:T(8,128)S(1)}, f32[8,16,32,256]{3,2,1,0:T(8,128)}, u32[]{:S(2)}) %copy-start) | copy-done | bytes 4194328
  4.4 0.7 pack.1
  5.6 0.8 collective-permute-start.1
  6.4 2.6 %collective-permute-start.2 = (f32[10,16,256]{2,1,0:T(8,128)S(1)}, f32[10,16,256]{2,1,0:T(8,128)S(1)}, u32[]{:S(2)}, u32[]{:S(2)}) collective-permute-start(f32[10,16,256]{2,1,0:T(8,128)S(1)} %get-tuple-element.55), channel_id=1, source_target_pairs={{0,1},{1,0},{2,3},{3,2},{4,5},{5,4},{6,7},{7,6},{8,9},{9,8},{10,11... | collective-permute-start | bytes 491528 | tf_op jit(solution)/shard_map/ppermute | solution.py:23
  9.0 0.7 collective-permute-start.3
  9.7 5.8 %inner.1 = (f32[17,32,256]{2,1,0:T(8,128)S(1)}, f32[16,32,256]{2,1,0:T(8,128)S(1)}, f32[16,32,256]{2,1,0:T(8,128)S(1)}, f32[16,32,256]{2,1,0:T(8,128)S(1)}, f32[...) custom-call(s32[7]{0:T(128)S(1)} %stack.48.ids.refs_0_, f32[16,32,256]{2,1,0:T(8,128)S(1)} %copy-done.2, ...), custom_call_target="tpu_custom_call" | custom-call | flops 262144000 | bytes 16777216 | tf_op jit(solution)/shard_map/inner/pallas_call | solution.py:520
  15.6 3.1 %prepare.1 = (f32[17,32,256]{2,1,0:T(8,128)S(1)}, f32[16,32,256]{2,1,0:T(8,128)S(1)}, f32[16,32,256]{2,1,0:T(8,128)S(1)}, f32[16,32,256]{2,1,0:T(8,128)S(1)}, f3...) custom-call(s32[7]{0:T(128)S(1)} %stack.48.ids.refs_0_, ...), custom_call_target="tpu_custom_call" | custom-call | tf_op jit(solution)/shard_map/prepare/pallas_call | solution.py:520
  18.8 16.4 %all_to_all.20.got = f32[32,2,128]{2,1,0:T(2,128)S(1)} all-to-all(f32[32,2,128]{2,1,0:T(2,128)S(1)} %get-tuple-element.64), channel_id=1, replica_groups=mesh['gx'=4,'gy'=8] {'gx','gy'}, dimensions={0} | all-to-all | bytes 65536 | tf_op jit(solution)/shard_map/all_to_all | solution.py:31
  35.2 9.5 %start.1 = (f32[256,256]{1,0:T(8,128)S(1)}, f32[16,32,256]{2,1,0:T(8,128)S(1)}, f32[16,32,256]{2,1,0:T(8,128)S(1)}, f32[16,32,256]{2,1,0:T(8,128)S(1)}, f32[32,2...) custom-call(s32[7]{0:T(128)S(1)} %stack.48.ids.refs_0_, ...), custom_call_target="tpu_custom_call" | custom-call | tf_op jit(solution)/shard_map/start/pallas_call | solution.py:520
  44.9 0.7 collective-permute-start.5
  45.5 0.7 collective-permute-start.6
  46.9 2.4 %collective-permute-done.6.refs_12_ = f32[16,256]{1,0:T(8,128)S(1)} collective-permute-done((f32[16,256]{1,0:T(8,128)S(1)}, f32[16,256]{1,0:T(8,128)S(1)}, u32[]{:S(2)}, u32[]{:S(2)}) %collective-permute-start.6) | collective-permute-done | bytes 16416 | tf_op jit(solution)/shard_map/ppermute | solution.py:23
  49.3 1.7 %product.2 = (f32[16,32,256]{2,1,0:T(8,128)S(1)}, f32[32,1,128]{2,1,0:T(1,128)S(1)}) custom-call(s32[7]{0:T(128)S(1)} %stack.48.ids.refs_0_, f32[16,32,256]{2,1,0:T(8,128)S(1)} %get-tuple-element.75.refs_1_.refs_15_, f32[16,32,256]{2,1,0:T(8,128)S(1)} %get-tuple-element.76.refs_2_.refs_18_, f32[8,16,32,256]{3,2,1,0:T(8,128)S(1)} %copy-done.1, ...), custom_call_target="tpu_custom_call" | custom-call | tf_op jit(solution)/shard_map/product/pallas_call | solution.py:520
  51.0 14.9 %all_to_all.21.refs_1_ = f32[32,1,128]{2,1,0:T(1,128)S(1)} all-to-all(f32[32,1,128]{2,1,0:T(1,128)S(1)} %get-tuple-element.81), channel_id=1, replica_groups=mesh['gx'=4,'gy'=8] {'gx','gy'}, dimensions={0} | all-to-all | bytes 32768 | tf_op jit(solution)/shard_map/all_to_all | solution.py:31
  66.0 2.2 %update.2 = (f32[16,32,256]{2,1,0:T(8,128)S(1)}, f32[16,32,256]{2,1,0:T(8,128)S(1)}, f32[16,32,256]{2,1,0:T(8,128)S(1)}, f32[16,32,256]{2,1,0:T(8,128)S(1)}, f32...) custom-call(s32[7]{0:T(128)S(1)} %stack.48.ids.refs_0_, ...), custom_call_target="tpu_custom_call" | custom-call | tf_op jit(solution)/shard_map/update/pallas_call | solution.py:520
  68.2 0.7 collective-permute-start.9
  68.9 0.7 collective-permute-start.10
  70.2 2.5 %collective-permute-done.10.refs_12_ = f32[16,256]{1,0:T(8,128)S(1)} collective-permute-done((f32[16,256]{1,0:T(8,128)S(1)}, f32[16,256]{1,0:T(8,128)S(1)}, u32[]{:S(2)}, u32[]{:S(2)}) %collective-permute-start.10) | collective-permute-done | bytes 16416 | tf_op jit(solution)/shard_map/ppermute | solution.py:23
  72.7 1.7 %product.3 = (f32[16,32,256]{2,1,0:T(8,128)S(1)}, f32[32,1,128]{2,1,0:T(1,128)S(1)}) custom-call(s32[7]{0:T(128)S(1)} %stack.48.ids.refs_0_, f32[16,32,256]{2,1,0:T(8,128)S(1)} %get-tuple-element.85.refs_1_.refs_15_, f32[16,32,256]{2,1,0:T(8,128)S(1)} %get-tuple-element.86.refs_2_.refs_18_, f32[8,16,32,256]{3,2,1,0:T(8,128)S(1)} %copy-done.1, ...), custom_call_target="tpu_custom_call" | custom-call | tf_op jit(solution)/shard_map/product/pallas_call | solution.py:520
  74.4 15.0 %all_to_all.22.refs_1_ = f32[32,1,128]{2,1,0:T(1,128)S(1)} all-to-all(f32[32,1,128]{2,1,0:T(1,128)S(1)} %get-tuple-element.92), channel_id=1, replica_groups=mesh['gx'=4,'gy'=8] {'gx','gy'}, dimensions={0} | all-to-all | bytes 32768 | tf_op jit(solution)/shard_map/all_to_all | solution.py:31
  89.4 4.4 %update.3 = (f32[16,32,256]{2,1,0:T(8,128)S(1)}, f32[16,32,256]{2,1,0:T(8,128)}, f32[16,32,256]{2,1,0:T(8,128)}, f32[16,32,256]{2,1,0:T(8,128)}, f32[16,32,256]{...) custom-call(s32[7]{0:T(128)S(1)} %stack.48.ids.refs_0_, f32[32,1,128]{2,1,0:T(1,128)S(1)} %all_to_all.22.refs_1_, ...), custom_call_target="tpu_custom_call" | custom-call | tf_op jit(solution)/shard_map/update/pallas_call | solution.py:520
  93.7 8.8 %all_to_all.23.got = f32[32,1,128]{2,1,0:T(1,128)S(1)} all-to-all(f32[32,1,128]{2,1,0:T(1,128)S(1)} %get-tuple-element.99), channel_id=1, replica_groups=mesh['gx'=4,'gy'=8] {'gx','gy'}, dimensions={0} | all-to-all | bytes 32768 | tf_op jit(solution)/shard_map/all_to_all | solution.py:31
  102.5 2.3 %finish.1 = f32[16,32,256]{2,1,0:T(8,128)} custom-call(s32[7]{0:T(128)S(1)} %stack.48.ids.refs_0_, f32[32,1,128]{2,1,0:T(1,128)S(1)} %all_to_all.23.got, f32[256,256]{1,0:T(8,128)S(1)} %get-tuple-element.82.refs_2_.e, f32[8,16,32,256]{3,2,1,0:T(8,128)S(1)} %copy-done.1, f32[16,32,256]{2,1,0:T(8,128)S(1)} %get-tuple-element.100.p, ...), custom_call_target="tpu_custom_call" | custom-call | tf_op jit(solution)/shard_map/finish/pallas_call | solution.py:520
  (25 shorter events, 2.2 us)
Async XLA Ops:
  0.6 9.0 %copy-start.2 = (f32[16,32,256]{2,1,0:T(8,128)S(1)}, f32[16,32,256]{2,1,0:T(8,128)}, u32[]{:S(2)}) copy-start(f32[16,32,256]{2,1,0:T(8,128)} %coef.3) | copy-start | bytes 1572868
  2.2 2.2 %copy-start = (f32[8,16,32,256]{3,2,1,0:T(8,128)S(1)}, f32[8,16,32,256]{3,2,1,0:T(8,128)}, u32[]{:S(2)}) copy-start(f32[8,16,32,256]{3,2,1,0:T(8,128)} %z.9) | copy-start | bytes 12582916
  4.4 5.3 %copy-start.1 = (f32[8,16,32,256]{3,2,1,0:T(8,128)S(1)}, f32[8,16,32,256]{3,2,1,0:T(8,128)}, u32[]{:S(2)}) copy-start(f32[8,16,32,256]{3,2,1,0:T(8,128)} %z.9) | copy-start | bytes 12582916
  4.4 11.2 %copy-start.3 = (f32[16,32,256]{2,1,0:T(8,128)S(1)}, f32[16,32,256]{2,1,0:T(8,128)}, u32[]{:S(2)}) copy-start(f32[16,32,256]{2,1,0:T(8,128)} %x0.3) | copy-start | bytes 1572868
  4.4 11.2 %copy-start.4 = (f32[16,32,256]{2,1,0:T(8,128)S(1)}, f32[16,32,256]{2,1,0:T(8,128)}, u32[]{:S(2)}) copy-start(f32[16,32,256]{2,1,0:T(8,128)} %b.1) | copy-start | bytes 1572868
  5.1 10.5 %collective-permute-start = (f32[10,32,256]{2,1,0:T(8,128)S(1)}, f32[10,32,256]{2,1,0:T(8,128)S(1)}, u32[]{:S(2)}, u32[]{:S(2)}) collective-permute-start(f32[10,32,256]{2,1,0:T(8,128)S(1)} %get-tuple-element.53), channel_id=1, source_target_pairs={{0,8},{8,0},{16,24},{24,16},{1,9},{9,1},{17,25},{25,17},{2,10},{10... | collective-permute-start | bytes 983048 | tf_op jit(solution)/shard_map/ppermute | solution.py:23
  5.6 10.0 %collective-permute-start.1 = (f32[10,32,256]{2,1,0:T(8,128)S(1)}, f32[10,32,256]{2,1,0:T(8,128)S(1)}, u32[]{:S(2)}, u32[]{:S(2)}) collective-permute-start(f32[10,32,256]{2,1,0:T(8,128)S(1)} %get-tuple-element.54), channel_id=1, source_target_pairs={{8,16},{16,8},{9,17},{17,9},{10,18},{18,10},{11,19},{19,11},{12,20... | collective-permute-start | bytes 983048 | tf_op jit(solution)/shard_map/ppermute | solution.py:23
  6.4 9.1 %collective-permute-start.2 = (f32[10,16,256]{2,1,0:T(8,128)S(1)}, f32[10,16,256]{2,1,0:T(8,128)S(1)}, u32[]{:S(2)}, u32[]{:S(2)}) collective-permute-start(f32[10,16,256]{2,1,0:T(8,128)S(1)} %get-tuple-element.55), channel_id=1, source_target_pairs={{0,1},{1,0},{2,3},{3,2},{4,5},{5,4},{6,7},{7,6},{8,9},{9,8},{10,11... | collective-permute-start | bytes 491528 | tf_op jit(solution)/shard_map/ppermute | solution.py:23
  9.0 6.5 %collective-permute-start.3 = (f32[10,16,256]{2,1,0:T(8,128)S(1)}, f32[10,16,256]{2,1,0:T(8,128)S(1)}, u32[]{:S(2)}, u32[]{:S(2)}) collective-permute-start(f32[10,16,256]{2,1,0:T(8,128)S(1)} %get-tuple-element.56), channel_id=1, source_target_pairs={{1,2},{2,1},{3,4},{4,3},{5,6},{6,5},{9,10},{10,9},{11,12},{12,11},... | collective-permute-start | bytes 491528 | tf_op jit(solution)/shard_map/ppermute | solution.py:23
  44.7 4.7 %collective-permute-start.4 = (f32[32,256]{1,0:T(8,128)S(1)}, f32[32,256]{1,0:T(8,128)S(1)}, u32[]{:S(2)}, u32[]{:S(2)}) collective-permute-start(f32[32,256]{1,0:T(8,128)S(1)} %get-tuple-element.77), channel_id=1, source_target_pairs={{0,8},{8,0},{16,24},{24,16},{1,9},{9,1},{17,25},{25,17},{2,10},{10... | collective-permute-start | bytes 98312 | tf_op jit(solution)/shard_map/ppermute | solution.py:23
  44.9 4.5 %collective-permute-start.5 = (f32[32,256]{1,0:T(8,128)S(1)}, f32[32,256]{1,0:T(8,128)S(1)}, u32[]{:S(2)}, u32[]{:S(2)}) collective-permute-start(f32[32,256]{1,0:T(8,128)S(1)} %get-tuple-element.78), channel_id=1, source_target_pairs={{8,16},{16,8},{9,17},{17,9},{10,18},{18,10},{11,19},{19,11},{12,20... | collective-permute-start | bytes 98312 | tf_op jit(solution)/shard_map/ppermute | solution.py:23
  45.5 3.8 %collective-permute-start.6 = (f32[16,256]{1,0:T(8,128)S(1)}, f32[16,256]{1,0:T(8,128)S(1)}, u32[]{:S(2)}, u32[]{:S(2)}) collective-permute-start(f32[16,256]{1,0:T(8,128)S(1)} %get-tuple-element.79), channel_id=1, source_target_pairs={{0,1},{1,0},{2,3},{3,2},{4,5},{5,4},{6,7},{7,6},{8,9},{9,8},{10,11... | collective-permute-start | bytes 49160 | tf_op jit(solution)/shard_map/ppermute | solution.py:23
  46.3 3.1 %collective-permute-start.7 = (f32[16,256]{1,0:T(8,128)S(1)}, f32[16,256]{1,0:T(8,128)S(1)}, u32[]{:S(2)}, u32[]{:S(2)}) collective-permute-start(f32[16,256]{1,0:T(8,128)S(1)} %get-tuple-element.80), channel_id=1, source_target_pairs={{1,2},{2,1},{3,4},{4,3},{5,6},{6,5},{9,10},{10,9},{11,12},{12,11},... | collective-permute-start | bytes 49160 | tf_op jit(solution)/shard_map/ppermute | solution.py:23
  68.1 4.6 %collective-permute-start.8 = (f32[32,256]{1,0:T(8,128)S(1)}, f32[32,256]{1,0:T(8,128)S(1)}, u32[]{:S(2)}, u32[]{:S(2)}) collective-permute-start(f32[32,256]{1,0:T(8,128)S(1)} %get-tuple-element.87), channel_id=1, source_target_pairs={{0,8},{8,0},{16,24},{24,16},{1,9},{9,1},{17,25},{25,17},{2,10},{10... | collective-permute-start | bytes 98312 | tf_op jit(solution)/shard_map/ppermute | solution.py:23
  68.2 4.5 %collective-permute-start.9 = (f32[32,256]{1,0:T(8,128)S(1)}, f32[32,256]{1,0:T(8,128)S(1)}, u32[]{:S(2)}, u32[]{:S(2)}) collective-permute-start(f32[32,256]{1,0:T(8,128)S(1)} %get-tuple-element.88), channel_id=1, source_target_pairs={{8,16},{16,8},{9,17},{17,9},{10,18},{18,10},{11,19},{19,11},{12,20... | collective-permute-start | bytes 98312 | tf_op jit(solution)/shard_map/ppermute | solution.py:23
  68.9 3.8 %collective-permute-start.10 = (f32[16,256]{1,0:T(8,128)S(1)}, f32[16,256]{1,0:T(8,128)S(1)}, u32[]{:S(2)}, u32[]{:S(2)}) collective-permute-start(f32[16,256]{1,0:T(8,128)S(1)} %get-tuple-element.89), channel_id=1, source_target_pairs={{0,1},{1,0},{2,3},{3,2},{4,5},{5,4},{6,7},{7,6},{8,9},{9,8},{10,11... | collective-permute-start | bytes 49160 | tf_op jit(solution)/shard_map/ppermute | solution.py:23
  69.6 3.1 %collective-permute-start.11 = (f32[16,256]{1,0:T(8,128)S(1)}, f32[16,256]{1,0:T(8,128)S(1)}, u32[]{:S(2)}, u32[]{:S(2)}) collective-permute-start(f32[16,256]{1,0:T(8,128)S(1)} %get-tuple-element.90), channel_id=1, source_target_pairs={{1,2},{2,1},{3,4},{4,3},{5,6},{6,5},{9,10},{10,9},{11,12},{12,11},... | collective-permute-start | bytes 49160 | tf_op jit(solution)/shard_map/ppermute | solution.py:23
